TPU v7x, 512 devices: a whole 4x4x16 slice. The times are simulated.
512 devices in a mesh: field: 16 (over z_lo, core), spatial: 32 (over x, y, z_hi).
Axes of the slice: x: 4, y: 4, z: 16 (z_hi: 2, z_lo: 8; z = z_hi * 8 + z_lo), core: 2. Of those that a mesh axis runs over, the one named last changes fastest.
Arguments:
- field_in: bfloat16 [512, 384, 1024], P('field', 'spatial'), may hold values from -6 to 6
- spectral_weight: float32 [2, 512, 384], P(None, 'field'), may hold values from -5 to 5
- proj_in: bfloat16 [2048, 512], P(('field', 'spatial')), may hold values from -0.25 to 0.25
- bias_in: float32 [2048], replicated, may hold values from -4 to 4
- proj_out: bfloat16 [2048, 512], P(('field', 'spatial')), may hold values from -0.125 to 0.125
Outputs:
- field_out: bfloat16 [512, 384, 1024], P('field', 'spatial')
All inputs are finite; a program needn't handle non-finite values.
Results may differ from a plain program's by a relative error of at most 0.0095.
Values may be sent and summed in bfloat16 or wider, within the bound.
No kernel may reach another device: no remote copies, remote signals or barrier semaphores. Data moves between devices by JAX's collectives and lax.ppermute only.
A program may use at most 128 MiB of HBM per device.

v0:
```python
import math

import jax
import jax.numpy as jnp
from jax import lax
from jax.sharding import PartitionSpec as P

NLAT = 384
NLON = 1024
LMAX = 384
MMAX = 384


def legendre_table(orders, cosines, sines):
    order = orders[:, None]
    log_start = (
        0.5
        * (
            jnp.log((2.0 * order + 1.0) / 2.0)
            + lax.lgamma(order + 0.5)
            - lax.lgamma(jnp.ones_like(order) * 0.5)
            - lax.lgamma(order + 1.0)
        )
        + order * jnp.log(sines)[None, :]
    )
    unity = jnp.ones_like(log_start)
    nought = jnp.zeros_like(log_start)

    def advance(carry, degree):
        current, previous, scale = carry
        level = degree.astype(jnp.float32)
        below = level < order
        start = level == order
        fresh = jnp.logical_or(below, start)
        denom = jnp.maximum(level * level - order * order, 1.0)
        alpha = jnp.sqrt(jnp.maximum(4.0 * level * level - 1.0, 0.0) / denom)
        beta = jnp.sqrt(
            jnp.maximum((2.0 * level + 1.0) * ((level - 1.0) ** 2 - order * order), 0.0)
            / (jnp.maximum(2.0 * level - 3.0, 1.0) * denom)
        )
        stepped = alpha * cosines[None, :] * current - beta * previous
        total = jnp.abs(stepped) + jnp.abs(current)
        new_current = jnp.where(fresh, unity, stepped / total)
        new_previous = jnp.where(fresh, nought, current / total)
        new_scale = jnp.where(fresh, log_start, scale + jnp.log(total))
        value = jnp.where(below, nought, new_current * jnp.exp(new_scale))
        return ((new_current, new_previous, new_scale), value)

    carry_end, values = lax.scan(
        advance, (unity, nought, log_start), jnp.arange(LMAX, dtype=jnp.int32), unroll=min(LMAX, 32)
    )
    return jnp.transpose(values, (1, 0, 2))


def mirrored_table(order_ints, theta):
    half = NLAT // 2
    north = legendre_table(
        order_ints.astype(jnp.float32), jnp.cos(theta[:half]), jnp.sin(theta[:half])
    )
    degrees = jnp.arange(LMAX, dtype=jnp.int32)
    parity = (order_ints[:, None] + degrees[None, :]) % 2
    signs = (1 - 2 * parity).astype(jnp.float32)[:, :, None]
    return jnp.concatenate([north, signs * north[:, :, ::-1]], axis=-1)


def fourier_angles():
    orders = jnp.arange(MMAX, dtype=jnp.int32)[:, None]
    places = jnp.arange(NLON, dtype=jnp.int32)[None, :]
    return 2.0 * math.pi / NLON * (orders * places % NLON).astype(jnp.float32)


def shards(field_in, spectral_weight, proj_in, bias_in, proj_out):
    chans = field_in.shape[0]
    band = field_in.shape[1]
    angles = fourier_angles()
    forward_table = jnp.concatenate([jnp.cos(angles), -jnp.sin(angles)], axis=0).T / NLON
    gains = jnp.where(jnp.arange(MMAX) == 0, 1.0, 2.0).astype(jnp.float32)[:, None]
    inverse_table = jnp.concatenate([gains * jnp.cos(angles), -gains * jnp.sin(angles)], axis=0)
    flat = field_in.reshape(chans * band, NLON).astype(jnp.float32)
    spectrum = jnp.dot(flat, forward_table, precision=lax.Precision.HIGHEST)
    spectrum = jnp.transpose(spectrum.reshape(chans, band, 2, MMAX), (3, 1, 2, 0)).reshape(
        MMAX, band, 2 * chans
    )
    pencil = lax.all_to_all(
        spectrum.astype(jnp.bfloat16), "spatial", split_axis=0, concat_axis=1, tiled=True
    )
    local_orders = pencil.shape[0]
    theta = math.pi * (jnp.arange(NLAT, dtype=jnp.float32) + 0.5) / NLAT
    quad = math.pi / NLAT * jnp.sin(theta)
    first = lax.axis_index("spatial") * local_orders
    order_ints = first + jnp.arange(local_orders, dtype=jnp.int32)
    table = mirrored_table(order_ints, theta)
    weighted = pencil.astype(jnp.float32) * quad[None, :, None]
    coef = jnp.einsum("mlj,mjf->mlf", table, weighted, precision=lax.Precision.HIGHEST)
    real_w = spectral_weight[0].T[None, :, :]
    imag_w = spectral_weight[1].T[None, :, :]
    coef_re = coef[..., :chans]
    coef_im = coef[..., chans:]
    filtered = jnp.concatenate(
        [real_w * coef_re - imag_w * coef_im, real_w * coef_im + imag_w * coef_re], axis=-1
    )
    synth = jnp.einsum("mlj,mlf->mjf", table, filtered, precision=lax.Precision.HIGHEST)
    returned = lax.all_to_all(
        synth.astype(jnp.bfloat16), "spatial", split_axis=1, concat_axis=0, tiled=True
    )
    spectra = jnp.transpose(
        returned.astype(jnp.float32).reshape(MMAX, band, 2, chans), (3, 1, 2, 0)
    ).reshape(chans * band, 2 * MMAX)
    smooth = jnp.dot(spectra, inverse_table, precision=lax.Precision.HIGHEST)
    mixed = (flat + smooth).astype(jnp.bfloat16).reshape(chans, band * NLON)
    points = lax.all_to_all(mixed, "field", split_axis=1, concat_axis=0, tiled=True)
    full_in, full_out = (
        lax.all_gather(proj_in, ("field", "spatial"), axis=0, tiled=True),
        lax.all_gather(proj_out, ("field", "spatial"), axis=0, tiled=True),
    )
    hidden_pre = jnp.dot(full_in, points, preferred_element_type=jnp.float32) + bias_in[:, None]
    act = jax.nn.gelu(hidden_pre, approximate=True).astype(jnp.bfloat16)
    branch = lax.dot_general(
        full_out, act, (((0,), (0,)), ((), ())), preferred_element_type=jnp.float32
    )
    result = (points.astype(jnp.float32) + branch).astype(jnp.bfloat16)
    homed = lax.all_to_all(result, "field", split_axis=0, concat_axis=1, tiled=True)
    return homed.reshape(chans, band, NLON)


def solution(mesh):
    in_specs = (
        P("field", "spatial", None),
        P(None, "field", None),
        P(("field", "spatial"), None),
        P(),
        P(("field", "spatial"), None),
    )
    out_specs = P("field", "spatial", None)
    return jax.shard_map(shards, mesh=mesh, in_specs=in_specs, out_specs=out_specs, check_vma=False)
```

profile of v0, /device:TPU:1, one launch (start us, length us, event | category | flops | bytes accessed | tf_op | source)
XLA Modules:
  0.0 2256.0 jit_solution(12608349814941514451)
XLA Ops:
  6.5 7.0 fusion.75
  14.2 5.1 fusion.69
  19.3 1.3 copy.39
  20.9 1.6 copy.41
  22.5 1.6 reshape.2751
  24.2 21.1 all-to-all-start
  46.3 333.0 %while.23 = (s32[]{:T(128)}, f32[12,192]{1,0:T(8,128)S(1)}, f32[12,192]{1,0:T(8,128)S(1)}, f32[12,192]{1,0:T(8,128)S(1)}, f32[12,32,12,192]{3,1,0,2:T(8,128)}, /...) while((s32[]{:T(128)}, f32[12,192]{1,0:T(8,128)S(1)}, ...), condition=%wide.region_1.2_spmd.clone.clone.clone.clone, body=%wide.region_0.1_spmd.clone.clone.clone.clone.sunk | while | flops 1954562 | bytes 4313376 | solution.py:49
  46.3 0.7 fusion.142
  73.0 1.0 copy_dynamic-update-slice_fusion.2
  74.1 0.7 fusion.142
  100.8 1.0 copy_dynamic-update-slice_fusion.2
  101.8 0.7 fusion.142
  116.7 0.7 fusion.143
  128.5 1.0 copy_dynamic-update-slice_fusion.2
  129.6 0.7 fusion.142
  156.3 1.0 copy_dynamic-update-slice_fusion.2
  157.3 0.7 fusion.142
  172.2 0.7 fusion.143
  184.0 1.0 copy_dynamic-update-slice_fusion.2
  185.1 0.7 fusion.142
  211.8 1.0 copy_dynamic-update-slice_fusion.2
  212.8 0.7 fusion.142
  239.5 1.0 copy_dynamic-update-slice_fusion.2
  240.6 0.7 fusion.142
  267.3 1.0 copy_dynamic-update-slice_fusion.2
  268.3 0.7 fusion.142
  295.0 1.0 copy_dynamic-update-slice_fusion.2
  296.1 0.7 fusion.142
  322.8 1.0 copy_dynamic-update-slice_fusion.2
  323.8 0.7 fusion.142
  350.5 1.0 copy_dynamic-update-slice_fusion.2
  351.6 0.7 fusion.142
  378.3 1.0 copy_dynamic-update-slice_fusion.2
  379.3 38.4 %reverse = f32[12,384,256]{2,1,0:T(8,128)} reverse(f32[12,384,256]{2,1,0:T(8,128)} %bitcast.758), dimensions={2} | reverse | bytes 9437184
  417.9 5.1 broadcast_multiply_fusion
  423.0 0.9 reshape.2752
  423.9 1.5 copy.42
  425.5 1.9 copy.43
  427.3 2.4 reshape.2647
  429.8 3.2 copy.44
  432.9 2.7 reshape.2646
  435.6 11.4 fusion.48
  447.2 7.2 fusion.68
  454.4 1.6 copy.46
  456.0 1.6 reshape.2753
  457.7 16.4 all-to-all-start.1
  474.2 0.7 all-gather.7.cloned.1.call-update
  474.9 8.1 broadcast_multiply_fusion.1
  483.0 11.9 all-to-all-done.1
  494.8 0.9 reshape.2754
  495.8 1.6 copy.48
  497.4 4.5 reshape.2611
  501.9 4.3 copy.49
  506.2 1.1 copy.58
  507.3 4.1 add_convert_fusion
  512.0 1.1 copy.50
  513.1 25.5 %all-to-all-start.2 = ((bf16[32,16,768]{2,0,1:T(8,128)(2,1)}), bf16[32,16,768]{2,0,1:T(8,128)(2,1)S(1)}, u32[]{:S(2)}, u32[]{:S(2)}) async-start(bf16[32,16,768]{2,0,1:T(8,128)(2,1)} %copy.50), calls=%async_computation.2 | async-start | bytes 1572864 | tf_op jit(solution)/shard_map/all_to_all | solution.py:111
  538.6 598.6 %all-gather.5.cloned.1.call-done = bf16[512,4,512]{2,1,0:T(4,128)(2,1)} async-done(((bf16[1,4,512]{2,1,0:T(4,128)(2,1)}), bf16[512,4,512]{2,1,0:T(4,128)(2,1)}) %all-gather.5.cloned.1.call-update) | async-done | bytes 2097168 | tf_op jit(solution)/shard_map/all_gather | solution.py:113
  1137.2 2.5 reshape.2649
  1139.8 1048.2 %all-gather.7.cloned.1.call-done = bf16[512,4,512]{2,1,0:T(4,128)(2,1)} async-done(((bf16[1,4,512]{2,1,0:T(4,128)(2,1)}), bf16[512,4,512]{2,1,0:T(4,128)(2,1)}) %all-gather.7.cloned.1.call-update) | async-done | bytes 2097168 | tf_op jit(solution)/shard_map/all_gather | solution.py:114
  2188.0 4.0 reshape.2651
  2192.0 6.4 fusion.60
  2198.4 48.3 %all_to_all.59 = bf16[16,32,768]{2,1,0:T(8,128)(2,1)S(1)} all-to-all(bf16[16,32,768]{2,1,0:T(8,128)(2,1)} %bitcast.772), channel_id=1, replica_groups=mesh['field'=16,'spatial'=32] {'field'}, dimensions={0} | all-to-all | bytes 1572864 | tf_op jit(solution)/shard_map/all_to_all | solution.py:122
  2247.8 1.3 copy.52
  (1228 shorter events, 62.7 us)
Async XLA Ops:
  6.5 7.0 copy-start.2
  14.2 5.1 copy-start
  24.2 398.8 %all-to-all-start = ((bf16[32,2,4608]{2,1,0:T(2,128)(2,1)}), bf16[32,2,4608]{2,1,0:T(2,128)(2,1)S(1)}, u32[]{:S(2)}, u32[]{:S(2)}) async-start(bf16[32,2,4608]{2,1,0:T(2,128)(2,1)} %reshape.2751), calls=%async_computation | async-start | bytes 1179648 | tf_op jit(solution)/shard_map/all_to_all | solution.py:84
  45.3 1091.9 %all-gather.5.cloned.1.call-start = ((), (), s32[]{:S(2)}) async-start(), calls=%async_computation.4 | async-start | bytes 2101248 | tf_op jit(solution)/shard_map/all_gather | solution.py:113
  379.3 38.5 %copy-start.3 = (f32[2,32,384]{2,1,0:T(8,128)S(1)}, f32[2,32,384]{2,1,0:T(8,128)}, u32[]{:S(2)}) copy-start(f32[2,32,384]{2,1,0:T(8,128)} %param.8) | copy-start | bytes 294916
  432.9 14.3 slice-start
  435.6 11.6 slice-start.1
  457.7 37.2 %all-to-all-start.1 = ((bf16[32,2,4608]{2,1,0:T(2,128)(2,1)}), bf16[32,2,4608]{2,1,0:T(2,128)(2,1)S(1)}, u32[]{:S(2)}, u32[]{:S(2)}) async-start(bf16[32,2,4608]{2,1,0:T(2,128)(2,1)} %reshape.2753), calls=%async_computation.1 | async-start | bytes 1179648 | tf_op jit(solution)/shard_map/all_to_all | solution.py:103
  474.1 1713.9 %all-gather.7.cloned.1.call-start = ((), (), s32[]{:S(2)}) async-start(), calls=%async_computation.5 | async-start | bytes 2101248 | tf_op jit(solution)/shard_map/all_gather | solution.py:114
  501.9 5.4 copy-start.1
  513.1 1678.9 %all-to-all-start.2 = ((bf16[32,16,768]{2,0,1:T(8,128)(2,1)}), bf16[32,16,768]{2,0,1:T(8,128)(2,1)S(1)}, u32[]{:S(2)}, u32[]{:S(2)}) async-start(bf16[32,16,768]{2,0,1:T(8,128)(2,1)} %copy.50), calls=%async_computation.2 | async-start | bytes 1572864 | tf_op jit(solution)/shard_map/all_to_all | solution.py:111
  1139.8 1052.2 %copy-start.4 = (f32[2048]{0:T(1024)S(1)}, f32[2048]{0:T(1024)}, u32[]{:S(2)}) copy-start(f32[2048]{0:T(1024)} %param.10) | copy-start | bytes 24580
Sparse Core Ops, SparseCore 0:
  48.3 1088.8 all-gather.4
  1139.4 1048.6 all-gather.6
where the time goes:
time: 2260 us
  waiting for transfers between devices  1660 us (73%)
  loops' own time  252 us (11%)
  local copies, waits for them, and re-layouts  112 us (5%)
  other arithmetic  72.5 us (3%)
  starting transfers between devices  63.3 us (3%)
  blocking collectives  48.3 us (2%)
  matrix products  34.2 us (2%)
    all_gather x1, waiting for transfers between devices, shards(): lax.all_gather(proj_out, ('field', 'spatial'), axis=0, tiled=True)  1050 us
    all_gather x1, waiting for transfers between devices, shards(): lax.all_gather(proj_in, ('field', 'spatial'), axis=0, tiled=True)  599 us
    another operation x1, loops' own time, legendre_table(): lax.scan(advance, (unity, nought, log_start), jnp.arange(LMAX, dtype=jnp....  252 us
    unnamed x23, local copies, waits for them, and re-layouts  51.7 us
    all_to_all x1, blocking collectives, shards(): lax.all_to_all(result, 'field', split_axis=0, concat_axis=1, tiled=True)  48.3 us
  transfers between devices with their start and end apart: 5, of which 3 were waited for; matrix products, arithmetic and copies ran while one was open for 8% of the time, Pallas kernels for 0%

commit v1 on v0

v1 whole, which is shorter than its diff:
```python
import functools
import math

import jax
import jax.numpy as jnp
from jax import lax
from jax.experimental import pallas as pl
from jax.experimental.pallas import tpu as pltpu
from jax.sharding import PartitionSpec as P

F32 = jnp.float32
BF16 = jnp.bfloat16

CHANS = 32
BAND = 12
BANDS = 32
ORDERS = 12
NLAT = 384
NLON = 1024
LMAX = 384
HID = 2048
FULL = 512
MEMBERS = 16
ROWS = CHANS * BAND
PARTS = 2 * BANDS * ORDERS
POINTS = 768
LONS = 256
LATS = 3
BLOCK = LATS * CHANS
LANES = 128
PAD = 16
VMEM = 56 * 1024 * 1024


def params():
    return pltpu.CompilerParams(vmem_limit_bytes=VMEM)


def lanes(tile):
    return slice(tile * LANES, (tile + 1) * LANES)


def whole():
    return pl.BlockSpec(memory_space=pltpu.VMEM)


def forward_kernel(x_ref, y_ref, t_ref, xr_ref, rows_ref):
    unit = 2.0 * math.pi / NLON
    place = lax.broadcasted_iota(jnp.int32, (PAD, NLON), 1)
    row = lax.broadcasted_iota(jnp.int32, (PAD, NLON), 0)
    angle = unit * (((row >> 1) * place + (row & 1) * (NLON // 4)) & (NLON - 1)).astype(F32)
    turn = unit * ((place[:8] * 8) & (NLON - 1)).astype(F32)
    turn_cos = jnp.concatenate([jnp.cos(turn)] * 2, axis=0)
    turn_sin = jnp.concatenate([jnp.sin(turn)] * 2, axis=0)

    def turned(step, carry):
        cos, sin = carry
        t_ref[pl.ds(pl.multiple_of(step * PAD, PAD), PAD), :] = cos.astype(BF16)
        return (cos * turn_cos - sin * turn_sin, sin * turn_cos + cos * turn_sin)

    lax.fori_loop(0, PARTS // PAD, turned, (jnp.cos(angle), jnp.sin(angle)))

    for chan in range(CHANS):
        lats = x_ref[chan].astype(F32)
        for tile in range(NLON // LANES):
            rows_ref[tile, pl.ds(chan, BAND, stride=CHANS), :] = lats[:, lanes(tile)]
    for tile in range(NLON // LANES):
        xr_ref[:, lanes(tile)] = rows_ref[tile].astype(BF16)

    def transform(step, carry):
        at = pl.ds(pl.multiple_of(step * 128, 128), 128)
        y = lax.dot_general(
            t_ref[at, :], xr_ref[...], (((1,), (1,)), ((), ())), preferred_element_type=F32
        )
        y_ref[at, :] = (y * (1.0 / NLON)).astype(BF16)
        return carry

    lax.fori_loop(0, PARTS // 128, transform, 0)


def forward(x):
    return pl.pallas_call(
        forward_kernel,
        out_shape=(
            jax.ShapeDtypeStruct((PARTS, ROWS), BF16),
            jax.ShapeDtypeStruct((PARTS, NLON), BF16),
            jax.ShapeDtypeStruct((ROWS, NLON), BF16),
        ),
        in_specs=[whole()],
        out_specs=(whole(), whole(), whole()),
        scratch_shapes=[pltpu.VMEM((NLON // LANES, ROWS, LANES), F32)],
        compiler_params=params(),
        name="forward_fourier",
    )(x)


def theta_of(lane):
    lat = (lane & (BANDS - 1)) * BAND + (lane >> 5)
    return (lat.astype(F32) + 0.5) * (math.pi / NLAT)


def legendre_kernel(first_ref, table_ref, work_ref):
    first = first_ref[0]
    lane = lax.broadcasted_iota(jnp.int32, (PAD, NLAT), 1)
    theta = theta_of(lane)
    cosine = jnp.cos(theta)
    sine = jnp.sin(theta)
    order = first + lax.broadcasted_iota(jnp.int32, (PAD, NLAT), 0)
    order = jnp.minimum(order, LMAX - 1)
    level0 = order.astype(F32)
    step0 = (lane + 1).astype(F32)
    factor = jnp.where(lane < order, jnp.log2((2.0 * step0 - 1.0) / (2.0 * step0)), 0.0)
    log_start = 0.5 * (jnp.log2(level0 + 0.5) + jnp.sum(factor, axis=1, keepdims=True))
    log_start = log_start + level0 * jnp.log2(sine)
    whole_part = jnp.floor(log_start)
    start = jnp.exp2(log_start - whole_part)
    narrow = level0[:, :128]
    square = narrow * narrow

    def eight(group, carry):
        current, previous, power = carry
        half = jnp.exp2(0.5 * power)
        for inner in range(8):
            degree = group * 8 + inner
            level = degree.astype(F32)
            inverse = lax.rsqrt(jnp.maximum(level * level - square, 1.0))
            alpha = inverse * jnp.sqrt(
                jnp.maximum(jnp.full_like(square, 4.0) * (level * level) - 1.0, 0.0)
            )
            ratio = jnp.full_like(square, 1.0) * (2.0 * level + 1.0)
            ratio = ratio / jnp.maximum(jnp.full_like(square, 1.0) * (2.0 * level - 3.0), 1.0)
            below = level - 1.0
            beta = inverse * jnp.sqrt(jnp.maximum(ratio * (below * below - square), 0.0))
            alpha = jnp.concatenate([alpha] * 3, axis=1)
            beta = jnp.concatenate([beta] * 3, axis=1)
            stepped = (alpha * cosine) * current - beta * previous
            fresh = order == degree
            previous = jnp.where(fresh, 0.0, current)
            current = jnp.where(fresh, start, stepped)
            at = pl.ds(pl.multiple_of(degree * PAD, PAD), PAD)
            value = (current * half) * half
            for tile in range(3):
                work_ref[tile, at, :] = value[:, lanes(tile)]
        size = jnp.abs(current) + jnp.abs(previous)
        live = size > 0.0
        shift = jnp.where(live, jnp.floor(jnp.log2(jnp.where(live, size, 1.0))), 0.0)
        scale = jnp.exp2(-shift)
        return (current * scale, previous * scale, power + shift)

    nought = jnp.zeros((PAD, NLAT), F32)
    lax.fori_loop(0, LMAX // 8, eight, (nought, nought, whole_part))

    def store(item, carry):
        for tile in range(3):
            table_ref[item, :, lanes(tile)] = work_ref[
                tile, pl.ds(item, LMAX, stride=PAD), :
            ].astype(BF16)
        return carry

    lax.fori_loop(0, ORDERS, store, 0)


def legendre(first):
    return pl.pallas_call(
        legendre_kernel,
        out_shape=jax.ShapeDtypeStruct((ORDERS, LMAX, NLAT), BF16),
        in_specs=[pl.BlockSpec(memory_space=pltpu.SMEM)],
        out_specs=whole(),
        scratch_shapes=[pltpu.VMEM((3, LMAX * PAD, LANES), F32)],
        compiler_params=params(),
        cost_estimate=pl.CostEstimate(
            flops=100_000_000, bytes_accessed=20_000_000, transcendentals=1_000_000
        ),
        name="legendre_table",
    )(first)


def filter_kernel(r_ref, p_ref, w_ref, s_ref, rin, sout, data, gain0, gain1, quad):
    pair = pl.program_id(0)
    group = 4 * CHANS

    @pl.when(pair == 0)
    def _():
        for tile in range(3):
            rin[tile] = r_ref[:, lanes(tile)].astype(F32)
        lane = lax.broadcasted_iota(jnp.int32, (LMAX, group), 1)
        row = lax.broadcasted_iota(jnp.int32, (NLAT, group), 0)
        quad[...] = jnp.sin(theta_of(row)) * (math.pi / NLAT)
        gain0[...] = jnp.concatenate([w_ref[0]] * 4, axis=0).T
        turned = jnp.concatenate([w_ref[1]] * 4, axis=0).T
        gain1[...] = jnp.where((lane & CHANS) == 0, -turned, turned)

    lane32 = lax.broadcasted_iota(jnp.int32, (BANDS, group), 1)
    for tile in range(3):
        parts = [
            rin[tile, pl.ds(4 * pair + part, BANDS, stride=2 * ORDERS), :] for part in range(4)
        ]
        for lat in range(4):
            block = jnp.zeros((BANDS, group), F32)
            for part in range(4):
                shift = (part - lat) % 4 * CHANS
                moved = pltpu.roll(parts[part], shift, 1) if shift else parts[part]
                block = jnp.where((lane32 >> 5) == part, moved, block)
            rows = slice(group * tile + BANDS * lat, group * tile + BANDS * (lat + 1))
            data[rows, :] = (block * quad[rows, :]).astype(BF16)

    lane = lax.broadcasted_iota(jnp.int32, (LMAX, group), 1)
    upper = lane >= 2 * CHANS
    both = [
        jnp.dot(p_ref[item], data[...], preferred_element_type=F32) for item in range(2)
    ]
    coef = jnp.where(upper, both[1], both[0])
    other = jnp.where(
        (lane & CHANS) == 0, pltpu.roll(coef, group - CHANS, 1), pltpu.roll(coef, CHANS, 1)
    )
    filtered = (gain0[...] * coef + gain1[...] * other).astype(BF16)
    both = [
        lax.dot_general(
            p_ref[item], filtered, (((0,), (0,)), ((), ())), preferred_element_type=F32
        )
        for item in range(2)
    ]
    synth = jnp.where(upper, both[1], both[0])
    for tile in range(3):
        lats = [
            synth[group * tile + BANDS * lat : group * tile + BANDS * (lat + 1), :]
            for lat in range(4)
        ]
        for part in range(4):
            block = jnp.zeros((BANDS, group), F32)
            for lat in range(4):
                shift = (lat - part) % 4 * CHANS
                moved = pltpu.roll(lats[lat], shift, 1) if shift else lats[lat]
                block = jnp.where((lane32 >> 5) == lat, moved, block)
            sout[tile, pl.ds(4 * pair + part, BANDS, stride=2 * ORDERS), :] = block

    @pl.when(pair == ORDERS // 2 - 1)
    def _():
        for tile in range(3):
            s_ref[:, lanes(tile)] = sout[tile].astype(BF16)


def spectral_filter(received, table, weights):
    same2 = lambda pair: (0, 0)
    return pl.pallas_call(
        filter_kernel,
        grid=(ORDERS // 2,),
        out_shape=jax.ShapeDtypeStruct((PARTS, ROWS), BF16),
        in_specs=[
            pl.BlockSpec((PARTS, ROWS), same2),
            pl.BlockSpec((2, LMAX, NLAT), lambda pair: (pair, 0, 0)),
            pl.BlockSpec((2, CHANS, LMAX), lambda pair: (0, 0, 0)),
        ],
        out_specs=pl.BlockSpec((PARTS, ROWS), same2),
        scratch_shapes=[
            pltpu.VMEM((3, PARTS, LANES), F32),
            pltpu.VMEM((3, PARTS, LANES), F32),
            pltpu.VMEM((NLAT, 4 * CHANS), BF16),
            pltpu.VMEM((LMAX, 4 * CHANS), F32),
            pltpu.VMEM((LMAX, 4 * CHANS), F32),
            pltpu.VMEM((NLAT, 4 * CHANS), F32),
        ],
        compiler_params=params(),
        name="spectral_filter",
    )(received, table, weights)


def inverse_kernel(r_ref, t_ref, xr_ref, m_ref, spectra):
    row = lax.broadcasted_iota(jnp.int32, (PARTS, ROWS), 0)
    gained = jnp.where(row < 2, 1.0, 2.0) * r_ref[...].astype(F32)
    spectra[...] = gained.T.astype(BF16)

    def rows_of(step, carry):
        at = pl.ds(pl.multiple_of(step * BLOCK, BLOCK), BLOCK)
        smooth = jnp.dot(spectra[at, :], t_ref[...], preferred_element_type=F32)
        mixed = (xr_ref[at, :].astype(F32) + smooth).astype(BF16)
        for part in range(NLON // LONS):
            to = pl.ds(pl.multiple_of((step * 4 + part) * BLOCK, BLOCK), BLOCK)
            m_ref[to, :] = mixed[:, part * LONS : (part + 1) * LONS]
        return carry

    lax.fori_loop(0, BAND // LATS, rows_of, 0)


def inverse(returned, table, rows):
    return pl.pallas_call(
        inverse_kernel,
        out_shape=jax.ShapeDtypeStruct((MEMBERS * BLOCK, LONS), BF16),
        in_specs=[whole()] * 3,
        out_specs=whole(),
        scratch_shapes=[pltpu.VMEM((ROWS, PARTS), BF16)],
        compiler_params=params(),
        name="inverse_fourier",
    )(returned, table, rows)


def mlp_kernel(r_ref, win_ref, wout_ref, bias_ref, o_ref, points, total):
    step = pl.program_id(0)

    @pl.when(step == 0)
    def _():
        blocks = r_ref[...].reshape(MEMBERS, BLOCK, LONS)
        for lat in range(LATS):
            points[:, lat * LONS : (lat + 1) * LONS] = blocks[
                :, lat * CHANS : (lat + 1) * CHANS, :
            ].reshape(FULL, LONS)
        total[...] = points[...].astype(F32)

    rows = win_ref.shape[0] * win_ref.shape[2]
    w_in = win_ref[...].reshape(rows, FULL)
    w_out = wout_ref[...].reshape(rows, FULL)
    pre = jnp.dot(w_in, points[...], preferred_element_type=F32) + bias_ref[...]
    act = jax.nn.gelu(pre, approximate=True).astype(BF16)
    total[...] += lax.dot_general(
        w_out, act, (((0,), (0,)), ((), ())), preferred_element_type=F32
    )

    @pl.when(step == pl.num_programs(0) - 1)
    def _():
        out = total[...].astype(BF16)
        for member in range(MEMBERS):
            for lat in range(LATS):
                at = member * BLOCK + lat * CHANS
                o_ref[at : at + CHANS, :] = out[
                    member * CHANS : (member + 1) * CHANS, lat * LONS : (lat + 1) * LONS
                ]


def mlp(received, weights, bias):
    blocks, _, units, _ = weights.shape
    take = 256 // units
    same2 = lambda step: (0, 0)
    return pl.pallas_call(
        mlp_kernel,
        grid=(blocks // take,),
        out_shape=jax.ShapeDtypeStruct((MEMBERS * BLOCK, LONS), BF16),
        in_specs=[
            pl.BlockSpec((MEMBERS * BLOCK, LONS), same2),
            pl.BlockSpec((take, 1, units, FULL), lambda step: (step, 0, 0, 0)),
            pl.BlockSpec((take, 1, units, FULL), lambda step: (step, 1, 0, 0)),
            pl.BlockSpec((256, 1), lambda step: (step, 0)),
        ],
        out_specs=pl.BlockSpec((MEMBERS * BLOCK, LONS), same2),
        scratch_shapes=[pltpu.VMEM((FULL, POINTS), BF16), pltpu.VMEM((FULL, POINTS), F32)],
        compiler_params=params(),
        name="pointwise_mlp",
    )(received, weights, weights, bias)


def home_kernel(r_ref, o_ref, rows_ref):
    for member in range(MEMBERS):
        lat, part = member // 4, member % 4
        block = r_ref[member * BLOCK : (member + 1) * BLOCK, :].astype(F32)
        for tile in range(LONS // LANES):
            rows_ref[part * 2 + tile, lat * BLOCK : (lat + 1) * BLOCK, :] = block[:, lanes(tile)]
    for chan in range(CHANS):
        for tile in range(NLON // LANES):
            o_ref[chan, :, lanes(tile)] = rows_ref[
                tile, pl.ds(chan, BAND, stride=CHANS), :
            ].astype(BF16)


def home(received):
    return pl.pallas_call(
        home_kernel,
        out_shape=jax.ShapeDtypeStruct((CHANS, BAND, NLON), BF16),
        in_specs=[whole()],
        out_specs=whole(),
        scratch_shapes=[pltpu.VMEM((NLON // LANES, ROWS, LANES), F32)],
        compiler_params=params(),
        name="home_layout",
    )(received)


def gather_weights(proj_in, proj_out):
    units = proj_in.shape[0]
    both = jnp.concatenate([proj_in, proj_out], axis=0)
    column = [[xy * 32 + low * 2 + high * 16 + core for low in range(8) for core in range(2) for high in range(2)] for xy in range(16)]
    first = lax.all_gather(both, ("spatial", "field"), axis=0, axis_index_groups=column, tiled=True)
    split = first.reshape(32, 2, units, FULL).transpose(1, 0, 2, 3).reshape(64 * units, FULL)
    planes = [[xy * 2 + high for xy in range(16)] for high in range(2)]
    second = lax.all_gather(split, "spatial", axis=0, axis_index_groups=planes, tiled=True)
    return second.reshape(16, 2, 32 * units, FULL)


def shards(field_in, spectral_weight, proj_in, bias_in, proj_out):
    weights = gather_weights(proj_in, proj_out)
    bias = bias_in.reshape(16, 16, 8).transpose(1, 0, 2).reshape(HID, 1)
    spectrum, table, rows = forward(field_in)
    pencil = lax.all_to_all(
        spectrum.reshape(BANDS, 2 * ORDERS, ROWS), "spatial", split_axis=0, concat_axis=0, tiled=True
    )
    first = (lax.axis_index("spatial") * ORDERS).astype(jnp.int32).reshape(1)
    synth = spectral_filter(pencil.reshape(PARTS, ROWS), legendre(first), spectral_weight)
    returned = lax.all_to_all(
        synth.reshape(BANDS, 2 * ORDERS, ROWS), "spatial", split_axis=0, concat_axis=0, tiled=True
    )
    mixed = inverse(returned.reshape(PARTS, ROWS), table, rows)
    points = lax.all_to_all(
        mixed.reshape(MEMBERS, BLOCK, LONS), "field", split_axis=0, concat_axis=0, tiled=True
    )
    result = mlp(points.reshape(MEMBERS * BLOCK, LONS), weights, bias)
    homed = lax.all_to_all(
        result.reshape(MEMBERS, BLOCK, LONS), "field", split_axis=0, concat_axis=0, tiled=True
    )
    return home(homed.reshape(MEMBERS * BLOCK, LONS))


def solution(mesh):
    in_specs = (
        P("field", "spatial", None),
        P(None, "field", None),
        P(("field", "spatial"), None),
        P(),
        P(("field", "spatial"), None),
    )
    out_specs = P("field", "spatial", None)
    return jax.shard_map(shards, mesh=mesh, in_specs=in_specs, out_specs=out_specs, check_vma=False)
```

time: 2260 us -> 357 us (0.16)
  waiting for transfers between devices: 1660 us -> 43.5 us
  loops' own time: 252 us -> 0 us
  blocking collectives: 48.3 us -> 204 us
  local copies, waits for them, and re-layouts: 112 us -> 9.13 us
  other arithmetic: 72.5 us -> 0.71 us
  Pallas kernels: 0 us -> 47.4 us
  matrix products: 34.2 us -> 0 us
  starting transfers between devices: 63.3 us -> 38.2 us
    all_gather x2 -> x1, waiting for transfers between devices: 1650 us -> 0.01 us  [gather_weights(): lax.all_gather(split, 'spatial', axis=0, axis_index_groups=planes, tiled=...]
    another operation x1 -> x0, loops' own time: 252 us -> none  [legendre_table(): lax.scan(advance, (unity, nought, log_start), jnp.arange(LMAX, dtype=jnp....]
    all_gather x0 -> x1, blocking collectives: none -> 128 us  [gather_weights(): lax.all_gather(both, ('spatial', 'field'), axis=0, axis_index_groups=colu...]
    pallas_call x0 -> x6, Pallas kernels: none -> 47.4 us  [the longest x1 11.9 us: legendre(): pl.pallas_call(legendre_kernel, out_shape=jax.ShapeDtypeStruct((ORDERS, L...]
    unnamed x23 -> x7, local copies, waits for them, and re-layouts: 51.7 us -> 4.25 us
    while x372 -> x0, other arithmetic: 38.9 us -> none
    dot_general x5 -> x0, matrix products: 34.2 us -> none  [the longest x1 11.4 us: shards(): jnp.einsum('mlj,mjf->mlf', table, weighted, precision=lax.Precision.HIGHEST)]
    all_to_all x3 -> x2, waiting for transfers between devices: 11.9 us -> 43.5 us  [the longest x1 33.9 us: shards(): lax.all_to_all(mixed.reshape(MEMBERS, BLOCK, LONS), 'field', split_axis=0...]
  transfers between devices with their start and end apart: 5 -> 3, of which waited for: 3 -> 2; matrix products, arithmetic and copies ran while one was open for 8% -> 1% of each run, Pallas kernels for 0% -> 10%
where the time goes in v1:
time: 357 us; the launch traced here: 356 us
  blocking collectives  204 us (57%)
  Pallas kernels  47.4 us (13%)
  waiting for transfers between devices  43.5 us (12%)
  starting transfers between devices  38.2 us (11%)
  between operations  13.4 us (4%)
  local copies, waits for them, and re-layouts  9.13 us (3%)
    all_gather x1, blocking collectives, gather_weights(): lax.all_gather(both, ('spatial', 'field'), axis=0, axis_index_groups=colu...  128 us
    all_to_all x1, blocking collectives, shards(): lax.all_to_all(result.reshape(MEMBERS, BLOCK, LONS), 'field', split_axis=...  48.8 us
    all_to_all x1, waiting for transfers between devices, shards(): lax.all_to_all(mixed.reshape(MEMBERS, BLOCK, LONS), 'field', split_axis=0...  33.9 us
    all_to_all x1, starting transfers between devices, shards(): lax.all_to_all(mixed.reshape(MEMBERS, BLOCK, LONS), 'field', split_axis=0...  31.1 us
    all_to_all x1, blocking collectives, shards(): lax.all_to_all(synth.reshape(BANDS, 2 * ORDERS, ROWS), 'spatial', split_a...  27.3 us
    pallas_call x1, Pallas kernels, legendre(): pl.pallas_call(legendre_kernel, out_shape=jax.ShapeDtypeStruct((ORDERS, L...  11.9 us
    pallas_call x1, Pallas kernels, mlp(): pl.pallas_call(mlp_kernel, grid=(blocks // take,), out_shape=jax.ShapeDty...  10 us
    pallas_call x1, Pallas kernels, spectral_filter(): pl.pallas_call(filter_kernel, grid=(ORDERS // 2,), out_shape=jax.ShapeDty...  9.92 us
  transfers between devices with their start and end apart: 3, of which 2 were waited for; matrix products, arithmetic and copies ran while one was open for 1% of the time, Pallas kernels for 10%

profile of v1, /device:TPU:1, one launch (start us, length us, event | category | flops | bytes accessed | tf_op | source)
XLA Modules:
  0.0 356.5 jit_solution(253600417249059097)
XLA Ops:
  6.5 0.0 all-gather.2.cloned.1.call-start
  6.5 0.7 pad_maximum_fusion
  7.2 127.9 %all_gather.6 = bf16[256,512]{1,0:T(8,128)(2,1)S(1)} all-gather(bf16[8,512]{1,0:T(8,128)(2,1)S(1)} %pad_maximum_fusion), channel_id=1, replica_groups={{0,1,32,33,64,65,96,97,128,129,160,161,192,193,224,225,256,257,288,289,..., dimensions={0}, use_global_device_ids=true | all-gather | bytes 270336 | tf_op jit(solution)/shard_map/all_gather | solution.py:379
  135.2 0.1 reshape.49
  135.2 0.1 copy.10
  135.3 0.8 reshape.50
  136.1 0.0 all-gather.2.cloned.1.call-update
  136.1 2.5 copy.9.x_ref
  138.7 7.7 %forward_fourier.1 = (bf16[768,384]{1,0:T(8,128)(2,1)}, bf16[768,1024]{1,0:T(8,128)(2,1)}, bf16[384,1024]{1,0:T(8,128)(2,1)}) custom-call(bf16[32,12,1024]{2,1,0:T(8,128)(2,1)} %copy.9.x_ref), custom_call_target="tpu_custom_call" | custom-call | tf_op jit(solution)/shard_map/forward_fourier/pallas_call | solution.py:82
  146.4 7.1 %all-to-all-start = ((bf16[32,24,384]{2,1,0:T(8,128)(2,1)}), bf16[32,24,384]{2,1,0:T(8,128)(2,1)S(1)}, u32[]{:S(2)}, u32[]{:S(2)}) async-start(bf16[32,24,384]{2,1,0:T(8,128)(2,1)} %bitcast.22), calls=%async_computation | async-start | bytes 1179648 | tf_op jit(solution)/shard_map/all_to_all | solution.py:390
  153.5 11.9 %legendre_table.1.p_ref = bf16[12,384,384]{2,1,0:T(8,128)(2,1)} custom-call(s32[1]{0:T(128)} %bitcast.2.first_ref), custom_call_target="tpu_custom_call" | custom-call | flops 100000000 | bytes 20000000 | tf_op jit(solution)/shard_map/legendre_table/pallas_call | solution.py:164
  165.4 9.7 %all-to-all-done = bf16[32,24,384]{2,1,0:T(8,128)(2,1)S(1)} async-done(((bf16[32,24,384]{2,1,0:T(8,128)(2,1)}), bf16[32,24,384]{2,1,0:T(8,128)(2,1)S(1)}, u32[]{:S(2)}, u32[]{:S(2)}) %all-to-all-start) | async-done | bytes 589856 | tf_op jit(solution)/shard_map/all_to_all | solution.py:390
  175.0 0.0 copy-start.1
  175.0 0.8 copy-done.1
  175.8 9.9 %spectral_filter.1 = bf16[768,384]{1,0:T(8,128)(2,1)} custom-call(bf16[768,384]{1,0:T(8,128)(2,1)} %bitcast.18, bf16[12,384,384]{2,1,0:T(8,128)(2,1)} %legendre_table.1.p_ref, f32[2,32,384]{2,1,0:T(8,128)} %w_ref.1), custom_call_target="tpu_custom_call" | custom-call | tf_op jit(solution)/shard_map/spectral_filter/pallas_call | solution.py:245
  185.8 0.0 copy-start.2
  185.8 27.3 %all_to_all.20 = bf16[32,24,384]{2,1,0:T(8,128)(2,1)} all-to-all(bf16[32,24,384]{2,1,0:T(8,128)(2,1)} %bitcast.19), channel_id=1, replica_groups=mesh['field'=16,'spatial'=32] {'spatial'}, dimensions={0} | all-to-all | bytes 1179648 | tf_op jit(solution)/shard_map/all_to_all | solution.py:395
  213.0 4.5 %inverse_fourier.1 = bf16[1536,256]{1,0:T(8,128)(2,1)} custom-call(bf16[768,384]{1,0:T(8,128)(2,1)} %bitcast.20, bf16[768,1024]{1,0:T(8,128)(2,1)} %get-tuple-element.9.t_ref, bf16[384,1024]{1,0:T(8,128)(2,1)} %get-tuple-element.10.xr_ref), custom_call_target="tpu_custom_call" | custom-call | tf_op jit(solution)/shard_map/inverse_fourier/pallas_call | solution.py:286
  217.6 31.1 %all-to-all-start.2 = ((bf16[16,96,256]{2,1,0:T(8,128)(2,1)}), bf16[16,96,256]{2,1,0:T(8,128)(2,1)S(1)}, u32[]{:S(2)}, u32[]{:S(2)}) async-start(bf16[16,96,256]{2,1,0:T(8,128)(2,1)} %bitcast.14), calls=%async_computation.2 | async-start | bytes 1572864 | tf_op jit(solution)/shard_map/all_to_all | solution.py:399
  248.7 0.0 copy-done.2
  248.7 0.1 reshape.52
  248.8 1.3 reshape.56.bias_ref
  250.1 33.9 %all-to-all-done.2 = bf16[16,96,256]{2,1,0:T(8,128)(2,1)S(1)} async-done(((bf16[16,96,256]{2,1,0:T(8,128)(2,1)}), bf16[16,96,256]{2,1,0:T(8,128)(2,1)S(1)}, u32[]{:S(2)}, u32[]{:S(2)}) %all-to-all-start.2) | async-done | bytes 786464 | tf_op jit(solution)/shard_map/all_to_all | solution.py:399
  284.0 0.0 copy-start
  284.0 0.0 all-gather.2.cloned.1.call-done
  284.0 0.9 copy-done
  284.8 10.0 %pointwise_mlp.1 = bf16[1536,256]{1,0:T(8,128)(2,1)} custom-call(bf16[1536,256]{1,0:T(8,128)(2,1)} %bitcast.16, bf16[16,2,128,512]{3,2,1,0:T(8,128)(2,1)} %bitcast.12, bf16[16,2,128,512]{3,2,1,0:T(8,128)(2,1)} %bitcast.13, f32[2048,1]{1,0:T(8,128)} %reshape.56.bias_ref), custom_call_target="tpu_custom_call" | custom-call | tf_op jit(solution)/shard_map/pointwise_mlp/pallas_call | solution.py:333
  294.9 48.8 %all_to_all.21 = bf16[16,96,256]{2,1,0:T(8,128)(2,1)} all-to-all(bf16[16,96,256]{2,1,0:T(8,128)(2,1)} %bitcast.17), channel_id=1, replica_groups=mesh['field'=16,'spatial'=32] {'field'}, dimensions={0} | all-to-all | bytes 1572864 | tf_op jit(solution)/shard_map/all_to_all | solution.py:403
  343.7 3.4 home_layout.1
  347.1 2.5 copy.13
  (1 shorter events, 0.0 us)
Async XLA Ops:
  6.5 277.4 %all-gather.2.cloned.1.call-start = ((), (), s32[]{:S(2)}) async-start(), calls=%async_computation.4 | async-start | bytes 4456448 | tf_op jit(solution)/shard_map/all_gather | solution.py:382
  146.4 28.6 %all-to-all-start = ((bf16[32,24,384]{2,1,0:T(8,128)(2,1)}), bf16[32,24,384]{2,1,0:T(8,128)(2,1)S(1)}, u32[]{:S(2)}, u32[]{:S(2)}) async-start(bf16[32,24,384]{2,1,0:T(8,128)(2,1)} %bitcast.22), calls=%async_computation | async-start | bytes 1179648 | tf_op jit(solution)/shard_map/all_to_all | solution.py:390
  175.0 0.8 copy-start.1
  185.8 62.9 %copy-start.2 = (f32[2048]{0:T(1024)S(1)}, f32[2048]{0:T(1024)}, u32[]{:S(2)}) copy-start(f32[2048]{0:T(1024)} %param.8) | copy-start | bytes 24580
  217.6 66.4 %all-to-all-start.2 = ((bf16[16,96,256]{2,1,0:T(8,128)(2,1)}), bf16[16,96,256]{2,1,0:T(8,128)(2,1)S(1)}, u32[]{:S(2)}, u32[]{:S(2)}) async-start(bf16[16,96,256]{2,1,0:T(8,128)(2,1)} %bitcast.14), calls=%async_computation.2 | async-start | bytes 1572864 | tf_op jit(solution)/shard_map/all_to_all | solution.py:399
  284.0 0.9 copy-start
Sparse Core Ops, SparseCore 0:
  136.3 69.5 all-gather.1

commit v2 on v1

--- a/solution.py
+++ b/solution.py
@@ -44,7 +44,7 @@
     return pl.BlockSpec(memory_space=pltpu.VMEM)
 
 
-def forward_kernel(x_ref, y_ref, t_ref, xr_ref, rows_ref):
+def forward_kernel(x_ref, y_ref, t_ref):
     unit = 2.0 * math.pi / NLON
     place = lax.broadcasted_iota(jnp.int32, (PAD, NLON), 1)
     row = lax.broadcasted_iota(jnp.int32, (PAD, NLON), 0)
@@ -60,17 +60,10 @@
 
     lax.fori_loop(0, PARTS // PAD, turned, (jnp.cos(angle), jnp.sin(angle)))
 
-    for chan in range(CHANS):
-        lats = x_ref[chan].astype(F32)
-        for tile in range(NLON // LANES):
-            rows_ref[tile, pl.ds(chan, BAND, stride=CHANS), :] = lats[:, lanes(tile)]
-    for tile in range(NLON // LANES):
-        xr_ref[:, lanes(tile)] = rows_ref[tile].astype(BF16)
-
     def transform(step, carry):
         at = pl.ds(pl.multiple_of(step * 128, 128), 128)
         y = lax.dot_general(
-            t_ref[at, :], xr_ref[...], (((1,), (1,)), ((), ())), preferred_element_type=F32
+            t_ref[at, :], x_ref[...], (((1,), (1,)), ((), ())), preferred_element_type=F32
         )
         y_ref[at, :] = (y * (1.0 / NLON)).astype(BF16)
         return carry
@@ -84,11 +77,9 @@
         out_shape=(
             jax.ShapeDtypeStruct((PARTS, ROWS), BF16),
             jax.ShapeDtypeStruct((PARTS, NLON), BF16),
-            jax.ShapeDtypeStruct((ROWS, NLON), BF16),
         ),
         in_specs=[whole()],
-        out_specs=(whole(), whole(), whole()),
-        scratch_shapes=[pltpu.VMEM((NLON // LANES, ROWS, LANES), F32)],
+        out_specs=(whole(), whole()),
         compiler_params=params(),
         name="forward_fourier",
     )(x)
@@ -175,7 +166,7 @@
     )(first)
 
 
-def filter_kernel(r_ref, p_ref, w_ref, s_ref, rin, sout, data, gain0, gain1, quad):
+def filter_kernel(r_ref, p_ref, w_ref, s_ref, rin, sout, quad):
     pair = pl.program_id(0)
     group = 4 * CHANS
 
@@ -183,55 +174,50 @@
     def _():
         for tile in range(3):
             rin[tile] = r_ref[:, lanes(tile)].astype(F32)
-        lane = lax.broadcasted_iota(jnp.int32, (LMAX, group), 1)
-        row = lax.broadcasted_iota(jnp.int32, (NLAT, group), 0)
-        quad[...] = jnp.sin(theta_of(row)) * (math.pi / NLAT)
-        gain0[...] = jnp.concatenate([w_ref[0]] * 4, axis=0).T
-        turned = jnp.concatenate([w_ref[1]] * 4, axis=0).T
-        gain1[...] = jnp.where((lane & CHANS) == 0, -turned, turned)
-
-    lane32 = lax.broadcasted_iota(jnp.int32, (BANDS, group), 1)
+        lane = lax.broadcasted_iota(jnp.int32, (8, NLAT), 1)
+        quad[...] = jnp.sin(theta_of(lane)) * (math.pi / NLAT)
+
+    lane32 = lax.broadcasted_iota(jnp.int32, (BANDS, group), 1) >> 5
+    tiles = []
     for tile in range(3):
         parts = [
             rin[tile, pl.ds(4 * pair + part, BANDS, stride=2 * ORDERS), :] for part in range(4)
         ]
+        blocks = []
         for lat in range(4):
             block = jnp.zeros((BANDS, group), F32)
             for part in range(4):
                 shift = (part - lat) % 4 * CHANS
                 moved = pltpu.roll(parts[part], shift, 1) if shift else parts[part]
-                block = jnp.where((lane32 >> 5) == part, moved, block)
-            rows = slice(group * tile + BANDS * lat, group * tile + BANDS * (lat + 1))
-            data[rows, :] = (block * quad[rows, :]).astype(BF16)
-
-    lane = lax.broadcasted_iota(jnp.int32, (LMAX, group), 1)
-    upper = lane >= 2 * CHANS
-    both = [
-        jnp.dot(p_ref[item], data[...], preferred_element_type=F32) for item in range(2)
-    ]
-    coef = jnp.where(upper, both[1], both[0])
-    other = jnp.where(
-        (lane & CHANS) == 0, pltpu.roll(coef, group - CHANS, 1), pltpu.roll(coef, CHANS, 1)
-    )
-    filtered = (gain0[...] * coef + gain1[...] * other).astype(BF16)
-    both = [
-        lax.dot_general(
-            p_ref[item], filtered, (((0,), (0,)), ((), ())), preferred_element_type=F32
+                block = jnp.where(lane32 == part, moved, block)
+            blocks.append(block)
+        tiles.append(jnp.concatenate(blocks, axis=0).T)
+    data = jnp.concatenate(tiles, axis=1)
+    data = (data * quad[:1, :]).astype(BF16)
+
+    out = []
+    for item in range(2):
+        coef = lax.dot_general(
+            data[2 * CHANS * item : 2 * CHANS * (item + 1), :],
+            p_ref[item],
+            (((1,), (1,)), ((), ())),
+            preferred_element_type=F32,
         )
-        for item in range(2)
-    ]
-    synth = jnp.where(upper, both[1], both[0])
+        real, imag = coef[:CHANS], coef[CHANS:]
+        filtered = jnp.concatenate(
+            [w_ref[0] * real - w_ref[1] * imag, w_ref[0] * imag + w_ref[1] * real], axis=0
+        ).astype(BF16)
+        out.append(jnp.dot(filtered, p_ref[item], preferred_element_type=F32))
+    synth = jnp.concatenate(out, axis=0)
     for tile in range(3):
-        lats = [
-            synth[group * tile + BANDS * lat : group * tile + BANDS * (lat + 1), :]
-            for lat in range(4)
-        ]
+        turned = synth[:, lanes(tile)].T
+        lats = [turned[BANDS * lat : BANDS * (lat + 1), :] for lat in range(4)]
         for part in range(4):
             block = jnp.zeros((BANDS, group), F32)
             for lat in range(4):
                 shift = (lat - part) % 4 * CHANS
                 moved = pltpu.roll(lats[lat], shift, 1) if shift else lats[lat]
-                block = jnp.where((lane32 >> 5) == lat, moved, block)
+                block = jnp.where(lane32 == lat, moved, block)
             sout[tile, pl.ds(4 * pair + part, BANDS, stride=2 * ORDERS), :] = block
 
     @pl.when(pair == ORDERS // 2 - 1)
@@ -255,10 +241,7 @@
         scratch_shapes=[
             pltpu.VMEM((3, PARTS, LANES), F32),
             pltpu.VMEM((3, PARTS, LANES), F32),
-            pltpu.VMEM((NLAT, 4 * CHANS), BF16),
-            pltpu.VMEM((LMAX, 4 * CHANS), F32),
-            pltpu.VMEM((LMAX, 4 * CHANS), F32),
-            pltpu.VMEM((NLAT, 4 * CHANS), F32),
+            pltpu.VMEM((8, NLAT), F32),
         ],
         compiler_params=params(),
         name="spectral_filter",
@@ -294,8 +277,9 @@
     )(returned, table, rows)
 
 
-def mlp_kernel(r_ref, win_ref, wout_ref, bias_ref, o_ref, points, total):
+def mlp_kernel(r_ref, w_ref, bias_ref, o_ref, points, act, w_out):
     step = pl.program_id(0)
+    rows = w_ref.shape[0] * LANES
 
     @pl.when(step == 0)
     def _():
@@ -304,31 +288,36 @@
             points[:, lat * LONS : (lat + 1) * LONS] = blocks[
                 :, lat * CHANS : (lat + 1) * CHANS, :
             ].reshape(FULL, LONS)
-        total[...] = points[...].astype(F32)
-
-    rows = win_ref.shape[0] * win_ref.shape[2]
-    w_in = win_ref[...].reshape(rows, FULL)
-    w_out = wout_ref[...].reshape(rows, FULL)
-    pre = jnp.dot(w_in, points[...], preferred_element_type=F32) + bias_ref[...]
-    act = jax.nn.gelu(pre, approximate=True).astype(BF16)
-    total[...] += lax.dot_general(
-        w_out, act, (((0,), (0,)), ((), ())), preferred_element_type=F32
-    )
+
+    w_in = []
+    for part in range(w_ref.shape[0]):
+        block = w_ref[part]
+        w_in.append(
+            jnp.concatenate([block[LANES * tile : LANES * (tile + 1)] for tile in range(4)], axis=1)
+        )
+        at = pl.ds(pl.multiple_of((step * w_ref.shape[0] + part) * LANES, LANES), LANES)
+        w_out[:, at] = block[FULL:]
+    w_in = jnp.concatenate(w_in, axis=0)
+    at = pl.ds(pl.multiple_of(step * rows, rows), rows)
+    for lat in range(LATS):
+        cols = slice(lat * LONS, (lat + 1) * LONS)
+        pre = jnp.dot(w_in, points[:, cols], preferred_element_type=F32) + bias_ref[...]
+        act[at, cols] = jax.nn.gelu(pre, approximate=True).astype(BF16)
 
     @pl.when(step == pl.num_programs(0) - 1)
     def _():
-        out = total[...].astype(BF16)
-        for member in range(MEMBERS):
-            for lat in range(LATS):
-                at = member * BLOCK + lat * CHANS
-                o_ref[at : at + CHANS, :] = out[
-                    member * CHANS : (member + 1) * CHANS, lat * LONS : (lat + 1) * LONS
-                ]
+        for lat in range(LATS):
+            cols = slice(lat * LONS, (lat + 1) * LONS)
+            branch = jnp.dot(w_out[...], act[:, cols], preferred_element_type=F32)
+            out = (points[:, cols].astype(F32) + branch).astype(BF16)
+            for member in range(MEMBERS):
+                to = member * BLOCK + lat * CHANS
+                o_ref[to : to + CHANS, :] = out[member * CHANS : (member + 1) * CHANS, :]
 
 
 def mlp(received, weights, bias):
-    blocks, _, units, _ = weights.shape
-    take = 256 // units
+    blocks = weights.shape[0]
+    take = 2
     same2 = lambda step: (0, 0)
     return pl.pallas_call(
         mlp_kernel,
@@ -336,62 +325,68 @@
         out_shape=jax.ShapeDtypeStruct((MEMBERS * BLOCK, LONS), BF16),
         in_specs=[
             pl.BlockSpec((MEMBERS * BLOCK, LONS), same2),
-            pl.BlockSpec((take, 1, units, FULL), lambda step: (step, 0, 0, 0)),
-            pl.BlockSpec((take, 1, units, FULL), lambda step: (step, 1, 0, 0)),
-            pl.BlockSpec((256, 1), lambda step: (step, 0)),
+            pl.BlockSpec((take, 2 * FULL, LANES), lambda step: (step, 0, 0)),
+            pl.BlockSpec((take * LANES, 1), lambda step: (step, 0)),
         ],
         out_specs=pl.BlockSpec((MEMBERS * BLOCK, LONS), same2),
-        scratch_shapes=[pltpu.VMEM((FULL, POINTS), BF16), pltpu.VMEM((FULL, POINTS), F32)],
+        scratch_shapes=[
+            pltpu.VMEM((FULL, POINTS), BF16),
+            pltpu.VMEM((HID, POINTS), BF16),
+            pltpu.VMEM((FULL, HID), BF16),
+        ],
         compiler_params=params(),
         name="pointwise_mlp",
-    )(received, weights, weights, bias)
-
-
-def home_kernel(r_ref, o_ref, rows_ref):
+    )(received, weights, bias)
+
+
+def home_kernel(r_ref, o_ref):
     for member in range(MEMBERS):
         lat, part = member // 4, member % 4
-        block = r_ref[member * BLOCK : (member + 1) * BLOCK, :].astype(F32)
-        for tile in range(LONS // LANES):
-            rows_ref[part * 2 + tile, lat * BLOCK : (lat + 1) * BLOCK, :] = block[:, lanes(tile)]
-    for chan in range(CHANS):
-        for tile in range(NLON // LANES):
-            o_ref[chan, :, lanes(tile)] = rows_ref[
-                tile, pl.ds(chan, BAND, stride=CHANS), :
-            ].astype(BF16)
+        o_ref[lat * BLOCK : (lat + 1) * BLOCK, part * LONS : (part + 1) * LONS] = r_ref[
+            member * BLOCK : (member + 1) * BLOCK, :
+        ]
 
 
 def home(received):
     return pl.pallas_call(
         home_kernel,
-        out_shape=jax.ShapeDtypeStruct((CHANS, BAND, NLON), BF16),
+        out_shape=jax.ShapeDtypeStruct((ROWS, NLON), BF16),
         in_specs=[whole()],
         out_specs=whole(),
-        scratch_shapes=[pltpu.VMEM((NLON // LANES, ROWS, LANES), F32)],
         compiler_params=params(),
         name="home_layout",
     )(received)
 
 
-def gather_weights(proj_in, proj_out):
-    units = proj_in.shape[0]
+def gather_first(proj_in, proj_out):
+    column = [[xy * 32 + place for place in range(32)] for xy in range(16)]
     both = jnp.concatenate([proj_in, proj_out], axis=0)
-    column = [[xy * 32 + low * 2 + high * 16 + core for low in range(8) for core in range(2) for high in range(2)] for xy in range(16)]
-    first = lax.all_gather(both, ("spatial", "field"), axis=0, axis_index_groups=column, tiled=True)
-    split = first.reshape(32, 2, units, FULL).transpose(1, 0, 2, 3).reshape(64 * units, FULL)
+    return lax.all_gather(both, ("spatial", "field"), axis=0, axis_index_groups=column, tiled=True)
+
+
+def gather_second(column):
+    split = column.reshape(32, 2, HID // FULL, FULL)
+    w_in = split[:, 0].reshape(LANES, 4, LANES).transpose(1, 0, 2).reshape(FULL, LANES)
+    w_out = split[:, 1].reshape(LANES, FULL).T
+    block = jnp.concatenate([w_in, w_out], axis=0)
     planes = [[xy * 2 + high for xy in range(16)] for high in range(2)]
-    second = lax.all_gather(split, "spatial", axis=0, axis_index_groups=planes, tiled=True)
-    return second.reshape(16, 2, 32 * units, FULL)
+    whole_weights = lax.all_gather(block, "spatial", axis=0, axis_index_groups=planes, tiled=True)
+    return whole_weights.reshape(16, 2 * FULL, LANES)
 
 
 def shards(field_in, spectral_weight, proj_in, bias_in, proj_out):
-    weights = gather_weights(proj_in, proj_out)
-    bias = bias_in.reshape(16, 16, 8).transpose(1, 0, 2).reshape(HID, 1)
-    spectrum, table, rows = forward(field_in)
+    column = gather_first(proj_in, proj_out)
+    bias = bias_in.reshape(16, 16, 2, 4).transpose(1, 2, 0, 3).reshape(HID, 1)
+    rows = field_in.transpose(1, 0, 2).reshape(ROWS, NLON)
+    spectrum, table = forward(rows)
     pencil = lax.all_to_all(
         spectrum.reshape(BANDS, 2 * ORDERS, ROWS), "spatial", split_axis=0, concat_axis=0, tiled=True
     )
     first = (lax.axis_index("spatial") * ORDERS).astype(jnp.int32).reshape(1)
-    synth = spectral_filter(pencil.reshape(PARTS, ROWS), legendre(first), spectral_weight)
+    polar = legendre(first)
+    polar, column = lax.optimization_barrier((polar, column))
+    weights = gather_second(column)
+    synth = spectral_filter(pencil.reshape(PARTS, ROWS), polar, spectral_weight)
     returned = lax.all_to_all(
         synth.reshape(BANDS, 2 * ORDERS, ROWS), "spatial", split_axis=0, concat_axis=0, tiled=True
     )
@@ -403,7 +398,7 @@
     homed = lax.all_to_all(
         result.reshape(MEMBERS, BLOCK, LONS), "field", split_axis=0, concat_axis=0, tiled=True
     )
-    return home(homed.reshape(MEMBERS * BLOCK, LONS))
+    return home(homed.reshape(MEMBERS * BLOCK, LONS)).reshape(BAND, CHANS, NLON).transpose(1, 0, 2)
 
 
 def solution(mesh):

time: 357 us -> 274 us (0.77)
  blocking collectives: 204 us -> 145 us
  waiting for transfers between devices: 43.5 us -> 33.5 us
  local copies, waits for them, and re-layouts: 9.13 us -> 3.08 us
  starting transfers between devices: 38.2 us -> 33.8 us
    all_gather x1, blocking collectives: 128 us -> 38.3 us  [gather_first(): lax.all_gather(both, ('spatial', 'field'), axis=0, axis_index_groups=colu...]
    all_to_all x0 -> x1, blocking collectives: none -> 33.7 us  [shards(): lax.all_to_all(spectrum.reshape(BANDS, 2 * ORDERS, ROWS), 'spatial', spli...]
    all_to_all x1 -> x0, waiting for transfers between devices: 9.67 us -> none  [shards(): lax.all_to_all(spectrum.reshape(BANDS, 2 * ORDERS, ROWS), 'spatial', spli...]
    all_to_all x1 -> x0, starting transfers between devices: 7.09 us -> none  [shards(): lax.all_to_all(spectrum.reshape(BANDS, 2 * ORDERS, ROWS), 'spatial', spli...]
  transfers between devices with their start and end apart: 3 -> 2, of which waited for: 2 -> 1; matrix products, arithmetic and copies ran while one was open for 1% -> 1% of each run, Pallas kernels for 10% -> 7%
where the time goes in v2:
time: 274 us; the launch traced here: 273 us
  blocking collectives  145 us (53%)
  Pallas kernels  43.9 us (16%)
  starting transfers between devices  33.8 us (12%)
  waiting for transfers between devices  33.5 us (12%)
  between operations  13.5 us (5%)
  local copies, waits for them, and re-layouts  3.08 us (1%)
    all_to_all x1, blocking collectives, shards(): lax.all_to_all(result.reshape(MEMBERS, BLOCK, LONS), 'field', split_axis=...  48.8 us
    all_gather x1, blocking collectives, gather_first(): lax.all_gather(both, ('spatial', 'field'), axis=0, axis_index_groups=colu...  38.3 us
    all_to_all x1, starting transfers between devices, shards(): lax.all_to_all(mixed.reshape(MEMBERS, BLOCK, LONS), 'field', split_axis=0...  33.8 us
    all_to_all x1, blocking collectives, shards(): lax.all_to_all(spectrum.reshape(BANDS, 2 * ORDERS, ROWS), 'spatial', spli...  33.7 us
    all_to_all x1, waiting for transfers between devices, shards(): lax.all_to_all(mixed.reshape(MEMBERS, BLOCK, LONS), 'field', split_axis=0...  33.5 us
    all_to_all x1, blocking collectives, shards(): lax.all_to_all(synth.reshape(BANDS, 2 * ORDERS, ROWS), 'spatial', split_a...  23.7 us
    pallas_call x1, Pallas kernels, legendre(): pl.pallas_call(legendre_kernel, out_shape=jax.ShapeDtypeStruct((ORDERS, L...  11.9 us
    pallas_call x1, Pallas kernels, mlp(): pl.pallas_call(mlp_kernel, grid=(blocks // take,), out_shape=jax.ShapeDty...  10.3 us
  transfers between devices with their start and end apart: 2, of which 1 were waited for; matrix products, arithmetic and copies ran while one was open for 1% of the time, Pallas kernels for 7%

profile of v2, /device:TPU:1, one launch (start us, length us, event | category | flops | bytes accessed | tf_op | source)
XLA Modules:
  0.0 273.0 jit_solution(3750022925210319986)
XLA Ops:
  6.5 0.0 copy-start.3
  6.5 0.0 copy-start.2
  6.5 0.0 all-gather.2.cloned.1.call-start
  6.5 11.9 %legendre_table.1.p_ref = bf16[12,384,384]{2,1,0:T(8,128)(2,1)} custom-call(s32[1]{0:T(128)} %bitcast.4.first_ref), custom_call_target="tpu_custom_call" | custom-call | flops 100000000 | bytes 20000000 | tf_op jit(solution)/shard_map/legendre_table/pallas_call | solution.py:155
  18.4 0.0 copy-done.3
  18.4 0.0 copy-done.2
  18.4 38.3 %all_gather.6 = bf16[256,512]{1,0:T(8,128)(2,1)S(1)} all-gather(bf16[8,512]{1,0:T(8,128)(2,1)S(1)} %pad_maximum_fusion.1), channel_id=1, replica_groups={{0,32,64,96,128,160,192,224,256,288,320,352,384,416,448,480,1,33,65,97,..., dimensions={0}, use_global_device_ids=true | all-gather | bytes 270336 | tf_op jit(solution)/shard_map/all_gather | solution.py:364
  56.7 0.1 reshape.56
  56.8 0.1 slice_bitcast_fusion.1
  56.9 0.1 reshape_squeeze.6
  57.0 0.1 copy.20
  57.1 0.7 pad_maximum_fusion
  57.8 0.0 all-gather.2.cloned.1.call-update
  57.9 5.6 %forward_fourier.1 = (bf16[768,384]{1,0:T(8,128)(2,1)}, bf16[768,1024]{1,0:T(8,128)(2,1)}) custom-call(bf16[384,1024]{1,0:T(8,128)(2,1)} %bitcast.31), custom_call_target="tpu_custom_call" | custom-call | tf_op jit(solution)/shard_map/forward_fourier/pallas_call | solution.py:75
  63.4 33.7 %all_to_all.20 = bf16[32,24,384]{2,1,0:T(8,128)(2,1)} all-to-all(bf16[32,24,384]{2,1,0:T(8,128)(2,1)} %bitcast.41), channel_id=1, replica_groups=mesh['field'=16,'spatial'=32] {'spatial'}, dimensions={0} | all-to-all | bytes 1179648 | tf_op jit(solution)/shard_map/all_to_all | solution.py:382
  97.1 9.6 %spectral_filter.1 = bf16[768,384]{1,0:T(8,128)(2,1)} custom-call(bf16[768,384]{1,0:T(8,128)(2,1)} %bitcast.37, bf16[12,384,384]{2,1,0:T(8,128)(2,1)} %legendre_table.1.p_ref, f32[2,32,384]{2,1,0:T(8,128)} %w_ref.1), custom_call_target="tpu_custom_call" | custom-call | tf_op jit(solution)/shard_map/spectral_filter/pallas_call | solution.py:231
  106.7 0.0 copy-start.1
  106.7 23.7 %all_to_all.21 = bf16[32,24,384]{2,1,0:T(8,128)(2,1)} all-to-all(bf16[32,24,384]{2,1,0:T(8,128)(2,1)} %bitcast.38), channel_id=1, replica_groups=mesh['field'=16,'spatial'=32] {'spatial'}, dimensions={0} | all-to-all | bytes 1179648 | tf_op jit(solution)/shard_map/all_to_all | solution.py:390
  130.4 4.5 %inverse_fourier.1 = bf16[1536,256]{1,0:T(8,128)(2,1)} custom-call(bf16[768,384]{1,0:T(8,128)(2,1)} %bitcast.39, bf16[768,1024]{1,0:T(8,128)(2,1)} %get-tuple-element.11.t_ref, bf16[384,1024]{1,0:T(8,128)(2,1)} %bitcast.32), custom_call_target="tpu_custom_call" | custom-call | tf_op jit(solution)/shard_map/inverse_fourier/pallas_call | solution.py:269
  134.9 33.8 %all-to-all-start.2 = ((bf16[16,96,256]{2,1,0:T(8,128)(2,1)}), bf16[16,96,256]{2,1,0:T(8,128)(2,1)S(1)}, u32[]{:S(2)}, u32[]{:S(2)}) async-start(bf16[16,96,256]{2,1,0:T(8,128)(2,1)} %bitcast.33), calls=%async_computation.2 | async-start | bytes 1572864 | tf_op jit(solution)/shard_map/all_to_all | solution.py:394
  168.7 0.0 copy-done.1
  168.7 0.4 reshape.59
  169.1 0.2 copy.21
  169.3 1.2 reshape.64.bias_ref
  170.5 33.5 %all-to-all-done.2 = bf16[16,96,256]{2,1,0:T(8,128)(2,1)S(1)} async-done(((bf16[16,96,256]{2,1,0:T(8,128)(2,1)}), bf16[16,96,256]{2,1,0:T(8,128)(2,1)S(1)}, u32[]{:S(2)}, u32[]{:S(2)}) %all-to-all-start.2) | async-done | bytes 786464 | tf_op jit(solution)/shard_map/all_to_all | solution.py:394
  204.0 0.0 copy-start
  204.0 0.0 all-gather.2.cloned.1.call-done
  204.0 0.9 copy-done
  204.9 10.3 %pointwise_mlp.1 = bf16[1536,256]{1,0:T(8,128)(2,1)} custom-call(bf16[1536,256]{1,0:T(8,128)(2,1)} %bitcast.35, bf16[16,1024,128]{2,1,0:T(8,128)(2,1)} %bitcast.30, f32[2048,1]{1,0:T(8,128)} %reshape.64.bias_ref), custom_call_target="tpu_custom_call" | custom-call | tf_op jit(solution)/shard_map/pointwise_mlp/pallas_call | solution.py:322
  215.2 48.8 %all_to_all.22 = bf16[16,96,256]{2,1,0:T(8,128)(2,1)} all-to-all(bf16[16,96,256]{2,1,0:T(8,128)(2,1)} %bitcast.36), channel_id=1, replica_groups=mesh['field'=16,'spatial'=32] {'field'}, dimensions={0} | all-to-all | bytes 1572864 | tf_op jit(solution)/shard_map/all_to_all | solution.py:398
  264.1 2.1 home_layout.1
  (3 shorter events, 0.1 us)
Async XLA Ops:
  6.5 11.9 %copy-start.3 = (bf16[4,512]{1,0:T(4,128)(2,1)S(1)}, bf16[4,512]{1,0:T(4,128)(2,1)}, u32[]{:S(2)}) copy-start(bf16[4,512]{1,0:T(4,128)(2,1)} %param.7) | copy-start | bytes 12292
  6.5 11.9 %copy-start.2 = (bf16[4,512]{1,0:T(4,128)(2,1)S(1)}, bf16[4,512]{1,0:T(4,128)(2,1)}, u32[]{:S(2)}) copy-start(bf16[4,512]{1,0:T(4,128)(2,1)} %param.9) | copy-start | bytes 12292
  6.5 197.5 %all-gather.2.cloned.1.call-start = ((), (), s32[]{:S(2)}) async-start(), calls=%async_computation.4 | async-start | bytes 4456448 | tf_op jit(solution)/shard_map/all_gather | solution.py:373
  106.7 62.0 %copy-start.1 = (f32[2048]{0:T(1024)S(1)}, f32[2048]{0:T(1024)}, u32[]{:S(2)}) copy-start(f32[2048]{0:T(1024)} %param.8) | copy-start | bytes 24580
  134.9 69.1 %all-to-all-start.2 = ((bf16[16,96,256]{2,1,0:T(8,128)(2,1)}), bf16[16,96,256]{2,1,0:T(8,128)(2,1)S(1)}, u32[]{:S(2)}, u32[]{:S(2)}) async-start(bf16[16,96,256]{2,1,0:T(8,128)(2,1)} %bitcast.33), calls=%async_computation.2 | async-start | bytes 1572864 | tf_op jit(solution)/shard_map/all_to_all | solution.py:394
  204.0 0.9 copy-start
Sparse Core Ops, SparseCore 0:
  58.0 71.4 all-gather.1

commit v3 on v2

--- a/solution.py
+++ b/solution.py
@@ -90,7 +90,8 @@
     return (lat.astype(F32) + 0.5) * (math.pi / NLAT)
 
 
-def legendre_kernel(first_ref, table_ref, work_ref):
+def legendre_kernel(first_ref, bias_ref, table_ref, laid_ref, work_ref):
+    laid_ref[...] = bias_ref[...]
     first = first_ref[0]
     lane = lax.broadcasted_iota(jnp.int32, (PAD, NLAT), 1)
     theta = theta_of(lane)
@@ -151,19 +152,22 @@
     lax.fori_loop(0, ORDERS, store, 0)
 
 
-def legendre(first):
+def legendre(first, bias):
     return pl.pallas_call(
         legendre_kernel,
-        out_shape=jax.ShapeDtypeStruct((ORDERS, LMAX, NLAT), BF16),
-        in_specs=[pl.BlockSpec(memory_space=pltpu.SMEM)],
-        out_specs=whole(),
+        out_shape=(
+            jax.ShapeDtypeStruct((ORDERS, LMAX, NLAT), BF16),
+            jax.ShapeDtypeStruct(bias.shape, F32),
+        ),
+        in_specs=[pl.BlockSpec(memory_space=pltpu.SMEM), whole()],
+        out_specs=(whole(), whole()),
         scratch_shapes=[pltpu.VMEM((3, LMAX * PAD, LANES), F32)],
         compiler_params=params(),
         cost_estimate=pl.CostEstimate(
             flops=100_000_000, bytes_accessed=20_000_000, transcendentals=1_000_000
         ),
         name="legendre_table",
-    )(first)
+    )(first, bias)
 
 
 def filter_kernel(r_ref, p_ref, w_ref, s_ref, rin, sout, quad):
@@ -289,19 +293,22 @@
                 :, lat * CHANS : (lat + 1) * CHANS, :
             ].reshape(FULL, LONS)
 
-    w_in = []
+    w_in, bias = [], []
     for part in range(w_ref.shape[0]):
         block = w_ref[part]
+        column = bias_ref[pl.ds(step * w_ref.shape[0] + part, 1), :]
+        bias.append(jnp.broadcast_to(column, (LANES, LANES)).T)
         w_in.append(
             jnp.concatenate([block[LANES * tile : LANES * (tile + 1)] for tile in range(4)], axis=1)
         )
         at = pl.ds(pl.multiple_of((step * w_ref.shape[0] + part) * LANES, LANES), LANES)
         w_out[:, at] = block[FULL:]
     w_in = jnp.concatenate(w_in, axis=0)
+    bias = jnp.concatenate([jnp.concatenate(bias, axis=0)] * (LONS // LANES), axis=1)
     at = pl.ds(pl.multiple_of(step * rows, rows), rows)
     for lat in range(LATS):
         cols = slice(lat * LONS, (lat + 1) * LONS)
-        pre = jnp.dot(w_in, points[:, cols], preferred_element_type=F32) + bias_ref[...]
+        pre = jnp.dot(w_in, points[:, cols], preferred_element_type=F32) + bias
         act[at, cols] = jax.nn.gelu(pre, approximate=True).astype(BF16)
 
     @pl.when(step == pl.num_programs(0) - 1)
@@ -326,7 +333,7 @@
         in_specs=[
             pl.BlockSpec((MEMBERS * BLOCK, LONS), same2),
             pl.BlockSpec((take, 2 * FULL, LANES), lambda step: (step, 0, 0)),
-            pl.BlockSpec((take * LANES, 1), lambda step: (step, 0)),
+            pl.BlockSpec((blocks, LANES), same2),
         ],
         out_specs=pl.BlockSpec((MEMBERS * BLOCK, LONS), same2),
         scratch_shapes=[
@@ -358,14 +365,18 @@
     )(received)
 
 
+SENT = 32
+
+
 def gather_first(proj_in, proj_out):
     column = [[xy * 32 + place for place in range(32)] for xy in range(16)]
     both = jnp.concatenate([proj_in, proj_out], axis=0)
+    both = jnp.pad(both, ((0, SENT - both.shape[0]), (0, 0)))
     return lax.all_gather(both, ("spatial", "field"), axis=0, axis_index_groups=column, tiled=True)
 
 
 def gather_second(column):
-    split = column.reshape(32, 2, HID // FULL, FULL)
+    split = column.reshape(32, SENT // 4, HID // FULL, FULL)
     w_in = split[:, 0].reshape(LANES, 4, LANES).transpose(1, 0, 2).reshape(FULL, LANES)
     w_out = split[:, 1].reshape(LANES, FULL).T
     block = jnp.concatenate([w_in, w_out], axis=0)
@@ -376,17 +387,17 @@
 
 def shards(field_in, spectral_weight, proj_in, bias_in, proj_out):
     column = gather_first(proj_in, proj_out)
-    bias = bias_in.reshape(16, 16, 2, 4).transpose(1, 2, 0, 3).reshape(HID, 1)
+    bias = bias_in.reshape(16, 16, 2, 4).transpose(1, 2, 0, 3).reshape(16, LANES)
     rows = field_in.transpose(1, 0, 2).reshape(ROWS, NLON)
     spectrum, table = forward(rows)
     pencil = lax.all_to_all(
         spectrum.reshape(BANDS, 2 * ORDERS, ROWS), "spatial", split_axis=0, concat_axis=0, tiled=True
     )
     first = (lax.axis_index("spatial") * ORDERS).astype(jnp.int32).reshape(1)
-    polar = legendre(first)
-    polar, column = lax.optimization_barrier((polar, column))
+    polar, bias = legendre(first, bias)
+    synth = spectral_filter(pencil.reshape(PARTS, ROWS), polar, spectral_weight)
+    synth, column = lax.optimization_barrier((synth, column))
     weights = gather_second(column)
-    synth = spectral_filter(pencil.reshape(PARTS, ROWS), polar, spectral_weight)
     returned = lax.all_to_all(
         synth.reshape(BANDS, 2 * ORDERS, ROWS), "spatial", split_axis=0, concat_axis=0, tiled=True
     )

time: 274 us -> 280 us (1.022)
  waiting for transfers between devices: 33.5 us -> 50.6 us
  starting transfers between devices: 33.8 us -> 21.2 us
    all_gather x0 -> x1, waiting for transfers between devices: none -> 45.3 us  [gather_first(): lax.all_gather(both, ('spatial', 'field'), axis=0, axis_index_groups=colu...]
    all_gather x1 -> x0, blocking collectives: 38.3 us -> none  [gather_first(): lax.all_gather(both, ('spatial', 'field'), axis=0, axis_index_groups=colu...]
    all_to_all x1, blocking collectives: 33.7 us -> 65.1 us  [shards(): lax.all_to_all(mixed.reshape(MEMBERS, BLOCK, LONS), 'field', split_axis=0...]
    all_to_all x1, waiting for transfers between devices: 33.5 us -> 5.25 us  [shards(): lax.all_to_all(spectrum.reshape(BANDS, 2 * ORDERS, ROWS), 'spatial', spli...]
    all_to_all x1, starting transfers between devices: 33.8 us -> 21.1 us  [shards(): lax.all_to_all(spectrum.reshape(BANDS, 2 * ORDERS, ROWS), 'spatial', spli...]
    all_to_all x1, blocking collectives: 23.7 us -> 32.9 us  [shards(): lax.all_to_all(synth.reshape(BANDS, 2 * ORDERS, ROWS), 'spatial', split_a...]
    all_to_all x1, blocking collectives: 48.8 us -> 45.1 us  [shards(): lax.all_to_all(result.reshape(MEMBERS, BLOCK, LONS), 'field', split_axis=...]
  transfers between devices with their start and end apart: 2 -> 3, of which waited for: 1 -> 2; matrix products, arithmetic and copies ran while one was open for 1% -> 1% of each run, Pallas kernels for 7% -> 10%
where the time goes in v3:
time: 280 us; the launch traced here: 279 us
  blocking collectives  143 us (51%)
  waiting for transfers between devices  50.6 us (18%)
  Pallas kernels  44.5 us (16%)
  starting transfers between devices  21.2 us (8%)
  between operations  13.5 us (5%)
  local copies, waits for them, and re-layouts  4.54 us (2%)
    all_to_all x1, blocking collectives, shards(): lax.all_to_all(mixed.reshape(MEMBERS, BLOCK, LONS), 'field', split_axis=0...  65.1 us
    all_gather x1, waiting for transfers between devices, gather_first(): lax.all_gather(both, ('spatial', 'field'), axis=0, axis_index_groups=colu...  45.3 us
    all_to_all x1, blocking collectives, shards(): lax.all_to_all(result.reshape(MEMBERS, BLOCK, LONS), 'field', split_axis=...  45.1 us
    all_to_all x1, blocking collectives, shards(): lax.all_to_all(synth.reshape(BANDS, 2 * ORDERS, ROWS), 'spatial', split_a...  32.9 us
    all_to_all x1, starting transfers between devices, shards(): lax.all_to_all(spectrum.reshape(BANDS, 2 * ORDERS, ROWS), 'spatial', spli...  21.1 us
    pallas_call x1, Pallas kernels, legendre(): pl.pallas_call(legendre_kernel, out_shape=(jax.ShapeDtypeStruct((ORDERS,...  12.5 us
    pallas_call x1, Pallas kernels, mlp(): pl.pallas_call(mlp_kernel, grid=(blocks // take,), out_shape=jax.ShapeDty...  10.2 us
    pallas_call x1, Pallas kernels, spectral_filter(): pl.pallas_call(filter_kernel, grid=(ORDERS // 2,), out_shape=jax.ShapeDty...  9.59 us
  transfers between devices with their start and end apart: 3, of which 2 were waited for; matrix products, arithmetic and copies ran while one was open for 1% of the time, Pallas kernels for 10%

profile of v3, /device:TPU:1, one launch (start us, length us, event | category | flops | bytes accessed | tf_op | source)
XLA Modules:
  0.0 279.4 jit_solution(6903083538724359294)
XLA Ops:
  6.5 5.6 %forward_fourier.1 = (bf16[768,384]{1,0:T(8,128)(2,1)}, bf16[768,1024]{1,0:T(8,128)(2,1)}) custom-call(bf16[384,1024]{1,0:T(8,128)(2,1)} %bitcast.30), custom_call_target="tpu_custom_call" | custom-call | tf_op jit(solution)/shard_map/forward_fourier/pallas_call | solution.py:75
  12.1 21.1 %all-to-all-start = ((bf16[32,24,384]{2,1,0:T(8,128)(2,1)}), bf16[32,24,384]{2,1,0:T(8,128)(2,1)S(1)}, u32[]{:S(2)}, u32[]{:S(2)}) async-start(bf16[32,24,384]{2,1,0:T(8,128)(2,1)} %bitcast.40), calls=%async_computation | async-start | bytes 1179648 | tf_op jit(solution)/shard_map/all_to_all | solution.py:393
  33.2 0.0 all-gather.3.cloned.1.call-start
  33.3 1.3 fusion.2
  34.6 0.0 all-gather.3.cloned.1.call-update
  34.6 0.0 all-gather.5.cloned.1.call-start
  34.7 1.1 reshape.52
  35.8 0.3 copy.17
  36.1 0.7 copy.18.bias_ref
  36.7 12.5 %legendre_table.1 = (bf16[12,384,384]{2,1,0:T(8,128)(2,1)}, f32[16,128]{1,0:T(8,128)}) custom-call(s32[1]{0:T(128)} %bitcast.4.first_ref, f32[16,128]{1,0:T(8,128)} %copy.18.bias_ref), custom_call_target="tpu_custom_call" | custom-call | flops 100000000 | bytes 20000000 | tf_op jit(solution)/shard_map/legendre_table/pallas_call | solution.py:156
  49.2 5.2 %all-to-all-done = bf16[32,24,384]{2,1,0:T(8,128)(2,1)S(1)} async-done(((bf16[32,24,384]{2,1,0:T(8,128)(2,1)}), bf16[32,24,384]{2,1,0:T(8,128)(2,1)S(1)}, u32[]{:S(2)}, u32[]{:S(2)}) %all-to-all-start) | async-done | bytes 589856 | tf_op jit(solution)/shard_map/all_to_all | solution.py:393
  54.5 0.0 copy-start
  54.5 0.8 copy-done
  55.3 9.6 %spectral_filter.1 = bf16[768,384]{1,0:T(8,128)(2,1)} custom-call(bf16[768,384]{1,0:T(8,128)(2,1)} %bitcast.36, bf16[12,384,384]{2,1,0:T(8,128)(2,1)} %get-tuple-element.12.p_ref, f32[2,32,384]{2,1,0:T(8,128)} %w_ref.1), custom_call_target="tpu_custom_call" | custom-call | tf_op jit(solution)/shard_map/spectral_filter/pallas_call | solution.py:235
  64.9 0.0 copy-start.1
  64.9 45.3 %all-gather.3.cloned.1.call-done = bf16[1024,512]{1,0:T(8,128)(2,1)} async-done(((bf16[32,512]{1,0:T(8,128)(2,1)}), bf16[1024,512]{1,0:T(8,128)(2,1)}) %all-gather.3.cloned.1.call-update) | async-done | bytes 1048592 | tf_op jit(solution)/shard_map/all_gather | solution.py:375
  110.2 1.3 reshape.58
  111.5 0.1 slice_bitcast_fusion.1
  111.7 0.1 copy.22
  111.8 0.1 reshape_squeeze.6
  111.9 0.7 pad_maximum_fusion
  112.6 0.0 all-gather.5.cloned.1.call-update
  112.6 0.0 copy-done.1
  112.7 32.9 %all_to_all.20 = bf16[32,24,384]{2,1,0:T(8,128)(2,1)} all-to-all(bf16[32,24,384]{2,1,0:T(8,128)(2,1)S(1)} %bitcast.37), channel_id=1, replica_groups=mesh['field'=16,'spatial'=32] {'spatial'}, dimensions={0} | all-to-all | bytes 1179648 | tf_op jit(solution)/shard_map/all_to_all | solution.py:401
  145.6 4.5 %inverse_fourier.1 = bf16[1536,256]{1,0:T(8,128)(2,1)} custom-call(bf16[768,384]{1,0:T(8,128)(2,1)} %bitcast.38, bf16[768,1024]{1,0:T(8,128)(2,1)} %get-tuple-element.14.t_ref, bf16[384,1024]{1,0:T(8,128)(2,1)} %bitcast.31), custom_call_target="tpu_custom_call" | custom-call | tf_op jit(solution)/shard_map/inverse_fourier/pallas_call | solution.py:273
  150.1 65.1 %all_to_all.21 = bf16[16,96,256]{2,1,0:T(8,128)(2,1)} all-to-all(bf16[16,96,256]{2,1,0:T(8,128)(2,1)} %bitcast.32), channel_id=1, replica_groups=mesh['field'=16,'spatial'=32] {'field'}, dimensions={0} | all-to-all | bytes 1572864 | tf_op jit(solution)/shard_map/all_to_all | solution.py:405
  215.2 0.0 all-gather.5.cloned.1.call-done
  215.2 10.2 %pointwise_mlp.1 = bf16[1536,256]{1,0:T(8,128)(2,1)} custom-call(bf16[1536,256]{1,0:T(8,128)(2,1)} %bitcast.34, bf16[16,1024,128]{2,1,0:T(8,128)(2,1)} %bitcast.29, f32[16,128]{1,0:T(8,128)} %get-tuple-element.16.bias_ref), custom_call_target="tpu_custom_call" | custom-call | tf_op jit(solution)/shard_map/pointwise_mlp/pallas_call | solution.py:329
  225.4 45.1 %all_to_all.22 = bf16[16,96,256]{2,1,0:T(8,128)(2,1)} all-to-all(bf16[16,96,256]{2,1,0:T(8,128)(2,1)} %bitcast.35), channel_id=1, replica_groups=mesh['field'=16,'spatial'=32] {'field'}, dimensions={0} | all-to-all | bytes 1572864 | tf_op jit(solution)/shard_map/all_to_all | solution.py:409
  270.5 2.1 home_layout.1
  (2 shorter events, 0.1 us)
Async XLA Ops:
  12.1 42.4 %all-to-all-start = ((bf16[32,24,384]{2,1,0:T(8,128)(2,1)}), bf16[32,24,384]{2,1,0:T(8,128)(2,1)S(1)}, u32[]{:S(2)}, u32[]{:S(2)}) async-start(bf16[32,24,384]{2,1,0:T(8,128)(2,1)} %bitcast.40), calls=%async_computation | async-start | bytes 1179648 | tf_op jit(solution)/shard_map/all_to_all | solution.py:393
  33.2 77.0 %all-gather.3.cloned.1.call-start = ((), (), s32[]{:S(2)}) async-start(), calls=%async_computation.4 | async-start | bytes 1081344 | tf_op jit(solution)/shard_map/all_gather | solution.py:375
  34.6 180.6 %all-gather.5.cloned.1.call-start = ((), (), s32[]{:S(2)}) async-start(), calls=%async_computation.5 | async-start | bytes 4456448 | tf_op jit(solution)/shard_map/all_gather | solution.py:384
  54.5 0.8 copy-start
  64.9 47.7 %copy-start.1 = (bf16[768,384]{1,0:T(8,128)(2,1)S(1)}, bf16[768,384]{1,0:T(8,128)(2,1)}, u32[]{:S(2)}) copy-start(bf16[768,384]{1,0:T(8,128)(2,1)} %spectral_filter.1) | copy-start | bytes 1769476
Sparse Core Ops, SparseCore 0:
  36.2 73.9 all-gather.2
  113.2 65.0 all-gather.4

commit v4 on v3

--- a/solution.py
+++ b/solution.py
@@ -365,18 +365,39 @@
     )(received)
 
 
-SENT = 32
+def place_in_column():
+    return (lax.axis_index("spatial") & 1) * 8 + (lax.axis_index("field") >> 1)
+
+
+def partner(bit):
+    pairs = []
+    for field in range(16):
+        for spatial in range(32):
+            other = ((spatial & 1) * 8 + (field >> 1)) ^ bit
+            pairs.append(
+                (
+                    field * 32 + spatial,
+                    ((other & 7) * 2 + (field & 1)) * 32 + (spatial & 30) + (other >> 3),
+                )
+            )
+    return pairs
 
 
 def gather_first(proj_in, proj_out):
-    column = [[xy * 32 + place for place in range(32)] for xy in range(16)]
-    both = jnp.concatenate([proj_in, proj_out], axis=0)
-    both = jnp.pad(both, ((0, SENT - both.shape[0]), (0, 0)))
-    return lax.all_gather(both, ("spatial", "field"), axis=0, axis_index_groups=column, tiled=True)
+    held = jnp.concatenate([proj_in, proj_out], axis=0)
+    place = place_in_column()
+    for bit in (1, 2, 4, 8):
+        other = lax.ppermute(held, ("field", "spatial"), partner(bit))
+        upper = (place & bit) != 0
+        held = jnp.concatenate(
+            [jnp.where(upper, other, held), jnp.where(upper, held, other)], axis=0
+        )
+    cores = [[2 * chip, 2 * chip + 1] for chip in range(8)]
+    return lax.all_gather(held, "field", axis=0, axis_index_groups=cores, tiled=True)
 
 
 def gather_second(column):
-    split = column.reshape(32, SENT // 4, HID // FULL, FULL)
+    split = column.reshape(32, 2, HID // FULL, FULL)
     w_in = split[:, 0].reshape(LANES, 4, LANES).transpose(1, 0, 2).reshape(FULL, LANES)
     w_out = split[:, 1].reshape(LANES, FULL).T
     block = jnp.concatenate([w_in, w_out], axis=0)
@@ -387,7 +408,7 @@
 
 def shards(field_in, spectral_weight, proj_in, bias_in, proj_out):
     column = gather_first(proj_in, proj_out)
-    bias = bias_in.reshape(16, 16, 2, 4).transpose(1, 2, 0, 3).reshape(16, LANES)
+    bias = bias_in.reshape(8, 2, 16, 2, 4).transpose(2, 1, 3, 0, 4).reshape(16, LANES)
     rows = field_in.transpose(1, 0, 2).reshape(ROWS, NLON)
     spectrum, table = forward(rows)
     pencil = lax.all_to_all(

time: 280 us -> 278 us (level)
  starting transfers between devices: 21.2 us -> 42.9 us
  waiting for transfers between devices: 50.6 us -> 29.7 us
    all_gather x1 -> x0, waiting for transfers between devices: 45.3 us -> none  [gather_first(): lax.all_gather(both, ('spatial', 'field'), axis=0, axis_index_groups=colu...]
    ppermute x0 -> x4, waiting for transfers between devices: none -> 29.7 us  [gather_first(): other = lax.ppermute(held, ('field', 'spatial'), partner(bit))]
    ppermute x0 -> x4, starting transfers between devices: none -> 21.7 us  [gather_first(): other = lax.ppermute(held, ('field', 'spatial'), partner(bit))]
    all_to_all x1, blocking collectives: 65.1 us -> 50.9 us  [shards(): lax.all_to_all(mixed.reshape(MEMBERS, BLOCK, LONS), 'field', split_axis=0...]
    all_to_all x1, blocking collectives: 32.9 us -> 39.3 us  [shards(): lax.all_to_all(synth.reshape(BANDS, 2 * ORDERS, ROWS), 'spatial', split_a...]
    all_gather x0 -> x1, blocking collectives: none -> 5.7 us  [gather_first(): lax.all_gather(held, 'field', axis=0, axis_index_groups=cores, tiled=True)]
    all_to_all x1, waiting for transfers between devices: 5.25 us -> 0.01 us  [shards(): lax.all_to_all(spectrum.reshape(BANDS, 2 * ORDERS, ROWS), 'spatial', spli...]
  transfers between devices with their start and end apart: 3 -> 6, of which waited for: 2 -> 3; matrix products, arithmetic and copies ran while one was open for 1% -> 1% of each run, Pallas kernels for 10% -> 6%
where the time goes in v4:
time: 278 us; the launch traced here: 277 us
  blocking collectives  141 us (51%)
  Pallas kernels  44.5 us (16%)
  starting transfers between devices  42.9 us (15%)
  waiting for transfers between devices  29.7 us (11%)
  between operations  13.6 us (5%)
  local copies, waits for them, and re-layouts  3.26 us (1%)
    all_to_all x1, blocking collectives, shards(): lax.all_to_all(mixed.reshape(MEMBERS, BLOCK, LONS), 'field', split_axis=0...  50.9 us
    all_to_all x1, blocking collectives, shards(): lax.all_to_all(result.reshape(MEMBERS, BLOCK, LONS), 'field', split_axis=...  45.1 us
    all_to_all x1, blocking collectives, shards(): lax.all_to_all(synth.reshape(BANDS, 2 * ORDERS, ROWS), 'spatial', split_a...  39.3 us
    ppermute x4, waiting for transfers between devices, gather_first(): other = lax.ppermute(held, ('field', 'spatial'), partner(bit))  29.7 us
    ppermute x4, starting transfers between devices, gather_first(): other = lax.ppermute(held, ('field', 'spatial'), partner(bit))  21.7 us
    all_to_all x1, starting transfers between devices, shards(): lax.all_to_all(spectrum.reshape(BANDS, 2 * ORDERS, ROWS), 'spatial', spli...  21.1 us
    pallas_call x1, Pallas kernels, legendre(): pl.pallas_call(legendre_kernel, out_shape=(jax.ShapeDtypeStruct((ORDERS,...  12.5 us
    pallas_call x1, Pallas kernels, mlp(): pl.pallas_call(mlp_kernel, grid=(blocks // take,), out_shape=jax.ShapeDty...  10.2 us
  transfers between devices with their start and end apart: 6, of which 3 were waited for; matrix products, arithmetic and copies ran while one was open for 1% of the time, Pallas kernels for 6%

profile of v4, /device:TPU:1, one launch (start us, length us, event | category | flops | bytes accessed | tf_op | source)
XLA Modules:
  0.0 277.2 jit_solution(1439865328441669120)
XLA Ops:
  6.5 5.6 %forward_fourier.1 = (bf16[768,384]{1,0:T(8,128)(2,1)}, bf16[768,1024]{1,0:T(8,128)(2,1)}) custom-call(bf16[384,1024]{1,0:T(8,128)(2,1)} %bitcast.30), custom_call_target="tpu_custom_call" | custom-call | tf_op jit(solution)/shard_map/forward_fourier/pallas_call | solution.py:75
  12.1 21.1 %all-to-all-start = ((bf16[32,24,384]{2,1,0:T(8,128)(2,1)}), bf16[32,24,384]{2,1,0:T(8,128)(2,1)S(1)}, u32[]{:S(2)}, u32[]{:S(2)}) async-start(bf16[32,24,384]{2,1,0:T(8,128)(2,1)} %bitcast.40), calls=%async_computation | async-start | bytes 1179648 | tf_op jit(solution)/shard_map/all_to_all | solution.py:414
  33.2 0.0 all-gather.2.cloned.1.call-start
  33.3 0.7 pad_maximum_fusion.5
  34.0 2.6 collective-permute-start
  36.6 23.0 %collective-permute-done = bf16[8,512]{1,0:T(8,128)(2,1)S(1)} collective-permute-done((bf16[8,512]{1,0:T(8,128)(2,1)S(1)}, bf16[8,512]{1,0:T(8,128)(2,1)S(1)}, u32[]{:S(2)}, u32[]{:S(2)}) %collective-permute-start) | collective-permute-done | bytes 8224 | tf_op jit(solution)/shard_map/ppermute | solution.py:390
  59.6 0.7 broadcast_select_fusion.7
  60.3 1.9 collective-permute-start.1
  62.3 4.5 %collective-permute-done.1 = bf16[16,512]{1,0:T(8,128)(2,1)S(1)} collective-permute-done((bf16[16,512]{1,0:T(8,128)(2,1)S(1)}, bf16[16,512]{1,0:T(8,128)(2,1)S(1)}, u32[]{:S(2)}, u32[]{:S(2)}) %collective-permute-start.1) | collective-permute-done | bytes 16416 | tf_op jit(solution)/shard_map/ppermute | solution.py:390
  66.8 6.3 %collective-permute-start.2 = (bf16[32,512]{1,0:T(8,128)(2,1)S(1)}, bf16[32,512]{1,0:T(8,128)(2,1)S(1)}, u32[]{:S(2)}, u32[]{:S(2)}) collective-permute-start(bf16[32,512]{1,0:T(8,128)(2,1)S(1)} %pad_maximum_fusion.3), channel_id=1, source_target_pairs={{0,256},{1,257},{2,258},{3,259},{4,260},{5,261},{6,262},{7,263},{8... | collective-permute-start | bytes 98312 | tf_op jit(solution)/shard_map/ppermute | solution.py:390
  73.1 2.3 collective-permute-done.2
  75.4 10.9 %collective-permute-start.3 = (bf16[64,512]{1,0:T(8,128)(2,1)S(1)}, bf16[64,512]{1,0:T(8,128)(2,1)S(1)}, u32[]{:S(2)}, u32[]{:S(2)}) collective-permute-start(bf16[64,512]{1,0:T(8,128)(2,1)S(1)} %pad_maximum_fusion.2), channel_id=1, source_target_pairs={{0,1},{1,0},{2,3},{3,2},{4,5},{5,4},{6,7},{7,6},{8,9},{9,8},{10,11... | collective-permute-start | bytes 196616 | tf_op jit(solution)/shard_map/ppermute | solution.py:390
  86.3 1.1 reshape.52
  87.4 0.3 copy.17
  87.6 0.7 copy.18.bias_ref
  88.3 12.5 %legendre_table.1 = (bf16[12,384,384]{2,1,0:T(8,128)(2,1)}, f32[16,128]{1,0:T(8,128)}) custom-call(s32[1]{0:T(128)} %bitcast.4.first_ref, f32[16,128]{1,0:T(8,128)} %copy.18.bias_ref), custom_call_target="tpu_custom_call" | custom-call | flops 100000000 | bytes 20000000 | tf_op jit(solution)/shard_map/legendre_table/pallas_call | solution.py:156
  100.8 0.0 collective-permute-done.3
  100.9 5.7 %all_gather.6 = bf16[256,512]{1,0:T(8,128)(2,1)S(1)} all-gather(bf16[128,512]{1,0:T(8,128)(2,1)S(1)} %pad_maximum_fusion.1), channel_id=1, replica_groups={{0,32},{64,96},{128,160},{192,224},{256,288},{320,352},{384,416},{448,4..., dimensions={0}, use_global_device_ids=true | all-gather | bytes 393216 | tf_op jit(solution)/shard_map/all_gather | solution.py:396
  106.6 0.0 all-to-all-done
  106.6 0.0 copy-start
  106.6 0.8 copy-done
  107.4 9.6 %spectral_filter.1 = bf16[768,384]{1,0:T(8,128)(2,1)} custom-call(bf16[768,384]{1,0:T(8,128)(2,1)} %bitcast.36, bf16[12,384,384]{2,1,0:T(8,128)(2,1)} %get-tuple-element.12.p_ref, f32[2,32,384]{2,1,0:T(8,128)} %w_ref.1), custom_call_target="tpu_custom_call" | custom-call | tf_op jit(solution)/shard_map/spectral_filter/pallas_call | solution.py:235
  117.0 0.1 reshape.58
  117.1 0.1 slice_bitcast_fusion.1
  117.2 0.1 copy.22
  117.3 0.1 reshape_squeeze.6
  117.4 0.7 pad_maximum_fusion
  118.2 0.0 all-gather.2.cloned.1.call-update
  118.2 39.3 %all_to_all.20 = bf16[32,24,384]{2,1,0:T(8,128)(2,1)} all-to-all(bf16[32,24,384]{2,1,0:T(8,128)(2,1)} %bitcast.37), channel_id=1, replica_groups=mesh['field'=16,'spatial'=32] {'spatial'}, dimensions={0} | all-to-all | bytes 1179648 | tf_op jit(solution)/shard_map/all_to_all | solution.py:422
  157.5 4.5 %inverse_fourier.1 = bf16[1536,256]{1,0:T(8,128)(2,1)} custom-call(bf16[768,384]{1,0:T(8,128)(2,1)} %bitcast.38, bf16[768,1024]{1,0:T(8,128)(2,1)} %get-tuple-element.14.t_ref, bf16[384,1024]{1,0:T(8,128)(2,1)} %bitcast.31), custom_call_target="tpu_custom_call" | custom-call | tf_op jit(solution)/shard_map/inverse_fourier/pallas_call | solution.py:273
  162.0 50.9 %all_to_all.21 = bf16[16,96,256]{2,1,0:T(8,128)(2,1)} all-to-all(bf16[16,96,256]{2,1,0:T(8,128)(2,1)} %bitcast.32), channel_id=1, replica_groups=mesh['field'=16,'spatial'=32] {'field'}, dimensions={0} | all-to-all | bytes 1572864 | tf_op jit(solution)/shard_map/all_to_all | solution.py:426
  212.9 0.0 all-gather.2.cloned.1.call-done
  212.9 10.2 %pointwise_mlp.1 = bf16[1536,256]{1,0:T(8,128)(2,1)} custom-call(bf16[1536,256]{1,0:T(8,128)(2,1)} %bitcast.34, bf16[16,1024,128]{2,1,0:T(8,128)(2,1)} %bitcast.29, f32[16,128]{1,0:T(8,128)} %get-tuple-element.16.bias_ref), custom_call_target="tpu_custom_call" | custom-call | tf_op jit(solution)/shard_map/pointwise_mlp/pallas_call | solution.py:329
  223.2 45.1 %all_to_all.22 = bf16[16,96,256]{2,1,0:T(8,128)(2,1)} all-to-all(bf16[16,96,256]{2,1,0:T(8,128)(2,1)} %bitcast.35), channel_id=1, replica_groups=mesh['field'=16,'spatial'=32] {'field'}, dimensions={0} | all-to-all | bytes 1572864 | tf_op jit(solution)/shard_map/all_to_all | solution.py:430
  268.2 2.1 home_layout.1
  (9 shorter events, 0.1 us)
Async XLA Ops:
  12.1 94.5 %all-to-all-start = ((bf16[32,24,384]{2,1,0:T(8,128)(2,1)}), bf16[32,24,384]{2,1,0:T(8,128)(2,1)S(1)}, u32[]{:S(2)}, u32[]{:S(2)}) async-start(bf16[32,24,384]{2,1,0:T(8,128)(2,1)} %bitcast.40), calls=%async_computation | async-start | bytes 1179648 | tf_op jit(solution)/shard_map/all_to_all | solution.py:414
  33.2 179.7 %all-gather.2.cloned.1.call-start = ((), (), s32[]{:S(2)}) async-start(), calls=%async_computation.4 | async-start | bytes 4456448 | tf_op jit(solution)/shard_map/all_gather | solution.py:405
  34.0 25.6 %collective-permute-start = (bf16[8,512]{1,0:T(8,128)(2,1)S(1)}, bf16[8,512]{1,0:T(8,128)(2,1)S(1)}, u32[]{:S(2)}, u32[]{:S(2)}) collective-permute-start(bf16[8,512]{1,0:T(8,128)(2,1)S(1)} %pad_maximum_fusion.5), channel_id=1, source_target_pairs={{0,64},{1,65},{2,66},{3,67},{4,68},{5,69},{6,70},{7,71},{8,72},{9,... | collective-permute-start | bytes 24584 | tf_op jit(solution)/shard_map/ppermute | solution.py:390
  60.3 6.4 %collective-permute-start.1 = (bf16[16,512]{1,0:T(8,128)(2,1)S(1)}, bf16[16,512]{1,0:T(8,128)(2,1)S(1)}, u32[]{:S(2)}, u32[]{:S(2)}) collective-permute-start(bf16[16,512]{1,0:T(8,128)(2,1)S(1)} %pad_maximum_fusion.4), channel_id=1, source_target_pairs={{0,128},{1,129},{2,130},{3,131},{4,132},{5,133},{6,134},{7,135},{8... | collective-permute-start | bytes 49160 | tf_op jit(solution)/shard_map/ppermute | solution.py:390
  66.8 8.6 %collective-permute-start.2 = (bf16[32,512]{1,0:T(8,128)(2,1)S(1)}, bf16[32,512]{1,0:T(8,128)(2,1)S(1)}, u32[]{:S(2)}, u32[]{:S(2)}) collective-permute-start(bf16[32,512]{1,0:T(8,128)(2,1)S(1)} %pad_maximum_fusion.3), channel_id=1, source_target_pairs={{0,256},{1,257},{2,258},{3,259},{4,260},{5,261},{6,262},{7,263},{8... | collective-permute-start | bytes 98312 | tf_op jit(solution)/shard_map/ppermute | solution.py:390
  75.4 25.5 %collective-permute-start.3 = (bf16[64,512]{1,0:T(8,128)(2,1)S(1)}, bf16[64,512]{1,0:T(8,128)(2,1)S(1)}, u32[]{:S(2)}, u32[]{:S(2)}) collective-permute-start(bf16[64,512]{1,0:T(8,128)(2,1)S(1)} %pad_maximum_fusion.2), channel_id=1, source_target_pairs={{0,1},{1,0},{2,3},{3,2},{4,5},{5,4},{6,7},{7,6},{8,9},{9,8},{10,11... | collective-permute-start | bytes 196616 | tf_op jit(solution)/shard_map/ppermute | solution.py:390
  106.6 0.8 copy-start
Sparse Core Ops, SparseCore 0:
  118.3 62.4 all-gather.1

commit v5 on v3

--- a/solution.py
+++ b/solution.py
@@ -389,13 +389,27 @@
     column = gather_first(proj_in, proj_out)
     bias = bias_in.reshape(16, 16, 2, 4).transpose(1, 2, 0, 3).reshape(16, LANES)
     rows = field_in.transpose(1, 0, 2).reshape(ROWS, NLON)
-    spectrum, table = forward(rows)
-    pencil = lax.all_to_all(
-        spectrum.reshape(BANDS, 2 * ORDERS, ROWS), "spatial", split_axis=0, concat_axis=0, tiled=True
+    first = (lax.axis_index("spatial") * ORDERS).astype(jnp.int32).reshape(1)
+
+    def analyse(step, carry):
+        spectrum, table = forward(rows)
+        pencil = lax.all_to_all(
+            spectrum.reshape(BANDS, 2 * ORDERS, ROWS),
+            "spatial",
+            split_axis=0,
+            concat_axis=0,
+            tiled=True,
+        )
+        polar, laid = legendre(first, bias)
+        return spectral_filter(pencil.reshape(PARTS, ROWS), polar, spectral_weight), table, laid
+
+    steps = 1 + (lax.axis_index("field") >> 8)
+    synth, table, bias = lax.fori_loop(
+        0,
+        steps,
+        analyse,
+        (jnp.zeros((PARTS, ROWS), BF16), jnp.zeros((PARTS, NLON), BF16), bias),
     )
-    first = (lax.axis_index("spatial") * ORDERS).astype(jnp.int32).reshape(1)
-    polar, bias = legendre(first, bias)
-    synth = spectral_filter(pencil.reshape(PARTS, ROWS), polar, spectral_weight)
     synth, column = lax.optimization_barrier((synth, column))
     weights = gather_second(column)
     returned = lax.all_to_all(

time: 280 us -> 274 us (0.979)
  waiting for transfers between devices: 50.6 us -> 42.7 us
    all_gather x1, waiting for transfers between devices: 45.3 us -> 32.1 us  [gather_first(): lax.all_gather(both, ('spatial', 'field'), axis=0, axis_index_groups=colu...]
    all_to_all x1, waiting for transfers between devices: 5.25 us -> 10.6 us  [analyse(): lax.all_to_all(spectrum.reshape(BANDS, 2 * ORDERS, ROWS), 'spatial', spli...]
  transfers between devices with their start and end apart: 3 -> 3, of which waited for: 2 -> 2; matrix products, arithmetic and copies ran while one was open for 1% -> 2% of each run, Pallas kernels for 10% -> 11%
where the time goes in v5:
time: 274 us; the launch traced here: 273 us
  blocking collectives  145 us (53%)
  waiting for transfers between devices  42.7 us (16%)
  Pallas kernels  41.9 us (15%)
  starting transfers between devices  21.2 us (8%)
  between operations  13.5 us (5%)
  local copies, waits for them, and re-layouts  6.81 us (2%)
    all_to_all x1, blocking collectives, shards(): lax.all_to_all(mixed.reshape(MEMBERS, BLOCK, LONS), 'field', split_axis=0...  65.1 us
    all_to_all x1, blocking collectives, shards(): lax.all_to_all(result.reshape(MEMBERS, BLOCK, LONS), 'field', split_axis=...  45.1 us
    all_to_all x1, blocking collectives, shards(): lax.all_to_all(synth.reshape(BANDS, 2 * ORDERS, ROWS), 'spatial', split_a...  34.4 us
    all_gather x1, waiting for transfers between devices, gather_first(): lax.all_gather(both, ('spatial', 'field'), axis=0, axis_index_groups=colu...  32.1 us
    all_to_all x1, starting transfers between devices, analyse(): lax.all_to_all(spectrum.reshape(BANDS, 2 * ORDERS, ROWS), 'spatial', spli...  21.1 us
    pallas_call x1, Pallas kernels, legendre(): pl.pallas_call(legendre_kernel, out_shape=(jax.ShapeDtypeStruct((ORDERS,...  11.8 us
    all_to_all x1, waiting for transfers between devices, analyse(): lax.all_to_all(spectrum.reshape(BANDS, 2 * ORDERS, ROWS), 'spatial', spli...  10.6 us
    pallas_call x1, Pallas kernels, mlp(): pl.pallas_call(mlp_kernel, grid=(blocks // take,), out_shape=jax.ShapeDty...  10.2 us
  transfers between devices with their start and end apart: 3, of which 2 were waited for; matrix products, arithmetic and copies ran while one was open for 2% of the time, Pallas kernels for 11%

profile of v5, /device:TPU:1, one launch (start us, length us, event | category | flops | bytes accessed | tf_op | source)
XLA Modules:
  0.0 272.8 jit_solution(6045508912407880158)
XLA Ops:
  6.5 0.0 copy-start.1
  6.5 0.0 copy-start.3
  6.5 0.0 all-gather.3.cloned.1.call-start
  6.5 1.4 fusion.2
  7.9 0.0 all-gather.3.cloned.1.call-update
  8.0 0.0 all-gather.5.cloned.1.call-start
  8.0 1.1 reshape.48
  9.1 0.3 copy.19
  9.4 0.1 copy.20
  9.5 0.6 copy.31
  10.1 0.9 broadcast_in_dim.6
  10.9 1.4 broadcast_in_dim.7
  12.3 0.0 copy-done.1
  12.3 0.0 copy-done.3
  12.3 58.3 %while.14 = (s32[]{:T(128)}, bf16[768,384]{1,0:T(8,128)(2,1)}, bf16[768,1024]{1,0:T(8,128)(2,1)}, f32[16,128]{1,0:T(8,128)}, s32[]{:T(128)}, /*index=5*/bf16[384...) while((s32[]{:T(128)}, bf16[768,384]{1,0:T(8,128)(2,1)}, ...), condition=%wide.region_1.2_spmd, body=%wide.region_0.1_spmd.sunk | while | flops 100000000 | bytes 24128928 | solution.py:407
  12.3 4.4 %forward_fourier.1 = (bf16[768,384]{1,0:T(8,128)(2,1)}, bf16[768,1024]{1,0:T(8,128)(2,1)}) custom-call(bf16[384,1024]{1,0:T(8,128)(2,1)S(1)} %get-tuple-element.193.x_ref), custom_call_target="tpu_custom_call" | custom-call | tf_op jit(solution)/shard_map/while/body/forward_fourier/pallas_call | solution.py:75
  16.8 21.1 %all-to-all-start = ((bf16[32,24,384]{2,1,0:T(8,128)(2,1)}), bf16[32,24,384]{2,1,0:T(8,128)(2,1)S(1)}, u32[]{:S(2)}, u32[]{:S(2)}) async-start(bf16[32,24,384]{2,1,0:T(8,128)(2,1)} %bitcast.35), calls=%async_computation | async-start | bytes 1179648 | tf_op jit(solution)/shard_map/while/body/all_to_all | solution.py:396
  37.9 11.8 %legendre_table.1 = (bf16[12,384,384]{2,1,0:T(8,128)(2,1)}, f32[16,128]{1,0:T(8,128)}) custom-call(s32[1]{0:T(128)} %get-tuple-element.194.first_ref, f32[16,128]{1,0:T(8,128)S(1)} %get-tuple-element.195.bias_ref), custom_call_target="tpu_custom_call" | custom-call | flops 100000000 | bytes 20000000 | tf_op jit(solution)/shard_map/while/body/legendre_table/pallas_call | solution.py:156
  49.7 10.6 %all-to-all-done = bf16[32,24,384]{2,1,0:T(8,128)(2,1)S(1)} async-done(((bf16[32,24,384]{2,1,0:T(8,128)(2,1)}), bf16[32,24,384]{2,1,0:T(8,128)(2,1)S(1)}, u32[]{:S(2)}, u32[]{:S(2)}) %all-to-all-start) | async-done | bytes 589856 | tf_op jit(solution)/shard_map/while/body/all_to_all | solution.py:396
  60.3 0.0 copy-start
  60.3 0.8 copy-done
  61.1 9.6 %spectral_filter.1 = bf16[768,384]{1,0:T(8,128)(2,1)} custom-call(bf16[768,384]{1,0:T(8,128)(2,1)} %bitcast.33, bf16[12,384,384]{2,1,0:T(8,128)(2,1)} %get-tuple-element.165.p_ref, f32[2,32,384]{2,1,0:T(8,128)S(1)} %get-tuple-element.196.w_ref), custom_call_target="tpu_custom_call" | custom-call | tf_op jit(solution)/shard_map/while/body/spectral_filter/pallas_call | solution.py:235
  70.7 32.1 %all-gather.3.cloned.1.call-done = bf16[1024,512]{1,0:T(8,128)(2,1)} async-done(((bf16[32,512]{1,0:T(8,128)(2,1)}), bf16[1024,512]{1,0:T(8,128)(2,1)}) %all-gather.3.cloned.1.call-update) | async-done | bytes 1048592 | tf_op jit(solution)/shard_map/all_gather | solution.py:375
  102.8 1.3 reshape.56
  104.1 0.0 copy-start.4
  104.1 0.1 slice_bitcast_fusion.1
  104.2 0.0 copy-start.2
  104.3 0.1 copy.25
  104.4 0.1 reshape_squeeze.6
  104.5 0.7 pad_maximum_fusion
  105.2 0.0 all-gather.5.cloned.1.call-update
  105.2 0.0 copy-done.4
  105.3 34.4 %all_to_all.21 = bf16[32,24,384]{2,1,0:T(8,128)(2,1)} all-to-all(bf16[32,24,384]{2,1,0:T(8,128)(2,1)S(1)} %bitcast.42), channel_id=1, replica_groups=mesh['field'=16,'spatial'=32] {'spatial'}, dimensions={0} | all-to-all | bytes 1179648 | tf_op jit(solution)/shard_map/all_to_all | solution.py:415
  139.7 0.0 copy-done.2
  139.7 3.8 %inverse_fourier.1 = bf16[1536,256]{1,0:T(8,128)(2,1)} custom-call(bf16[768,384]{1,0:T(8,128)(2,1)} %bitcast.41, bf16[768,1024]{1,0:T(8,128)(2,1)S(1)} %copy-done.2, bf16[384,1024]{1,0:T(8,128)(2,1)S(1)} %get-tuple-element.201), custom_call_target="tpu_custom_call" | custom-call | tf_op jit(solution)/shard_map/inverse_fourier/pallas_call | solution.py:273
  143.4 0.0 copy-start.5
  143.4 65.1 %all_to_all.22 = bf16[16,96,256]{2,1,0:T(8,128)(2,1)} all-to-all(bf16[16,96,256]{2,1,0:T(8,128)(2,1)} %bitcast.37), channel_id=1, replica_groups=mesh['field'=16,'spatial'=32] {'field'}, dimensions={0} | all-to-all | bytes 1572864 | tf_op jit(solution)/shard_map/all_to_all | solution.py:419
  208.6 0.0 all-gather.5.cloned.1.call-done
  208.6 0.0 copy-done.5
  208.6 10.2 %pointwise_mlp.1 = bf16[1536,256]{1,0:T(8,128)(2,1)} custom-call(bf16[1536,256]{1,0:T(8,128)(2,1)} %bitcast.39, bf16[16,1024,128]{2,1,0:T(8,128)(2,1)} %bitcast.36, f32[16,128]{1,0:T(8,128)S(1)} %copy-done.5), custom_call_target="tpu_custom_call" | custom-call | tf_op jit(solution)/shard_map/pointwise_mlp/pallas_call | solution.py:329
  218.8 45.1 %all_to_all.23 = bf16[16,96,256]{2,1,0:T(8,128)(2,1)} all-to-all(bf16[16,96,256]{2,1,0:T(8,128)(2,1)} %bitcast.40), channel_id=1, replica_groups=mesh['field'=16,'spatial'=32] {'field'}, dimensions={0} | all-to-all | bytes 1572864 | tf_op jit(solution)/shard_map/all_to_all | solution.py:423
  263.9 2.1 home_layout.1
  (2 shorter events, 0.1 us)
Async XLA Ops:
  6.5 5.8 %copy-start.1 = (bf16[32,12,1024]{2,0,1:T(8,128)(2,1)S(1)}, bf16[32,12,1024]{2,0,1:T(8,128)(2,1)}, u32[]{:S(2)}) copy-start(bf16[32,12,1024]{2,0,1:T(8,128)(2,1)} %param.7) | copy-start | bytes 2359300
  6.5 5.8 %copy-start.3 = (f32[2,32,384]{2,1,0:T(8,128)S(1)}, f32[2,32,384]{2,1,0:T(8,128)}, u32[]{:S(2)}) copy-start(f32[2,32,384]{2,1,0:T(8,128)} %param.8) | copy-start | bytes 294916
  6.5 96.2 %all-gather.3.cloned.1.call-start = ((), (), s32[]{:S(2)}) async-start(), calls=%async_computation.4 | async-start | bytes 1081344 | tf_op jit(solution)/shard_map/all_gather | solution.py:375
  8.0 200.6 %all-gather.5.cloned.1.call-start = ((), (), s32[]{:S(2)}) async-start(), calls=%async_computation.5 | async-start | bytes 4456448 | tf_op jit(solution)/shard_map/all_gather | solution.py:384
  16.8 43.5 %all-to-all-start = ((bf16[32,24,384]{2,1,0:T(8,128)(2,1)}), bf16[32,24,384]{2,1,0:T(8,128)(2,1)S(1)}, u32[]{:S(2)}, u32[]{:S(2)}) async-start(bf16[32,24,384]{2,1,0:T(8,128)(2,1)} %bitcast.35), calls=%async_computation | async-start | bytes 1179648 | tf_op jit(solution)/shard_map/while/body/all_to_all | solution.py:396
  60.3 0.8 copy-start
  104.1 1.1 copy-start.4
  104.2 35.4 %copy-start.2 = (bf16[768,1024]{1,0:T(8,128)(2,1)S(1)}, bf16[768,1024]{1,0:T(8,128)(2,1)}, u32[]{:S(2)}) copy-start(bf16[768,1024]{1,0:T(8,128)(2,1)} %get-tuple-element.60.t_ref) | copy-start | bytes 4718596
  143.4 65.1 %copy-start.5 = (f32[16,128]{1,0:T(8,128)S(1)}, f32[16,128]{1,0:T(8,128)}, u32[]{:S(2)}) copy-start(f32[16,128]{1,0:T(8,128)} %get-tuple-element.62.bias_ref) | copy-start | bytes 24580
Sparse Core Ops, SparseCore 0:
  9.5 93.2 all-gather.2
  105.8 66.5 all-gather.4

commit v6 on v3

--- a/solution.py
+++ b/solution.py
@@ -28,6 +28,7 @@
 LATS = 3
 BLOCK = LATS * CHANS
 LANES = 128
+PAIRS = 3
 PAD = 16
 VMEM = 56 * 1024 * 1024
 
@@ -171,10 +172,10 @@
 
 
 def filter_kernel(r_ref, p_ref, w_ref, s_ref, rin, sout, quad):
-    pair = pl.program_id(0)
+    step = pl.program_id(0)
     group = 4 * CHANS
 
-    @pl.when(pair == 0)
+    @pl.when(step == 0)
     def _():
         for tile in range(3):
             rin[tile] = r_ref[:, lanes(tile)].astype(F32)
@@ -182,49 +183,51 @@
         quad[...] = jnp.sin(theta_of(lane)) * (math.pi / NLAT)
 
     lane32 = lax.broadcasted_iota(jnp.int32, (BANDS, group), 1) >> 5
-    tiles = []
-    for tile in range(3):
-        parts = [
-            rin[tile, pl.ds(4 * pair + part, BANDS, stride=2 * ORDERS), :] for part in range(4)
-        ]
-        blocks = []
-        for lat in range(4):
-            block = jnp.zeros((BANDS, group), F32)
+
+    def exchanged(blocks):
+        out = []
+        for to in range(4):
+            block = blocks[to]
+            for at in range(4):
+                if at != to:
+                    moved = pltpu.roll(blocks[at], (at - to) % 4 * CHANS, 1)
+                    block = jnp.where(lane32 == at, moved, block)
+            out.append(block)
+        return out
+
+    for part_pair in range(PAIRS):
+        row = 4 * (step * PAIRS + part_pair)
+        tiles = []
+        for tile in range(3):
+            parts = [
+                rin[tile, pl.ds(row + part, BANDS, stride=2 * ORDERS), :] for part in range(4)
+            ]
+            tiles.append(jnp.concatenate(exchanged(parts), axis=0).T)
+        data = jnp.concatenate(tiles, axis=1)
+        data = (data * quad[:1, :]).astype(BF16)
+
+        out = []
+        for item in range(2):
+            table = p_ref[2 * part_pair + item]
+            coef = lax.dot_general(
+                data[2 * CHANS * item : 2 * CHANS * (item + 1), :],
+                table,
+                (((1,), (1,)), ((), ())),
+                preferred_element_type=F32,
+            )
+            real, imag = coef[:CHANS], coef[CHANS:]
+            filtered = jnp.concatenate(
+                [w_ref[0] * real - w_ref[1] * imag, w_ref[0] * imag + w_ref[1] * real], axis=0
+            ).astype(BF16)
+            out.append(jnp.dot(filtered, table, preferred_element_type=F32))
+        synth = jnp.concatenate(out, axis=0)
+        for tile in range(3):
+            turned = synth[:, lanes(tile)].T
+            blocks = exchanged([turned[BANDS * lat : BANDS * (lat + 1), :] for lat in range(4)])
             for part in range(4):
-                shift = (part - lat) % 4 * CHANS
-                moved = pltpu.roll(parts[part], shift, 1) if shift else parts[part]
-                block = jnp.where(lane32 == part, moved, block)
-            blocks.append(block)
-        tiles.append(jnp.concatenate(blocks, axis=0).T)
-    data = jnp.concatenate(tiles, axis=1)
-    data = (data * quad[:1, :]).astype(BF16)
-
-    out = []
-    for item in range(2):
-        coef = lax.dot_general(
-            data[2 * CHANS * item : 2 * CHANS * (item + 1), :],
-            p_ref[item],
-            (((1,), (1,)), ((), ())),
-            preferred_element_type=F32,
-        )
-        real, imag = coef[:CHANS], coef[CHANS:]
-        filtered = jnp.concatenate(
-            [w_ref[0] * real - w_ref[1] * imag, w_ref[0] * imag + w_ref[1] * real], axis=0
-        ).astype(BF16)
-        out.append(jnp.dot(filtered, p_ref[item], preferred_element_type=F32))
-    synth = jnp.concatenate(out, axis=0)
-    for tile in range(3):
-        turned = synth[:, lanes(tile)].T
-        lats = [turned[BANDS * lat : BANDS * (lat + 1), :] for lat in range(4)]
-        for part in range(4):
-            block = jnp.zeros((BANDS, group), F32)
-            for lat in range(4):
-                shift = (lat - part) % 4 * CHANS
-                moved = pltpu.roll(lats[lat], shift, 1) if shift else lats[lat]
-                block = jnp.where(lane32 == lat, moved, block)
-            sout[tile, pl.ds(4 * pair + part, BANDS, stride=2 * ORDERS), :] = block
-
-    @pl.when(pair == ORDERS // 2 - 1)
+                sout[tile, pl.ds(row + part, BANDS, stride=2 * ORDERS), :] = blocks[part]
+
+    @pl.when(step == pl.num_programs(0) - 1)
     def _():
         for tile in range(3):
             s_ref[:, lanes(tile)] = sout[tile].astype(BF16)
@@ -234,11 +237,11 @@
     same2 = lambda pair: (0, 0)
     return pl.pallas_call(
         filter_kernel,
-        grid=(ORDERS // 2,),
+        grid=(ORDERS // 2 // PAIRS,),
         out_shape=jax.ShapeDtypeStruct((PARTS, ROWS), BF16),
         in_specs=[
             pl.BlockSpec((PARTS, ROWS), same2),
-            pl.BlockSpec((2, LMAX, NLAT), lambda pair: (pair, 0, 0)),
+            pl.BlockSpec((2 * PAIRS, LMAX, NLAT), lambda pair: (pair, 0, 0)),
             pl.BlockSpec((2, CHANS, LMAX), lambda pair: (0, 0, 0)),
         ],
         out_specs=pl.BlockSpec((PARTS, ROWS), same2),
@@ -279,6 +282,12 @@
         compiler_params=params(),
         name="inverse_fourier",
     )(returned, table, rows)
+
+
+def gelu(x):
+    root = math.sqrt(2.0 / math.pi)
+    half = 0.5 * x
+    return half + half * jnp.tanh(x * (root + (root * 0.044715) * (x * x)))
 
 
 def mlp_kernel(r_ref, w_ref, bias_ref, o_ref, points, act, w_out):
@@ -309,7 +318,7 @@
     for lat in range(LATS):
         cols = slice(lat * LONS, (lat + 1) * LONS)
         pre = jnp.dot(w_in, points[:, cols], preferred_element_type=F32) + bias
-        act[at, cols] = jax.nn.gelu(pre, approximate=True).astype(BF16)
+        act[at, cols] = gelu(pre).astype(BF16)
 
     @pl.when(step == pl.num_programs(0) - 1)
     def _():
@@ -324,7 +333,7 @@
 
 def mlp(received, weights, bias):
     blocks = weights.shape[0]
-    take = 2
+    take = 8
     same2 = lambda step: (0, 0)
     return pl.pallas_call(
         mlp_kernel,
@@ -390,17 +399,23 @@
     bias = bias_in.reshape(16, 16, 2, 4).transpose(1, 2, 0, 3).reshape(16, LANES)
     rows = field_in.transpose(1, 0, 2).reshape(ROWS, NLON)
     spectrum, table = forward(rows)
-    pencil = lax.all_to_all(
-        spectrum.reshape(BANDS, 2 * ORDERS, ROWS), "spatial", split_axis=0, concat_axis=0, tiled=True
+    first = (lax.axis_index("spatial") * ORDERS).astype(jnp.int32).reshape(1)
+
+    def swap(blocks):
+        return lax.all_to_all(blocks, "spatial", split_axis=0, concat_axis=0, tiled=True)
+
+    def filtered(step, carry):
+        held, laid = carry
+        polar, laid = legendre(first, laid)
+        synth = spectral_filter(swap(held).reshape(PARTS, ROWS), polar, spectral_weight)
+        return swap(synth.reshape(BANDS, 2 * ORDERS, ROWS)), laid
+
+    steps = 1 + (lax.axis_index("field") >> 8)
+    returned, bias = lax.fori_loop(
+        0, steps, filtered, (spectrum.reshape(BANDS, 2 * ORDERS, ROWS), bias)
     )
-    first = (lax.axis_index("spatial") * ORDERS).astype(jnp.int32).reshape(1)
-    polar, bias = legendre(first, bias)
-    synth = spectral_filter(pencil.reshape(PARTS, ROWS), polar, spectral_weight)
-    synth, column = lax.optimization_barrier((synth, column))
+    returned, column = lax.optimization_barrier((returned, column))
     weights = gather_second(column)
-    returned = lax.all_to_all(
-        synth.reshape(BANDS, 2 * ORDERS, ROWS), "spatial", split_axis=0, concat_axis=0, tiled=True
-    )
     mixed = inverse(returned.reshape(PARTS, ROWS), table, rows)
     points = lax.all_to_all(
         mixed.reshape(MEMBERS, BLOCK, LONS), "field", split_axis=0, concat_axis=0, tiled=True

time: 280 us -> 250 us (0.89)
  blocking collectives: 143 us -> 102 us
  waiting for transfers between devices: 50.6 us -> 59.8 us
  starting transfers between devices: 21.2 us -> 27.9 us
  Pallas kernels: 44.5 us -> 40 us
    all_to_all x1 -> x0, blocking collectives: 32.9 us -> none  [shards(): lax.all_to_all(synth.reshape(BANDS, 2 * ORDERS, ROWS), 'spatial', split_a...]
    all_to_all x1 -> x2, waiting for transfers between devices: 5.25 us -> 29.1 us  [swap(): lax.all_to_all(blocks, 'spatial', split_axis=0, concat_axis=0, tiled=True)]
    all_gather x1, waiting for transfers between devices: 45.3 us -> 23 us  [gather_first(): lax.all_gather(both, ('spatial', 'field'), axis=0, axis_index_groups=colu...]
    all_to_all x1, blocking collectives: 65.1 us -> 51.5 us  [shards(): lax.all_to_all(mixed.reshape(MEMBERS, BLOCK, LONS), 'field', split_axis=0...]
    all_gather x1, waiting for transfers between devices: 0.01 us -> 7.68 us  [gather_second(): lax.all_gather(block, 'spatial', axis=0, axis_index_groups=planes, tiled=...]
    all_to_all x1 -> x2, starting transfers between devices: 21.1 us -> 27.8 us  [swap(): lax.all_to_all(blocks, 'spatial', split_axis=0, concat_axis=0, tiled=True)]
    all_to_all x1, blocking collectives: 45.1 us -> 50.4 us  [shards(): lax.all_to_all(result.reshape(MEMBERS, BLOCK, LONS), 'field', split_axis=...]
  transfers between devices with their start and end apart: 3 -> 4, of which waited for: 2 -> 4; matrix products, arithmetic and copies ran while one was open for 1% -> 1% of each run, Pallas kernels for 10% -> 12%
where the time goes in v6:
time: 250 us
  blocking collectives  102 us (41%)
  waiting for transfers between devices  59.8 us (24%)
  Pallas kernels  40 us (16%)
  starting transfers between devices  27.9 us (11%)
  between operations  13.5 us (5%)
  local copies, waits for them, and re-layouts  4.52 us (2%)
    all_to_all x1, blocking collectives, shards(): lax.all_to_all(mixed.reshape(MEMBERS, BLOCK, LONS), 'field', split_axis=0...  51.5 us
    all_to_all x1, blocking collectives, shards(): lax.all_to_all(result.reshape(MEMBERS, BLOCK, LONS), 'field', split_axis=...  50.4 us
    all_to_all x2, waiting for transfers between devices, swap(): lax.all_to_all(blocks, 'spatial', split_axis=0, concat_axis=0, tiled=True)  29.1 us
    all_to_all x2, starting transfers between devices, swap(): lax.all_to_all(blocks, 'spatial', split_axis=0, concat_axis=0, tiled=True)  27.8 us
    all_gather x1, waiting for transfers between devices, gather_first(): lax.all_gather(both, ('spatial', 'field'), axis=0, axis_index_groups=colu...  23 us
    pallas_call x1, Pallas kernels, legendre(): pl.pallas_call(legendre_kernel, out_shape=(jax.ShapeDtypeStruct((ORDERS,...  12.5 us
    pallas_call x1, Pallas kernels, mlp(): pl.pallas_call(mlp_kernel, grid=(blocks // take,), out_shape=jax.ShapeDty...  8.05 us
    all_gather x1, waiting for transfers between devices, gather_second(): lax.all_gather(block, 'spatial', axis=0, axis_index_groups=planes, tiled=...  7.68 us
  transfers between devices with their start and end apart: 4, of which 4 were waited for; matrix products, arithmetic and copies ran while one was open for 1% of the time, Pallas kernels for 12%

profile of v6, /device:TPU:1, one launch (start us, length us, event | category | flops | bytes accessed | tf_op | source)
XLA Modules:
  0.0 249.5 jit_solution(3478772966191853069)
XLA Ops:
  6.5 0.0 all-gather.3.cloned.1.call-start
  6.5 1.3 fusion.2
  7.9 0.0 all-gather.3.cloned.1.call-update
  7.9 0.0 all-gather.5.cloned.1.call-start
  7.9 5.6 %forward_fourier.1 = (bf16[768,384]{1,0:T(8,128)(2,1)}, bf16[768,1024]{1,0:T(8,128)(2,1)}) custom-call(bf16[384,1024]{1,0:T(8,128)(2,1)} %bitcast.36), custom_call_target="tpu_custom_call" | custom-call | tf_op jit(solution)/shard_map/forward_fourier/pallas_call | solution.py:76
  13.5 1.1 reshape.50
  14.6 0.3 copy.17
  14.9 0.1 copy.18
  15.0 78.1 %while.12 = (s32[]{:T(128)}, bf16[32,24,384]{2,1,0:T(8,128)(2,1)}, f32[16,128]{1,0:T(8,128)S(1)}, s32[]{:T(128)}, s32[1]{0:T(128)}, /*index=5*/f32[2,32,384]{2,1,0:T(8,128)}, s32[]{:T(128)}) while((s32[]{:T(128)}, bf16[32,24,384]{2,1,0:T(8,128)(2,1)}, f32[16,128]{1,0:T(8,128)S(1)}, s32[]{:T(128)}, s32[1]{0:T(128)}, ...), condition=%wide.region_1.2_spmd, body=%wide.region_0.1_spmd.sunk | while | flops 100000000 | bytes 25914792 | solution.py:414
  15.0 21.1 %all-to-all-start = ((bf16[32,24,384]{2,1,0:T(8,128)(2,1)}), bf16[32,24,384]{2,1,0:T(8,128)(2,1)S(1)}, u32[]{:S(2)}, u32[]{:S(2)}) async-start(bf16[32,24,384]{2,1,0:T(8,128)(2,1)} %get-tuple-element.133), calls=%async_computation | async-start | bytes 1179648 | tf_op jit(solution)/shard_map/while/body/all_to_all | solution.py:405
  36.1 0.6 copy.37.bias_ref
  36.7 12.5 %legendre_table.1 = (bf16[12,384,384]{2,1,0:T(8,128)(2,1)}, f32[16,128]{1,0:T(8,128)S(1)}) custom-call(s32[1]{0:T(128)} %get-tuple-element.143.first_ref, f32[16,128]{1,0:T(8,128)} %copy.37.bias_ref), custom_call_target="tpu_custom_call" | custom-call | flops 100000000 | bytes 20000000 | tf_op jit(solution)/shard_map/while/body/legendre_table/pallas_call | solution.py:157
  49.2 9.9 %all-to-all-done = bf16[32,24,384]{2,1,0:T(8,128)(2,1)S(1)} async-done(((bf16[32,24,384]{2,1,0:T(8,128)(2,1)}), bf16[32,24,384]{2,1,0:T(8,128)(2,1)S(1)}, u32[]{:S(2)}, u32[]{:S(2)}) %all-to-all-start) | async-done | bytes 589856 | tf_op jit(solution)/shard_map/while/body/all_to_all | solution.py:405
  59.1 0.0 copy-start
  59.1 0.8 copy-done
  59.9 7.3 %spectral_filter.1 = bf16[768,384]{1,0:T(8,128)(2,1)} custom-call(bf16[768,384]{1,0:T(8,128)(2,1)} %bitcast.33, bf16[12,384,384]{2,1,0:T(8,128)(2,1)} %get-tuple-element.123.p_ref, f32[2,32,384]{2,1,0:T(8,128)} %get-tuple-element.144.w_ref), custom_call_target="tpu_custom_call" | custom-call | tf_op jit(solution)/shard_map/while/body/spectral_filter/pallas_call | solution.py:238
  67.2 6.7 %all-to-all-start.1 = ((bf16[32,24,384]{2,1,0:T(8,128)(2,1)}), bf16[32,24,384]{2,1,0:T(8,128)(2,1)}, u32[]{:S(2)}, u32[]{:S(2)}) async-start(bf16[32,24,384]{2,1,0:T(8,128)(2,1)} %bitcast.34), calls=%async_computation.1 | async-start | bytes 1179648 | tf_op jit(solution)/shard_map/while/body/all_to_all | solution.py:405
  73.9 19.2 %all-to-all-done.1 = bf16[32,24,384]{2,1,0:T(8,128)(2,1)} async-done(((bf16[32,24,384]{2,1,0:T(8,128)(2,1)}), bf16[32,24,384]{2,1,0:T(8,128)(2,1)}, u32[]{:S(2)}, u32[]{:S(2)}) %all-to-all-start.1) | async-done | bytes 589856 | tf_op jit(solution)/shard_map/while/body/all_to_all | solution.py:405
  93.1 23.0 %all-gather.3.cloned.1.call-done = bf16[1024,512]{1,0:T(8,128)(2,1)} async-done(((bf16[32,512]{1,0:T(8,128)(2,1)}), bf16[1024,512]{1,0:T(8,128)(2,1)}) %all-gather.3.cloned.1.call-update) | async-done | bytes 1048592 | tf_op jit(solution)/shard_map/all_gather | solution.py:384
  116.1 1.3 reshape.56
  117.4 0.1 slice_bitcast_fusion.1
  117.6 0.1 copy.22
  117.7 0.1 reshape_squeeze.6
  117.8 0.7 pad_maximum_fusion
  118.5 0.0 all-gather.5.cloned.1.call-update
  118.6 4.5 %inverse_fourier.1 = bf16[1536,256]{1,0:T(8,128)(2,1)} custom-call(bf16[768,384]{1,0:T(8,128)(2,1)} %bitcast.8.r_ref, bf16[768,1024]{1,0:T(8,128)(2,1)} %get-tuple-element.48.t_ref, bf16[384,1024]{1,0:T(8,128)(2,1)} %bitcast.37), custom_call_target="tpu_custom_call" | custom-call | tf_op jit(solution)/shard_map/inverse_fourier/pallas_call | solution.py:276
  123.1 51.5 %all_to_all.22 = bf16[16,96,256]{2,1,0:T(8,128)(2,1)} all-to-all(bf16[16,96,256]{2,1,0:T(8,128)(2,1)} %bitcast.38), channel_id=1, replica_groups=mesh['field'=16,'spatial'=32] {'field'}, dimensions={0} | all-to-all | bytes 1572864 | tf_op jit(solution)/shard_map/all_to_all | solution.py:420
  174.5 7.7 %all-gather.5.cloned.1.call-done = bf16[16384,128]{1,0:T(8,128)(2,1)} async-done(((bf16[1024,128]{1,0:T(8,128)(2,1)}), bf16[16384,128]{1,0:T(8,128)(2,1)}) %all-gather.5.cloned.1.call-update) | async-done | bytes 4194320 | tf_op jit(solution)/shard_map/all_gather | solution.py:393
  182.2 8.0 %pointwise_mlp.1 = bf16[1536,256]{1,0:T(8,128)(2,1)} custom-call(bf16[1536,256]{1,0:T(8,128)(2,1)} %bitcast.40, bf16[16,1024,128]{2,1,0:T(8,128)(2,1)} %bitcast.35, f32[16,128]{1,0:T(8,128)S(1)} %get-tuple-element.50.bias_ref), custom_call_target="tpu_custom_call" | custom-call | tf_op jit(solution)/shard_map/pointwise_mlp/pallas_call | solution.py:338
  190.2 50.4 %all_to_all.23 = bf16[16,96,256]{2,1,0:T(8,128)(2,1)} all-to-all(bf16[16,96,256]{2,1,0:T(8,128)(2,1)} %bitcast.41), channel_id=1, replica_groups=mesh['field'=16,'spatial'=32] {'field'}, dimensions={0} | all-to-all | bytes 1572864 | tf_op jit(solution)/shard_map/all_to_all | solution.py:424
  240.6 2.1 home_layout.1
  (2 shorter events, 0.1 us)
Async XLA Ops:
  6.5 109.6 %all-gather.3.cloned.1.call-start = ((), (), s32[]{:S(2)}) async-start(), calls=%async_computation.4 | async-start | bytes 1081344 | tf_op jit(solution)/shard_map/all_gather | solution.py:384
  7.9 174.3 %all-gather.5.cloned.1.call-start = ((), (), s32[]{:S(2)}) async-start(), calls=%async_computation.5 | async-start | bytes 4456448 | tf_op jit(solution)/shard_map/all_gather | solution.py:393
  15.0 44.2 %all-to-all-start = ((bf16[32,24,384]{2,1,0:T(8,128)(2,1)}), bf16[32,24,384]{2,1,0:T(8,128)(2,1)S(1)}, u32[]{:S(2)}, u32[]{:S(2)}) async-start(bf16[32,24,384]{2,1,0:T(8,128)(2,1)} %get-tuple-element.133), calls=%async_computation | async-start | bytes 1179648 | tf_op jit(solution)/shard_map/while/body/all_to_all | solution.py:405
  59.1 0.8 copy-start
  67.2 25.9 %all-to-all-start.1 = ((bf16[32,24,384]{2,1,0:T(8,128)(2,1)}), bf16[32,24,384]{2,1,0:T(8,128)(2,1)}, u32[]{:S(2)}, u32[]{:S(2)}) async-start(bf16[32,24,384]{2,1,0:T(8,128)(2,1)} %bitcast.34), calls=%async_computation.1 | async-start | bytes 1179648 | tf_op jit(solution)/shard_map/while/body/all_to_all | solution.py:405
Sparse Core Ops, SparseCore 0:
  9.5 106.5 all-gather.2
  119.1 63.0 all-gather.4

commit v7 on v6

--- a/solution.py
+++ b/solution.py
@@ -374,18 +374,21 @@
     )(received)
 
 
-SENT = 32
-
-
 def gather_first(proj_in, proj_out):
     column = [[xy * 32 + place for place in range(32)] for xy in range(16)]
     both = jnp.concatenate([proj_in, proj_out], axis=0)
-    both = jnp.pad(both, ((0, SENT - both.shape[0]), (0, 0)))
-    return lax.all_gather(both, ("spatial", "field"), axis=0, axis_index_groups=column, tiled=True)
+    return lax.all_to_all(
+        jnp.broadcast_to(both[None], (32,) + both.shape),
+        ("spatial", "field"),
+        split_axis=0,
+        concat_axis=0,
+        axis_index_groups=column,
+        tiled=True,
+    )
 
 
 def gather_second(column):
-    split = column.reshape(32, SENT // 4, HID // FULL, FULL)
+    split = column.reshape(32, 2, HID // FULL, FULL)
     w_in = split[:, 0].reshape(LANES, 4, LANES).transpose(1, 0, 2).reshape(FULL, LANES)
     w_out = split[:, 1].reshape(LANES, FULL).T
     block = jnp.concatenate([w_in, w_out], axis=0)
@@ -399,23 +402,17 @@
     bias = bias_in.reshape(16, 16, 2, 4).transpose(1, 2, 0, 3).reshape(16, LANES)
     rows = field_in.transpose(1, 0, 2).reshape(ROWS, NLON)
     spectrum, table = forward(rows)
+    spectrum, column = lax.optimization_barrier((spectrum, column))
+    weights = gather_second(column)
+    pencil = lax.all_to_all(
+        spectrum.reshape(BANDS, 2 * ORDERS, ROWS), "spatial", split_axis=0, concat_axis=0, tiled=True
+    )
     first = (lax.axis_index("spatial") * ORDERS).astype(jnp.int32).reshape(1)
-
-    def swap(blocks):
-        return lax.all_to_all(blocks, "spatial", split_axis=0, concat_axis=0, tiled=True)
-
-    def filtered(step, carry):
-        held, laid = carry
-        polar, laid = legendre(first, laid)
-        synth = spectral_filter(swap(held).reshape(PARTS, ROWS), polar, spectral_weight)
-        return swap(synth.reshape(BANDS, 2 * ORDERS, ROWS)), laid
-
-    steps = 1 + (lax.axis_index("field") >> 8)
-    returned, bias = lax.fori_loop(
-        0, steps, filtered, (spectrum.reshape(BANDS, 2 * ORDERS, ROWS), bias)
-    )
-    returned, column = lax.optimization_barrier((returned, column))
-    weights = gather_second(column)
+    polar, bias = legendre(first, bias)
+    synth = spectral_filter(pencil.reshape(PARTS, ROWS), polar, spectral_weight)
+    returned = lax.all_to_all(
+        synth.reshape(BANDS, 2 * ORDERS, ROWS), "spatial", split_axis=0, concat_axis=0, tiled=True
+    )
     mixed = inverse(returned.reshape(PARTS, ROWS), table, rows)
     points = lax.all_to_all(
         mixed.reshape(MEMBERS, BLOCK, LONS), "field", split_axis=0, concat_axis=0, tiled=True

time: 250 us -> 251 us (level)
  blocking collectives: 102 us -> 144 us
  waiting for transfers between devices: 59.8 us -> 23.5 us
  starting transfers between devices: 27.9 us -> 24.2 us
    all_to_all x0 -> x1, blocking collectives: none -> 29.6 us  [shards(): lax.all_to_all(synth.reshape(BANDS, 2 * ORDERS, ROWS), 'spatial', split_a...]
    all_gather x1 -> x0, waiting for transfers between devices: 23 us -> none  [gather_first(): lax.all_gather(both, ('spatial', 'field'), axis=0, axis_index_groups=colu...]
    all_to_all x1, blocking collectives: 51.5 us -> 69.5 us  [shards(): lax.all_to_all(mixed.reshape(MEMBERS, BLOCK, LONS), 'field', split_axis=0...]
    all_gather x1, waiting for transfers between devices: 7.68 us -> 0.01 us  [gather_second(): lax.all_gather(block, 'spatial', axis=0, axis_index_groups=planes, tiled=...]
    all_to_all x2, waiting for transfers between devices: 29.1 us -> 23.5 us  [the longest x1 16.4 us: gather_first(): lax.all_to_all(jnp.broadcast_to(both[None], (32,) + both.shape), ('spatia...]
    all_to_all x1, blocking collectives: 50.4 us -> 45.1 us  [shards(): lax.all_to_all(result.reshape(MEMBERS, BLOCK, LONS), 'field', split_axis=...]
    all_to_all x2, starting transfers between devices: 27.8 us -> 24.2 us  [the longest x1 16.7 us: gather_first(): lax.all_to_all(jnp.broadcast_to(both[None], (32,) + both.shape), ('spatia...]
  transfers between devices with their start and end apart: 4 -> 3, of which waited for: 4 -> 2; matrix products, arithmetic and copies ran while one was open for 1% -> 1% of each run, Pallas kernels for 12% -> 12%
where the time goes in v7:
time: 251 us; the launch traced here: 250 us
  blocking collectives  144 us (57%)
  Pallas kernels  40 us (16%)
  starting transfers between devices  24.2 us (10%)
  waiting for transfers between devices  23.5 us (9%)
  between operations  13.5 us (5%)
  local copies, waits for them, and re-layouts  3.44 us (1%)
    all_to_all x1, blocking collectives, shards(): lax.all_to_all(mixed.reshape(MEMBERS, BLOCK, LONS), 'field', split_axis=0...  69.5 us
    all_to_all x1, blocking collectives, shards(): lax.all_to_all(result.reshape(MEMBERS, BLOCK, LONS), 'field', split_axis=...  45.1 us
    all_to_all x1, blocking collectives, shards(): lax.all_to_all(synth.reshape(BANDS, 2 * ORDERS, ROWS), 'spatial', split_a...  29.6 us
    all_to_all x1, starting transfers between devices, gather_first(): lax.all_to_all(jnp.broadcast_to(both[None], (32,) + both.shape), ('spatia...  16.7 us
    all_to_all x1, waiting for transfers between devices, gather_first(): lax.all_to_all(jnp.broadcast_to(both[None], (32,) + both.shape), ('spatia...  16.4 us
    pallas_call x1, Pallas kernels, legendre(): pl.pallas_call(legendre_kernel, out_shape=(jax.ShapeDtypeStruct((ORDERS,...  12.5 us
    pallas_call x1, Pallas kernels, mlp(): pl.pallas_call(mlp_kernel, grid=(blocks // take,), out_shape=jax.ShapeDty...  8.05 us
    all_to_all x1, starting transfers between devices, shards(): lax.all_to_all(spectrum.reshape(BANDS, 2 * ORDERS, ROWS), 'spatial', spli...  7.43 us
  transfers between devices with their start and end apart: 3, of which 2 were waited for; matrix products, arithmetic and copies ran while one was open for 1% of the time, Pallas kernels for 12%

profile of v7, /device:TPU:1, one launch (start us, length us, event | category | flops | bytes accessed | tf_op | source)
XLA Modules:
  0.0 250.3 jit_solution(3815540288812665152)
XLA Ops:
  6.5 0.0 copy-start.1
  6.5 0.7 pad_maximum_fusion.1
  7.3 0.7 broadcast_in_dim.2
  8.0 16.7 %all-to-all-start = ((bf16[32,8,512]{2,1,0:T(8,128)(2,1)}), bf16[32,8,512]{2,1,0:T(8,128)(2,1)S(1)}, u32[]{:S(2)}, u32[]{:S(2)}) async-start(bf16[32,8,512]{2,1,0:T(8,128)(2,1)} %broadcast_in_dim.2), calls=%async_computation | async-start | bytes 524288 | tf_op jit(solution)/shard_map/all_to_all | solution.py:380
  24.7 0.0 all-gather.2.cloned.1.call-start
  24.8 5.6 %forward_fourier.1 = (bf16[768,384]{1,0:T(8,128)(2,1)}, bf16[768,1024]{1,0:T(8,128)(2,1)}) custom-call(bf16[384,1024]{1,0:T(8,128)(2,1)} %bitcast.27), custom_call_target="tpu_custom_call" | custom-call | tf_op jit(solution)/shard_map/forward_fourier/pallas_call | solution.py:76
  30.4 16.4 %all-to-all-done = bf16[32,8,512]{2,1,0:T(8,128)(2,1)S(1)} async-done(((bf16[32,8,512]{2,1,0:T(8,128)(2,1)}), bf16[32,8,512]{2,1,0:T(8,128)(2,1)S(1)}, u32[]{:S(2)}, u32[]{:S(2)}) %all-to-all-start) | async-done | bytes 262176 | tf_op jit(solution)/shard_map/all_to_all | solution.py:380
  46.7 0.1 copy.20
  46.9 0.1 copy.23
  47.0 0.1 copy.24
  47.1 0.1 copy.21
  47.2 0.1 reshape_squeeze.6
  47.3 0.7 pad_maximum_fusion
  48.0 0.0 all-gather.2.cloned.1.call-update
  48.1 7.4 %all-to-all-start.1 = ((bf16[32,24,384]{2,1,0:T(8,128)(2,1)}), bf16[32,24,384]{2,1,0:T(8,128)(2,1)S(1)}, u32[]{:S(2)}, u32[]{:S(2)}) async-start(bf16[32,24,384]{2,1,0:T(8,128)(2,1)} %bitcast.38), calls=%async_computation.1 | async-start | bytes 1179648 | tf_op jit(solution)/shard_map/all_to_all | solution.py:407
  55.5 0.0 copy-done.1
  55.5 0.4 reshape.53
  55.9 0.3 copy.18
  56.2 0.7 copy.19.bias_ref
  56.9 12.5 %legendre_table.1 = (bf16[12,384,384]{2,1,0:T(8,128)(2,1)}, f32[16,128]{1,0:T(8,128)}) custom-call(s32[1]{0:T(128)} %bitcast.4.first_ref, f32[16,128]{1,0:T(8,128)} %copy.19.bias_ref), custom_call_target="tpu_custom_call" | custom-call | flops 100000000 | bytes 20000000 | tf_op jit(solution)/shard_map/legendre_table/pallas_call | solution.py:157
  69.4 7.1 %all-to-all-done.1 = bf16[32,24,384]{2,1,0:T(8,128)(2,1)S(1)} async-done(((bf16[32,24,384]{2,1,0:T(8,128)(2,1)}), bf16[32,24,384]{2,1,0:T(8,128)(2,1)S(1)}, u32[]{:S(2)}, u32[]{:S(2)}) %all-to-all-start.1) | async-done | bytes 589856 | tf_op jit(solution)/shard_map/all_to_all | solution.py:407
  76.6 0.0 copy-start
  76.6 0.8 copy-done
  77.4 7.3 %spectral_filter.1 = bf16[768,384]{1,0:T(8,128)(2,1)} custom-call(bf16[768,384]{1,0:T(8,128)(2,1)} %bitcast.33, bf16[12,384,384]{2,1,0:T(8,128)(2,1)} %get-tuple-element.13.p_ref, f32[2,32,384]{2,1,0:T(8,128)} %w_ref.1), custom_call_target="tpu_custom_call" | custom-call | tf_op jit(solution)/shard_map/spectral_filter/pallas_call | solution.py:238
  84.6 29.6 %all_to_all.25 = bf16[32,24,384]{2,1,0:T(8,128)(2,1)} all-to-all(bf16[32,24,384]{2,1,0:T(8,128)(2,1)} %bitcast.34), channel_id=1, replica_groups=mesh['field'=16,'spatial'=32] {'spatial'}, dimensions={0} | all-to-all | bytes 1179648 | tf_op jit(solution)/shard_map/all_to_all | solution.py:413
  114.2 4.5 %inverse_fourier.1 = bf16[1536,256]{1,0:T(8,128)(2,1)} custom-call(bf16[768,384]{1,0:T(8,128)(2,1)} %bitcast.35, bf16[768,1024]{1,0:T(8,128)(2,1)} %get-tuple-element.14.t_ref, bf16[384,1024]{1,0:T(8,128)(2,1)} %bitcast.28), custom_call_target="tpu_custom_call" | custom-call | tf_op jit(solution)/shard_map/inverse_fourier/pallas_call | solution.py:276
  118.7 69.5 %all_to_all.26 = bf16[16,96,256]{2,1,0:T(8,128)(2,1)} all-to-all(bf16[16,96,256]{2,1,0:T(8,128)(2,1)} %bitcast.29), channel_id=1, replica_groups=mesh['field'=16,'spatial'=32] {'field'}, dimensions={0} | all-to-all | bytes 1572864 | tf_op jit(solution)/shard_map/all_to_all | solution.py:417
  188.3 0.0 all-gather.2.cloned.1.call-done
  188.3 8.1 %pointwise_mlp.1 = bf16[1536,256]{1,0:T(8,128)(2,1)} custom-call(bf16[1536,256]{1,0:T(8,128)(2,1)} %bitcast.31, bf16[16,1024,128]{2,1,0:T(8,128)(2,1)} %bitcast.26, f32[16,128]{1,0:T(8,128)} %get-tuple-element.16.bias_ref), custom_call_target="tpu_custom_call" | custom-call | tf_op jit(solution)/shard_map/pointwise_mlp/pallas_call | solution.py:338
  196.3 45.1 %all_to_all.27 = bf16[16,96,256]{2,1,0:T(8,128)(2,1)} all-to-all(bf16[16,96,256]{2,1,0:T(8,128)(2,1)} %bitcast.32), channel_id=1, replica_groups=mesh['field'=16,'spatial'=32] {'field'}, dimensions={0} | all-to-all | bytes 1572864 | tf_op jit(solution)/shard_map/all_to_all | solution.py:421
  241.4 2.1 home_layout.1
  (3 shorter events, 0.1 us)
Async XLA Ops:
  6.5 49.0 %copy-start.1 = (f32[2048]{0:T(1024)S(1)}, f32[2048]{0:T(1024)}, u32[]{:S(2)}) copy-start(f32[2048]{0:T(1024)} %param.8) | copy-start | bytes 24580
  8.0 38.8 %all-to-all-start = ((bf16[32,8,512]{2,1,0:T(8,128)(2,1)}), bf16[32,8,512]{2,1,0:T(8,128)(2,1)S(1)}, u32[]{:S(2)}, u32[]{:S(2)}) async-start(bf16[32,8,512]{2,1,0:T(8,128)(2,1)} %broadcast_in_dim.2), calls=%async_computation | async-start | bytes 524288 | tf_op jit(solution)/shard_map/all_to_all | solution.py:380
  24.7 163.5 %all-gather.2.cloned.1.call-start = ((), (), s32[]{:S(2)}) async-start(), calls=%async_computation.5 | async-start | bytes 4456448 | tf_op jit(solution)/shard_map/all_gather | solution.py:396
  48.1 28.5 %all-to-all-start.1 = ((bf16[32,24,384]{2,1,0:T(8,128)(2,1)}), bf16[32,24,384]{2,1,0:T(8,128)(2,1)S(1)}, u32[]{:S(2)}, u32[]{:S(2)}) async-start(bf16[32,24,384]{2,1,0:T(8,128)(2,1)} %bitcast.38), calls=%async_computation.1 | async-start | bytes 1179648 | tf_op jit(solution)/shard_map/all_to_all | solution.py:407
  76.6 0.8 copy-start
Sparse Core Ops, SparseCore 0:
  48.2 67.9 all-gather.1

commit v8 on v7

--- a/solution.py
+++ b/solution.py
@@ -375,16 +375,31 @@
 
 
 def gather_first(proj_in, proj_out):
-    column = [[xy * 32 + place for place in range(32)] for xy in range(16)]
-    both = jnp.concatenate([proj_in, proj_out], axis=0)
-    return lax.all_to_all(
-        jnp.broadcast_to(both[None], (32,) + both.shape),
-        ("spatial", "field"),
-        split_axis=0,
-        concat_axis=0,
-        axis_index_groups=column,
-        tiled=True,
-    )
+    held = jnp.concatenate([proj_in, proj_out], axis=0)
+    near = [
+        [xy * 32 + (4 * four + at) * 2 + core for at in range(4)]
+        for xy in range(16)
+        for four in range(4)
+        for core in range(2)
+    ]
+    far = [
+        [xy * 32 + (4 * four + at) * 2 + core for four in range(4)]
+        for xy in range(16)
+        for at in range(4)
+        for core in range(2)
+    ]
+    for groups in (near, far):
+        rows = held.shape[0]
+        held = lax.all_to_all(
+            jnp.broadcast_to(held[None], (4,) + held.shape),
+            ("spatial", "field"),
+            split_axis=0,
+            concat_axis=0,
+            axis_index_groups=groups,
+            tiled=True,
+        ).reshape(4 * rows, FULL)
+    cores = [[2 * chip, 2 * chip + 1] for chip in range(8)]
+    return lax.all_gather(held, "field", axis=0, axis_index_groups=cores, tiled=True)
 
 
 def gather_second(column):
@@ -399,7 +414,7 @@
 
 def shards(field_in, spectral_weight, proj_in, bias_in, proj_out):
     column = gather_first(proj_in, proj_out)
-    bias = bias_in.reshape(16, 16, 2, 4).transpose(1, 2, 0, 3).reshape(16, LANES)
+    bias = bias_in.reshape(8, 2, 16, 2, 4).transpose(2, 1, 3, 0, 4).reshape(16, LANES)
     rows = field_in.transpose(1, 0, 2).reshape(ROWS, NLON)
     spectrum, table = forward(rows)
     spectrum, column = lax.optimization_barrier((spectrum, column))

time: 251 us -> 254 us (1.012)
  blocking collectives: 144 us -> 160 us
  waiting for transfers between devices: 23.5 us -> 14.1 us
    all_to_all x0 -> x1, blocking collectives: none -> 10.7 us  [gather_first(): lax.all_to_all(jnp.broadcast_to(held[None], (4,) + held.shape), ('spatial...]
    all_to_all x1, waiting for transfers between devices: 16.4 us -> 6.53 us  [gather_first(): lax.all_to_all(jnp.broadcast_to(held[None], (4,) + held.shape), ('spatial...]
    all_gather x0 -> x1, blocking collectives: none -> 5.1 us  [gather_first(): lax.all_gather(held, 'field', axis=0, axis_index_groups=cores, tiled=True)]
    all_to_all x1, starting transfers between devices: 16.7 us -> 12.1 us  [gather_first(): lax.all_to_all(jnp.broadcast_to(held[None], (4,) + held.shape), ('spatial...]
where the time goes in v8:
time: 254 us
  blocking collectives  160 us (63%)
  Pallas kernels  40 us (16%)
  starting transfers between devices  21.7 us (9%)
  waiting for transfers between devices  14.1 us (6%)
  between operations  13.5 us (5%)
  local copies, waits for them, and re-layouts  3.22 us (1%)
    all_to_all x1, blocking collectives, shards(): lax.all_to_all(mixed.reshape(MEMBERS, BLOCK, LONS), 'field', split_axis=0...  69.3 us
    all_to_all x1, blocking collectives, shards(): lax.all_to_all(result.reshape(MEMBERS, BLOCK, LONS), 'field', split_axis=...  45.1 us
    all_to_all x1, blocking collectives, shards(): lax.all_to_all(synth.reshape(BANDS, 2 * ORDERS, ROWS), 'spatial', split_a...  29.4 us
    pallas_call x1, Pallas kernels, legendre(): pl.pallas_call(legendre_kernel, out_shape=(jax.ShapeDtypeStruct((ORDERS,...  12.5 us
    all_to_all x1, starting transfers between devices, gather_first(): lax.all_to_all(jnp.broadcast_to(held[None], (4,) + held.shape), ('spatial...  12.1 us
    all_to_all x1, blocking collectives, gather_first(): lax.all_to_all(jnp.broadcast_to(held[None], (4,) + held.shape), ('spatial...  10.7 us
    all_to_all x1, starting transfers between devices, shards(): lax.all_to_all(spectrum.reshape(BANDS, 2 * ORDERS, ROWS), 'spatial', spli...  9.61 us
    pallas_call x1, Pallas kernels, mlp(): pl.pallas_call(mlp_kernel, grid=(blocks // take,), out_shape=jax.ShapeDty...  8.05 us
  transfers between devices with their start and end apart: 3, of which 2 were waited for; matrix products, arithmetic and copies ran while one was open for 1% of the time, Pallas kernels for 12%

profile of v8, /device:TPU:1, one launch (start us, length us, event | category | flops | bytes accessed | tf_op | source)
XLA Modules:
  0.0 253.6 jit_solution(14850445946799620227)
XLA Ops:
  6.5 0.0 copy-start.1
  6.5 0.7 pad_maximum_fusion.1
  7.3 10.7 %all_to_all.30 = bf16[4,8,512]{2,1,0:T(8,128)(2,1)S(1)} all-to-all(bf16[4,8,512]{2,1,0:T(8,128)(2,1)S(1)} %broadcast_in_dim.6), channel_id=1, replica_groups={{0,64,128,192},{32,96,160,224},{256,320,384,448},{288,352,416,480},{1,6..., dimensions={0} | all-to-all | bytes 65536 | tf_op jit(solution)/shard_map/all_to_all | solution.py:393
  18.0 0.6 broadcast_in_dim.15
  18.7 12.1 %all-to-all-start.1 = ((bf16[4,32,512]{2,1,0:T(8,128)(2,1)}), bf16[4,32,512]{2,1,0:T(8,128)(2,1)S(1)}, u32[]{:S(2)}, u32[]{:S(2)}) async-start(bf16[4,32,512]{2,1,0:T(8,128)(2,1)} %broadcast_in_dim.15), calls=%async_computation.1 | async-start | bytes 262144 | tf_op jit(solution)/shard_map/all_to_all | solution.py:393
  30.8 0.0 all-gather.2.cloned.1.call-start
  30.8 5.6 %forward_fourier.1 = (bf16[768,384]{1,0:T(8,128)(2,1)}, bf16[768,1024]{1,0:T(8,128)(2,1)}) custom-call(bf16[384,1024]{1,0:T(8,128)(2,1)} %bitcast.24), custom_call_target="tpu_custom_call" | custom-call | tf_op jit(solution)/shard_map/forward_fourier/pallas_call | solution.py:76
  36.3 6.5 %all-to-all-done.1 = bf16[4,32,512]{2,1,0:T(8,128)(2,1)S(1)} async-done(((bf16[4,32,512]{2,1,0:T(8,128)(2,1)}), bf16[4,32,512]{2,1,0:T(8,128)(2,1)S(1)}, u32[]{:S(2)}, u32[]{:S(2)}) %all-to-all-start.1) | async-done | bytes 131104 | tf_op jit(solution)/shard_map/all_to_all | solution.py:393
  42.9 5.1 %all_gather.6 = bf16[256,512]{1,0:T(8,128)(2,1)S(1)} all-gather(bf16[128,512]{1,0:T(8,128)(2,1)S(1)} %bitcast.35), channel_id=1, replica_groups={{0,32},{64,96},{128,160},{192,224},{256,288},{320,352},{384,416},{448,4..., dimensions={0}, use_global_device_ids=true | all-gather | bytes 393216 | tf_op jit(solution)/shard_map/all_gather | solution.py:402
  48.0 0.1 reshape.64
  48.0 0.1 fusion
  48.2 0.1 copy.13
  48.3 0.1 reshape_squeeze.6
  48.4 0.7 pad_maximum_fusion
  49.1 0.0 all-gather.2.cloned.1.call-update
  49.1 9.6 %all-to-all-start.2 = ((bf16[32,24,384]{2,1,0:T(8,128)(2,1)}), bf16[32,24,384]{2,1,0:T(8,128)(2,1)S(1)}, u32[]{:S(2)}, u32[]{:S(2)}) async-start(bf16[32,24,384]{2,1,0:T(8,128)(2,1)} %bitcast.34), calls=%async_computation.2 | async-start | bytes 1179648 | tf_op jit(solution)/shard_map/all_to_all | solution.py:422
  58.8 0.0 copy-done.1
  58.8 0.4 reshape.58
  59.2 0.3 copy.10
  59.5 0.7 copy.11.bias_ref
  60.1 12.5 %legendre_table.1 = (bf16[12,384,384]{2,1,0:T(8,128)(2,1)}, f32[16,128]{1,0:T(8,128)}) custom-call(s32[1]{0:T(128)} %bitcast.6.first_ref, f32[16,128]{1,0:T(8,128)} %copy.11.bias_ref), custom_call_target="tpu_custom_call" | custom-call | flops 100000000 | bytes 20000000 | tf_op jit(solution)/shard_map/legendre_table/pallas_call | solution.py:157
  72.7 7.6 %all-to-all-done.2 = bf16[32,24,384]{2,1,0:T(8,128)(2,1)S(1)} async-done(((bf16[32,24,384]{2,1,0:T(8,128)(2,1)}), bf16[32,24,384]{2,1,0:T(8,128)(2,1)S(1)}, u32[]{:S(2)}, u32[]{:S(2)}) %all-to-all-start.2) | async-done | bytes 589856 | tf_op jit(solution)/shard_map/all_to_all | solution.py:422
  80.2 0.0 copy-start
  80.2 0.8 copy-done
  81.1 7.3 %spectral_filter.1 = bf16[768,384]{1,0:T(8,128)(2,1)} custom-call(bf16[768,384]{1,0:T(8,128)(2,1)} %bitcast.30, bf16[12,384,384]{2,1,0:T(8,128)(2,1)} %get-tuple-element.13.p_ref, f32[2,32,384]{2,1,0:T(8,128)} %w_ref.1), custom_call_target="tpu_custom_call" | custom-call | tf_op jit(solution)/shard_map/spectral_filter/pallas_call | solution.py:238
  88.3 29.4 %all_to_all.31 = bf16[32,24,384]{2,1,0:T(8,128)(2,1)} all-to-all(bf16[32,24,384]{2,1,0:T(8,128)(2,1)} %bitcast.31), channel_id=1, replica_groups=mesh['field'=16,'spatial'=32] {'spatial'}, dimensions={0} | all-to-all | bytes 1179648 | tf_op jit(solution)/shard_map/all_to_all | solution.py:428
  117.7 4.5 %inverse_fourier.1 = bf16[1536,256]{1,0:T(8,128)(2,1)} custom-call(bf16[768,384]{1,0:T(8,128)(2,1)} %bitcast.32, bf16[768,1024]{1,0:T(8,128)(2,1)} %get-tuple-element.14.t_ref, bf16[384,1024]{1,0:T(8,128)(2,1)} %bitcast.25), custom_call_target="tpu_custom_call" | custom-call | tf_op jit(solution)/shard_map/inverse_fourier/pallas_call | solution.py:276
  122.2 69.3 %all_to_all.32 = bf16[16,96,256]{2,1,0:T(8,128)(2,1)} all-to-all(bf16[16,96,256]{2,1,0:T(8,128)(2,1)} %bitcast.26), channel_id=1, replica_groups=mesh['field'=16,'spatial'=32] {'field'}, dimensions={0} | all-to-all | bytes 1572864 | tf_op jit(solution)/shard_map/all_to_all | solution.py:432
  191.5 0.0 all-gather.2.cloned.1.call-done
  191.5 8.1 %pointwise_mlp.1 = bf16[1536,256]{1,0:T(8,128)(2,1)} custom-call(bf16[1536,256]{1,0:T(8,128)(2,1)} %bitcast.28, bf16[16,1024,128]{2,1,0:T(8,128)(2,1)} %bitcast.23, f32[16,128]{1,0:T(8,128)} %get-tuple-element.16.bias_ref), custom_call_target="tpu_custom_call" | custom-call | tf_op jit(solution)/shard_map/pointwise_mlp/pallas_call | solution.py:338
  199.6 45.1 %all_to_all.33 = bf16[16,96,256]{2,1,0:T(8,128)(2,1)} all-to-all(bf16[16,96,256]{2,1,0:T(8,128)(2,1)} %bitcast.29), channel_id=1, replica_groups=mesh['field'=16,'spatial'=32] {'field'}, dimensions={0} | all-to-all | bytes 1572864 | tf_op jit(solution)/shard_map/all_to_all | solution.py:436
  244.6 2.1 home_layout.1
  (3 shorter events, 0.1 us)
Async XLA Ops:
  6.5 52.2 %copy-start.1 = (f32[2048]{0:T(1024)S(1)}, f32[2048]{0:T(1024)}, u32[]{:S(2)}) copy-start(f32[2048]{0:T(1024)} %param.8) | copy-start | bytes 24580
  18.7 24.2 %all-to-all-start.1 = ((bf16[4,32,512]{2,1,0:T(8,128)(2,1)}), bf16[4,32,512]{2,1,0:T(8,128)(2,1)S(1)}, u32[]{:S(2)}, u32[]{:S(2)}) async-start(bf16[4,32,512]{2,1,0:T(8,128)(2,1)} %broadcast_in_dim.15), calls=%async_computation.1 | async-start | bytes 262144 | tf_op jit(solution)/shard_map/all_to_all | solution.py:393
  30.8 160.7 %all-gather.2.cloned.1.call-start = ((), (), s32[]{:S(2)}) async-start(), calls=%async_computation.6 | async-start | bytes 4456448 | tf_op jit(solution)/shard_map/all_gather | solution.py:411
  49.1 31.1 %all-to-all-start.2 = ((bf16[32,24,384]{2,1,0:T(8,128)(2,1)}), bf16[32,24,384]{2,1,0:T(8,128)(2,1)S(1)}, u32[]{:S(2)}, u32[]{:S(2)}) async-start(bf16[32,24,384]{2,1,0:T(8,128)(2,1)} %bitcast.34), calls=%async_computation.2 | async-start | bytes 1179648 | tf_op jit(solution)/shard_map/all_to_all | solution.py:422
  80.2 0.8 copy-start
Sparse Core Ops, SparseCore 0:
  49.2 70.1 all-gather.1

commit v9 on v6

--- a/solution.py
+++ b/solution.py
@@ -400,20 +400,17 @@
     rows = field_in.transpose(1, 0, 2).reshape(ROWS, NLON)
     spectrum, table = forward(rows)
     first = (lax.axis_index("spatial") * ORDERS).astype(jnp.int32).reshape(1)
+    polar, bias = legendre(first, bias)
 
     def swap(blocks):
         return lax.all_to_all(blocks, "spatial", split_axis=0, concat_axis=0, tiled=True)
 
-    def filtered(step, carry):
-        held, laid = carry
-        polar, laid = legendre(first, laid)
+    def filtered(step, held):
         synth = spectral_filter(swap(held).reshape(PARTS, ROWS), polar, spectral_weight)
-        return swap(synth.reshape(BANDS, 2 * ORDERS, ROWS)), laid
+        return swap(synth.reshape(BANDS, 2 * ORDERS, ROWS))
 
     steps = 1 + (lax.axis_index("field") >> 8)
-    returned, bias = lax.fori_loop(
-        0, steps, filtered, (spectrum.reshape(BANDS, 2 * ORDERS, ROWS), bias)
-    )
+    returned = lax.fori_loop(0, steps, filtered, spectrum.reshape(BANDS, 2 * ORDERS, ROWS))
     returned, column = lax.optimization_barrier((returned, column))
     weights = gather_second(column)
     mixed = inverse(returned.reshape(PARTS, ROWS), table, rows)

time: 250 us -> 258 us (1.032)
  blocking collectives: 102 us -> 165 us
  waiting for transfers between devices: 59.8 us -> 29.6 us
  starting transfers between devices: 27.9 us -> 4.65 us
    all_to_all x0 -> x1, blocking collectives: none -> 43.6 us  [swap(): lax.all_to_all(blocks, 'spatial', split_axis=0, concat_axis=0, tiled=True)]
    all_to_all x2 -> x1, starting transfers between devices: 27.8 us -> 4.61 us  [swap(): lax.all_to_all(blocks, 'spatial', split_axis=0, concat_axis=0, tiled=True)]
    all_gather x1, waiting for transfers between devices: 23 us -> 2.88 us  [gather_first(): lax.all_gather(both, ('spatial', 'field'), axis=0, axis_index_groups=colu...]
    all_to_all x1, blocking collectives: 51.5 us -> 71.4 us  [shards(): lax.all_to_all(mixed.reshape(MEMBERS, BLOCK, LONS), 'field', split_axis=0...]
    all_to_all x2 -> x1, waiting for transfers between devices: 29.1 us -> 19.1 us  [swap(): lax.all_to_all(blocks, 'spatial', split_axis=0, concat_axis=0, tiled=True)]
  transfers between devices with their start and end apart: 4 -> 3, of which waited for: 4 -> 3; matrix products, arithmetic and copies ran while one was open for 1% -> 1% of each run, Pallas kernels for 12% -> 11%
where the time goes in v9:
time: 258 us; the launch traced here: 257 us
  blocking collectives  165 us (64%)
  Pallas kernels  38.3 us (15%)
  waiting for transfers between devices  29.6 us (11%)
  between operations  13.5 us (5%)
  starting transfers between devices  4.65 us (2%)
  local copies, waits for them, and re-layouts  3.72 us (1%)
    all_to_all x1, blocking collectives, shards(): lax.all_to_all(mixed.reshape(MEMBERS, BLOCK, LONS), 'field', split_axis=0...  71.4 us
    all_to_all x1, blocking collectives, shards(): lax.all_to_all(result.reshape(MEMBERS, BLOCK, LONS), 'field', split_axis=...  50.4 us
    all_to_all x1, blocking collectives, swap(): lax.all_to_all(blocks, 'spatial', split_axis=0, concat_axis=0, tiled=True)  43.6 us
    all_to_all x1, waiting for transfers between devices, swap(): lax.all_to_all(blocks, 'spatial', split_axis=0, concat_axis=0, tiled=True)  19.1 us
    pallas_call x1, Pallas kernels, legendre(): pl.pallas_call(legendre_kernel, out_shape=(jax.ShapeDtypeStruct((ORDERS,...  11.3 us
    pallas_call x1, Pallas kernels, mlp(): pl.pallas_call(mlp_kernel, grid=(blocks // take,), out_shape=jax.ShapeDty...  8.05 us
    all_gather x1, waiting for transfers between devices, gather_second(): lax.all_gather(block, 'spatial', axis=0, axis_index_groups=planes, tiled=...  7.54 us
    pallas_call x1, Pallas kernels, spectral_filter(): pl.pallas_call(filter_kernel, grid=(ORDERS // 2 // PAIRS,), out_shape=jax...  6.73 us
  transfers between devices with their start and end apart: 3, of which 3 were waited for; matrix products, arithmetic and copies ran while one was open for 1% of the time, Pallas kernels for 11%

profile of v9, /device:TPU:1, one launch (start us, length us, event | category | flops | bytes accessed | tf_op | source)
XLA Modules:
  0.0 257.2 jit_solution(13121127560451046624)
XLA Ops:
  6.5 0.0 all-gather.3.cloned.1.call-start
  6.5 1.3 fusion.2
  7.8 0.0 all-gather.3.cloned.1.call-update
  7.9 0.0 all-gather.5.cloned.1.call-start
  7.9 5.6 %forward_fourier.1 = (bf16[768,384]{1,0:T(8,128)(2,1)}, bf16[768,1024]{1,0:T(8,128)(2,1)}) custom-call(bf16[384,1024]{1,0:T(8,128)(2,1)} %bitcast.36), custom_call_target="tpu_custom_call" | custom-call | tf_op jit(solution)/shard_map/forward_fourier/pallas_call | solution.py:76
  13.5 1.1 reshape.51
  14.6 0.3 copy.17
  14.9 0.7 copy.18.bias_ref
  15.6 11.3 %legendre_table.1 = (bf16[12,384,384]{2,1,0:T(8,128)(2,1)S(1)}, f32[16,128]{1,0:T(8,128)}) custom-call(s32[1]{0:T(128)} %bitcast.5.first_ref, f32[16,128]{1,0:T(8,128)} %copy.18.bias_ref), custom_call_target="tpu_custom_call" | custom-call | flops 100000000 | bytes 20000000 | tf_op jit(solution)/shard_map/legendre_table/pallas_call | solution.py:157
  26.9 74.1 %while.10 = (s32[]{:T(128)}, bf16[32,24,384]{2,1,0:T(8,128)(2,1)}, s32[]{:T(128)}, bf16[12,384,384]{2,1,0:T(8,128)(2,1)S(1)}, f32[2,32,384]{2,1,0:T(8,128)}, /*index=5*/s32[]{:T(128)}) while((s32[]{:T(128)}, bf16[32,24,384]{2,1,0:T(8,128)(2,1)}, s32[]{:T(128)}, bf16[12,384,384]{2,1,0:T(8,128)(2,1)S(1)}, f32[2,32,384]{2,1,0:T(8,128)}, ...), condition=%wide.region_1.2_spmd, body=%wide.region_0.1_spmd.sunk | while | flops 2 | bytes 2949221 | solution.py:413
  26.9 43.6 %all_to_all.24 = bf16[32,24,384]{2,1,0:T(8,128)(2,1)} all-to-all(bf16[32,24,384]{2,1,0:T(8,128)(2,1)} %get-tuple-element.97), channel_id=1, replica_groups=mesh['field'=16,'spatial'=32] {'spatial'}, dimensions={0} | all-to-all | bytes 1179648 | tf_op jit(solution)/shard_map/while/body/all_to_all | solution.py:406
  70.6 6.7 %spectral_filter.1 = bf16[768,384]{1,0:T(8,128)(2,1)} custom-call(bf16[768,384]{1,0:T(8,128)(2,1)} %bitcast.34, bf16[12,384,384]{2,1,0:T(8,128)(2,1)S(1)} %get-tuple-element.105.p_ref, f32[2,32,384]{2,1,0:T(8,128)} %get-tuple-element.106.w_ref), custom_call_target="tpu_custom_call" | custom-call | tf_op jit(solution)/shard_map/while/body/spectral_filter/pallas_call | solution.py:238
  77.3 4.6 %all-to-all-start.1 = ((bf16[32,24,384]{2,1,0:T(8,128)(2,1)}), bf16[32,24,384]{2,1,0:T(8,128)(2,1)}, u32[]{:S(2)}, u32[]{:S(2)}) async-start(bf16[32,24,384]{2,1,0:T(8,128)(2,1)} %bitcast.33), calls=%async_computation.1 | async-start | bytes 1179648 | tf_op jit(solution)/shard_map/while/body/all_to_all | solution.py:406
  81.9 19.1 %all-to-all-done.1 = bf16[32,24,384]{2,1,0:T(8,128)(2,1)} async-done(((bf16[32,24,384]{2,1,0:T(8,128)(2,1)}), bf16[32,24,384]{2,1,0:T(8,128)(2,1)}, u32[]{:S(2)}, u32[]{:S(2)}) %all-to-all-start.1) | async-done | bytes 589856 | tf_op jit(solution)/shard_map/while/body/all_to_all | solution.py:406
  101.0 2.9 %all-gather.3.cloned.1.call-done = bf16[1024,512]{1,0:T(8,128)(2,1)} async-done(((bf16[32,512]{1,0:T(8,128)(2,1)}), bf16[1024,512]{1,0:T(8,128)(2,1)}) %all-gather.3.cloned.1.call-update) | async-done | bytes 1048592 | tf_op jit(solution)/shard_map/all_gather | solution.py:384
  103.9 1.3 reshape.56
  105.3 0.1 slice_bitcast_fusion.1
  105.4 0.1 copy.22
  105.5 0.1 reshape_squeeze.6
  105.6 0.7 pad_maximum_fusion
  106.3 0.0 all-gather.5.cloned.1.call-update
  106.4 4.5 %inverse_fourier.1 = bf16[1536,256]{1,0:T(8,128)(2,1)} custom-call(bf16[768,384]{1,0:T(8,128)(2,1)} %bitcast.8.r_ref, bf16[768,1024]{1,0:T(8,128)(2,1)} %get-tuple-element.43.t_ref, bf16[384,1024]{1,0:T(8,128)(2,1)} %bitcast.37), custom_call_target="tpu_custom_call" | custom-call | tf_op jit(solution)/shard_map/inverse_fourier/pallas_call | solution.py:276
  110.9 71.4 %all_to_all.22 = bf16[16,96,256]{2,1,0:T(8,128)(2,1)} all-to-all(bf16[16,96,256]{2,1,0:T(8,128)(2,1)} %bitcast.38), channel_id=1, replica_groups=mesh['field'=16,'spatial'=32] {'field'}, dimensions={0} | all-to-all | bytes 1572864 | tf_op jit(solution)/shard_map/all_to_all | solution.py:417
  182.3 7.5 %all-gather.5.cloned.1.call-done = bf16[16384,128]{1,0:T(8,128)(2,1)} async-done(((bf16[1024,128]{1,0:T(8,128)(2,1)}), bf16[16384,128]{1,0:T(8,128)(2,1)}) %all-gather.5.cloned.1.call-update) | async-done | bytes 4194320 | tf_op jit(solution)/shard_map/all_gather | solution.py:393
  189.8 8.1 %pointwise_mlp.1 = bf16[1536,256]{1,0:T(8,128)(2,1)} custom-call(bf16[1536,256]{1,0:T(8,128)(2,1)} %bitcast.40, bf16[16,1024,128]{2,1,0:T(8,128)(2,1)} %bitcast.35, f32[16,128]{1,0:T(8,128)} %get-tuple-element.45.bias_ref), custom_call_target="tpu_custom_call" | custom-call | tf_op jit(solution)/shard_map/pointwise_mlp/pallas_call | solution.py:338
  197.9 50.4 %all_to_all.23 = bf16[16,96,256]{2,1,0:T(8,128)(2,1)} all-to-all(bf16[16,96,256]{2,1,0:T(8,128)(2,1)} %bitcast.41), channel_id=1, replica_groups=mesh['field'=16,'spatial'=32] {'field'}, dimensions={0} | all-to-all | bytes 1572864 | tf_op jit(solution)/shard_map/all_to_all | solution.py:421
  248.3 2.1 home_layout.1
  (2 shorter events, 0.1 us)
Async XLA Ops:
  6.5 97.4 %all-gather.3.cloned.1.call-start = ((), (), s32[]{:S(2)}) async-start(), calls=%async_computation.4 | async-start | bytes 1081344 | tf_op jit(solution)/shard_map/all_gather | solution.py:384
  7.9 182.0 %all-gather.5.cloned.1.call-start = ((), (), s32[]{:S(2)}) async-start(), calls=%async_computation.5 | async-start | bytes 4456448 | tf_op jit(solution)/shard_map/all_gather | solution.py:393
  77.3 23.8 %all-to-all-start.1 = ((bf16[32,24,384]{2,1,0:T(8,128)(2,1)}), bf16[32,24,384]{2,1,0:T(8,128)(2,1)}, u32[]{:S(2)}, u32[]{:S(2)}) async-start(bf16[32,24,384]{2,1,0:T(8,128)(2,1)} %bitcast.33), calls=%async_computation.1 | async-start | bytes 1179648 | tf_op jit(solution)/shard_map/while/body/all_to_all | solution.py:406
Sparse Core Ops, SparseCore 0:
  9.5 94.3 all-gather.2
  106.9 82.8 all-gather.4

commit v10 on v6

--- a/solution.py
+++ b/solution.py
@@ -374,6 +374,10 @@
     )(received)
 
 
+RINGS = (
+    [x * 4 + (y if x % 2 == 0 else 3 - y) for x in range(4) for y in range(4)],
+    [(x if y % 2 == 0 else 3 - x) * 4 + y for y in range(4) for x in range(4)],
+)
 SENT = 32
 
 
@@ -389,14 +393,23 @@
     w_in = split[:, 0].reshape(LANES, 4, LANES).transpose(1, 0, 2).reshape(FULL, LANES)
     w_out = split[:, 1].reshape(LANES, FULL).T
     block = jnp.concatenate([w_in, w_out], axis=0)
-    planes = [[xy * 2 + high for xy in range(16)] for high in range(2)]
-    whole_weights = lax.all_gather(block, "spatial", axis=0, axis_index_groups=planes, tiled=True)
+    planes = [
+        [(xy * 2 + high) * 16 + low * 2 + core for xy in RINGS[core]]
+        for high in range(2)
+        for low in range(8)
+        for core in range(2)
+    ]
+    whole_weights = lax.all_gather(
+        block, ("spatial", "field"), axis=0, axis_index_groups=planes, tiled=True
+    )
     return whole_weights.reshape(16, 2 * FULL, LANES)
 
 
 def shards(field_in, spectral_weight, proj_in, bias_in, proj_out):
     column = gather_first(proj_in, proj_out)
     bias = bias_in.reshape(16, 16, 2, 4).transpose(1, 2, 0, 3).reshape(16, LANES)
+    turns = [jnp.concatenate([bias[xy : xy + 1] for xy in ring]) for ring in RINGS]
+    bias = jnp.where((lax.axis_index("field") & 1) == 0, turns[0], turns[1])
     rows = field_in.transpose(1, 0, 2).reshape(ROWS, NLON)
     spectrum, table = forward(rows)
     first = (lax.axis_index("spatial") * ORDERS).astype(jnp.int32).reshape(1)

time: 250 us -> 256 us (1.024)
  blocking collectives: 102 us -> 110 us
  waiting for transfers between devices: 59.8 us -> 54.8 us
    all_to_all x1, blocking collectives: 50.4 us -> 58.8 us  [shards(): lax.all_to_all(result.reshape(MEMBERS, BLOCK, LONS), 'field', split_axis=...]
    all_gather x1, waiting for transfers between devices: 23 us -> 20.3 us  [gather_first(): lax.all_gather(both, ('spatial', 'field'), axis=0, axis_index_groups=colu...]
where the time goes in v10:
time: 256 us; the launch traced here: 255 us
  blocking collectives  110 us (43%)
  waiting for transfers between devices  54.8 us (21%)
  Pallas kernels  40 us (16%)
  starting transfers between devices  28.5 us (11%)
  between operations  13.6 us (5%)
  local copies, waits for them, and re-layouts  6.09 us (2%)
    all_to_all x1, blocking collectives, shards(): lax.all_to_all(result.reshape(MEMBERS, BLOCK, LONS), 'field', split_axis=...  58.8 us
    all_to_all x1, blocking collectives, shards(): lax.all_to_all(mixed.reshape(MEMBERS, BLOCK, LONS), 'field', split_axis=0...  51.5 us
    all_to_all x2, waiting for transfers between devices, swap(): lax.all_to_all(blocks, 'spatial', split_axis=0, concat_axis=0, tiled=True)  28.9 us
    all_to_all x2, starting transfers between devices, swap(): lax.all_to_all(blocks, 'spatial', split_axis=0, concat_axis=0, tiled=True)  28.4 us
    all_gather x1, waiting for transfers between devices, gather_first(): lax.all_gather(both, ('spatial', 'field'), axis=0, axis_index_groups=colu...  20.3 us
    pallas_call x1, Pallas kernels, legendre(): pl.pallas_call(legendre_kernel, out_shape=(jax.ShapeDtypeStruct((ORDERS,...  12.5 us
    pallas_call x1, Pallas kernels, mlp(): pl.pallas_call(mlp_kernel, grid=(blocks // take,), out_shape=jax.ShapeDty...  8.04 us
    pallas_call x1, Pallas kernels, spectral_filter(): pl.pallas_call(filter_kernel, grid=(ORDERS // 2 // PAIRS,), out_shape=jax...  7.27 us
  transfers between devices with their start and end apart: 4, of which 4 were waited for; matrix products, arithmetic and copies ran while one was open for 1% of the time, Pallas kernels for 12%

profile of v10, /device:TPU:1, one launch (start us, length us, event | category | flops | bytes accessed | tf_op | source)
XLA Modules:
  0.0 255.3 jit_solution(10248238277607008546)
XLA Ops:
  6.5 0.0 all-gather.3.cloned.1.call-start
  6.5 1.3 fusion.2
  7.8 0.0 all-gather.3.cloned.1.call-update
  7.9 0.0 all-gather.5.cloned.1.call-start
  7.9 1.1 reshape.64
  9.0 0.1 fusion.3
  9.2 0.1 slice.119
  9.3 0.1 slice.121
  9.4 0.1 slice.123
  9.5 0.1 slice.125
  9.6 0.1 slice.127
  9.8 0.1 slice.129
  9.9 0.1 slice.131
  10.0 0.1 slice.133
  10.1 0.1 slice.135
  10.2 0.1 slice.137
  10.3 0.1 slice.139
  10.4 0.1 slice.141
  10.6 0.1 slice.143
  10.7 0.1 slice.145
  10.8 0.1 slice.147
  10.9 0.1 slice.149
  11.0 0.1 concatenate.12
  11.1 0.1 concatenate.13
  11.1 5.6 %forward_fourier.1 = (bf16[768,384]{1,0:T(8,128)(2,1)}, bf16[768,1024]{1,0:T(8,128)(2,1)}) custom-call(bf16[384,1024]{1,0:T(8,128)(2,1)} %bitcast.67), custom_call_target="tpu_custom_call" | custom-call | tf_op jit(solution)/shard_map/forward_fourier/pallas_call | solution.py:76
  16.7 78.5 %while.12 = (s32[]{:T(128)}, bf16[32,24,384]{2,1,0:T(8,128)(2,1)}, f32[16,128]{1,0:T(8,128)S(1)}, s32[]{:T(128)}, s32[1]{0:T(128)}, /*index=5*/f32[2,32,384]{2,1,0:T(8,128)}, s32[]{:T(128)}) while((s32[]{:T(128)}, bf16[32,24,384]{2,1,0:T(8,128)(2,1)}, f32[16,128]{1,0:T(8,128)S(1)}, s32[]{:T(128)}, s32[1]{0:T(128)}, ...), condition=%wide.region_1.2_spmd, body=%wide.region_0.1_spmd.sunk | while | flops 100000000 | bytes 25914792 | solution.py:427
  16.7 21.1 %all-to-all-start = ((bf16[32,24,384]{2,1,0:T(8,128)(2,1)}), bf16[32,24,384]{2,1,0:T(8,128)(2,1)S(1)}, u32[]{:S(2)}, u32[]{:S(2)}) async-start(bf16[32,24,384]{2,1,0:T(8,128)(2,1)} %get-tuple-element.131), calls=%async_computation | async-start | bytes 1179648 | tf_op jit(solution)/shard_map/while/body/all_to_all | solution.py:418
  37.8 0.6 copy.79.bias_ref
  38.4 12.5 %legendre_table.1 = (bf16[12,384,384]{2,1,0:T(8,128)(2,1)}, f32[16,128]{1,0:T(8,128)S(1)}) custom-call(s32[1]{0:T(128)} %get-tuple-element.141.first_ref, f32[16,128]{1,0:T(8,128)} %copy.79.bias_ref), custom_call_target="tpu_custom_call" | custom-call | flops 100000000 | bytes 20000000 | tf_op jit(solution)/shard_map/while/body/legendre_table/pallas_call | solution.py:157
  50.9 9.2 %all-to-all-done = bf16[32,24,384]{2,1,0:T(8,128)(2,1)S(1)} async-done(((bf16[32,24,384]{2,1,0:T(8,128)(2,1)}), bf16[32,24,384]{2,1,0:T(8,128)(2,1)S(1)}, u32[]{:S(2)}, u32[]{:S(2)}) %all-to-all-start) | async-done | bytes 589856 | tf_op jit(solution)/shard_map/while/body/all_to_all | solution.py:418
  60.2 0.0 copy-start
  60.2 0.8 copy-done
  61.0 7.3 %spectral_filter.1 = bf16[768,384]{1,0:T(8,128)(2,1)} custom-call(bf16[768,384]{1,0:T(8,128)(2,1)} %bitcast.64, bf16[12,384,384]{2,1,0:T(8,128)(2,1)} %get-tuple-element.121.p_ref, f32[2,32,384]{2,1,0:T(8,128)} %get-tuple-element.142.w_ref), custom_call_target="tpu_custom_call" | custom-call | tf_op jit(solution)/shard_map/while/body/spectral_filter/pallas_call | solution.py:238
  68.3 7.3 %all-to-all-start.1 = ((bf16[32,24,384]{2,1,0:T(8,128)(2,1)}), bf16[32,24,384]{2,1,0:T(8,128)(2,1)}, u32[]{:S(2)}, u32[]{:S(2)}) async-start(bf16[32,24,384]{2,1,0:T(8,128)(2,1)} %bitcast.65), calls=%async_computation.1 | async-start | bytes 1179648 | tf_op jit(solution)/shard_map/while/body/all_to_all | solution.py:418
  75.6 19.6 %all-to-all-done.1 = bf16[32,24,384]{2,1,0:T(8,128)(2,1)} async-done(((bf16[32,24,384]{2,1,0:T(8,128)(2,1)}), bf16[32,24,384]{2,1,0:T(8,128)(2,1)}, u32[]{:S(2)}, u32[]{:S(2)}) %all-to-all-start.1) | async-done | bytes 589856 | tf_op jit(solution)/shard_map/while/body/all_to_all | solution.py:418
  95.2 20.3 %all-gather.3.cloned.1.call-done = bf16[1024,512]{1,0:T(8,128)(2,1)} async-done(((bf16[32,512]{1,0:T(8,128)(2,1)}), bf16[1024,512]{1,0:T(8,128)(2,1)}) %all-gather.3.cloned.1.call-update) | async-done | bytes 1048592 | tf_op jit(solution)/shard_map/all_gather | solution.py:388
  115.5 1.3 reshape.69
  116.8 0.1 slice_bitcast_fusion.1
  117.0 0.1 copy.64
  117.1 0.1 reshape_squeeze.6
  117.2 0.7 pad_maximum_fusion
  117.9 0.0 all-gather.5.cloned.1.call-update
  118.0 4.5 %inverse_fourier.1 = bf16[1536,256]{1,0:T(8,128)(2,1)} custom-call(bf16[768,384]{1,0:T(8,128)(2,1)} %bitcast.7.r_ref, bf16[768,1024]{1,0:T(8,128)(2,1)} %get-tuple-element.48.t_ref, bf16[384,1024]{1,0:T(8,128)(2,1)} %bitcast.68), custom_call_target="tpu_custom_call" | custom-call | tf_op jit(solution)/shard_map/inverse_fourier/pallas_call | solution.py:276
  122.5 51.5 %all_to_all.22 = bf16[16,96,256]{2,1,0:T(8,128)(2,1)} all-to-all(bf16[16,96,256]{2,1,0:T(8,128)(2,1)} %bitcast.69), channel_id=1, replica_groups=mesh['field'=16,'spatial'=32] {'field'}, dimensions={0} | all-to-all | bytes 1572864 | tf_op jit(solution)/shard_map/all_to_all | solution.py:433
  173.9 5.6 %all-gather.5.cloned.1.call-done = bf16[16384,128]{1,0:T(8,128)(2,1)} async-done(((bf16[1024,128]{1,0:T(8,128)(2,1)}), bf16[16384,128]{1,0:T(8,128)(2,1)}) %all-gather.5.cloned.1.call-update) | async-done | bytes 4194320 | tf_op jit(solution)/shard_map/all_gather | solution.py:402
  179.6 8.0 %pointwise_mlp.1 = bf16[1536,256]{1,0:T(8,128)(2,1)} custom-call(bf16[1536,256]{1,0:T(8,128)(2,1)} %bitcast.71, bf16[16,1024,128]{2,1,0:T(8,128)(2,1)} %bitcast.66, f32[16,128]{1,0:T(8,128)S(1)} %get-tuple-element.50.bias_ref), custom_call_target="tpu_custom_call" | custom-call | tf_op jit(solution)/shard_map/pointwise_mlp/pallas_call | solution.py:338
  187.6 58.8 %all_to_all.23 = bf16[16,96,256]{2,1,0:T(8,128)(2,1)} all-to-all(bf16[16,96,256]{2,1,0:T(8,128)(2,1)} %bitcast.72), channel_id=1, replica_groups=mesh['field'=16,'spatial'=32] {'field'}, dimensions={0} | all-to-all | bytes 1572864 | tf_op jit(solution)/shard_map/all_to_all | solution.py:437
  246.4 2.1 home_layout.1
  (19 shorter events, 0.1 us)
Async XLA Ops:
  6.5 109.0 %all-gather.3.cloned.1.call-start = ((), (), s32[]{:S(2)}) async-start(), calls=%async_computation.4 | async-start | bytes 1081344 | tf_op jit(solution)/shard_map/all_gather | solution.py:388
  7.9 171.7 %all-gather.5.cloned.1.call-start = ((), (), s32[]{:S(2)}) async-start(), calls=%async_computation.5 | async-start | bytes 4456448 | tf_op jit(solution)/shard_map/all_gather | solution.py:402
  16.7 43.5 %all-to-all-start = ((bf16[32,24,384]{2,1,0:T(8,128)(2,1)}), bf16[32,24,384]{2,1,0:T(8,128)(2,1)S(1)}, u32[]{:S(2)}, u32[]{:S(2)}) async-start(bf16[32,24,384]{2,1,0:T(8,128)(2,1)} %get-tuple-element.131), calls=%async_computation | async-start | bytes 1179648 | tf_op jit(solution)/shard_map/while/body/all_to_all | solution.py:418
  60.2 0.8 copy-start
  68.3 27.0 %all-to-all-start.1 = ((bf16[32,24,384]{2,1,0:T(8,128)(2,1)}), bf16[32,24,384]{2,1,0:T(8,128)(2,1)}, u32[]{:S(2)}, u32[]{:S(2)}) async-start(bf16[32,24,384]{2,1,0:T(8,128)(2,1)} %bitcast.65), calls=%async_computation.1 | async-start | bytes 1179648 | tf_op jit(solution)/shard_map/while/body/all_to_all | solution.py:418
Sparse Core Ops, SparseCore 0:
  9.5 105.9 all-gather.2
  118.1 61.4 all-gather.4

commit v11 on v7

--- a/solution.py
+++ b/solution.py
@@ -402,13 +402,13 @@
     bias = bias_in.reshape(16, 16, 2, 4).transpose(1, 2, 0, 3).reshape(16, LANES)
     rows = field_in.transpose(1, 0, 2).reshape(ROWS, NLON)
     spectrum, table = forward(rows)
-    spectrum, column = lax.optimization_barrier((spectrum, column))
+    first = (lax.axis_index("spatial") * ORDERS).astype(jnp.int32).reshape(1)
+    polar, bias = legendre(first, bias)
+    spectrum, column, polar = lax.optimization_barrier((spectrum, column, polar))
     weights = gather_second(column)
     pencil = lax.all_to_all(
         spectrum.reshape(BANDS, 2 * ORDERS, ROWS), "spatial", split_axis=0, concat_axis=0, tiled=True
     )
-    first = (lax.axis_index("spatial") * ORDERS).astype(jnp.int32).reshape(1)
-    polar, bias = legendre(first, bias)
     synth = spectral_filter(pencil.reshape(PARTS, ROWS), polar, spectral_weight)
     returned = lax.all_to_all(
         synth.reshape(BANDS, 2 * ORDERS, ROWS), "spatial", split_axis=0, concat_axis=0, tiled=True

time: 251 us -> 258 us (1.028)
  blocking collectives: 144 us -> 180 us
  waiting for transfers between devices: 23.5 us -> 1.73 us
  starting transfers between devices: 24.2 us -> 16.8 us
    all_to_all x0 -> x1, blocking collectives: none -> 44 us  [shards(): lax.all_to_all(spectrum.reshape(BANDS, 2 * ORDERS, ROWS), 'spatial', spli...]
    all_to_all x1, waiting for transfers between devices: 16.4 us -> 1.72 us  [gather_first(): lax.all_to_all(jnp.broadcast_to(both[None], (32,) + both.shape), ('spatia...]
    all_to_all x1 -> x0, starting transfers between devices: 7.43 us -> none  [shards(): lax.all_to_all(spectrum.reshape(BANDS, 2 * ORDERS, ROWS), 'spatial', spli...]
    all_to_all x1 -> x0, waiting for transfers between devices: 7.14 us -> none  [shards(): lax.all_to_all(spectrum.reshape(BANDS, 2 * ORDERS, ROWS), 'spatial', spli...]
    all_to_all x1, blocking collectives: 69.5 us -> 64.3 us  [shards(): lax.all_to_all(mixed.reshape(MEMBERS, BLOCK, LONS), 'field', split_axis=0...]
    all_to_all x1, blocking collectives: 29.6 us -> 26.8 us  [shards(): lax.all_to_all(synth.reshape(BANDS, 2 * ORDERS, ROWS), 'spatial', split_a...]
  transfers between devices with their start and end apart: 3 -> 2, of which waited for: 2 -> 1; matrix products, arithmetic and copies ran while one was open for 1% -> 1% of each run, Pallas kernels for 12% -> 12%
where the time goes in v11:
time: 258 us; the launch traced here: 257 us
  blocking collectives  180 us (70%)
  Pallas kernels  40.1 us (16%)
  starting transfers between devices  16.8 us (7%)
  between operations  13.5 us (5%)
  local copies, waits for them, and re-layouts  3.31 us (1%)
    all_to_all x1, blocking collectives, shards(): lax.all_to_all(mixed.reshape(MEMBERS, BLOCK, LONS), 'field', split_axis=0...  64.3 us
    all_to_all x1, blocking collectives, shards(): lax.all_to_all(result.reshape(MEMBERS, BLOCK, LONS), 'field', split_axis=...  45.1 us
    all_to_all x1, blocking collectives, shards(): lax.all_to_all(spectrum.reshape(BANDS, 2 * ORDERS, ROWS), 'spatial', spli...  44 us
    all_to_all x1, blocking collectives, shards(): lax.all_to_all(synth.reshape(BANDS, 2 * ORDERS, ROWS), 'spatial', split_a...  26.8 us
    all_to_all x1, starting transfers between devices, gather_first(): lax.all_to_all(jnp.broadcast_to(both[None], (32,) + both.shape), ('spatia...  16.8 us
    pallas_call x1, Pallas kernels, legendre(): pl.pallas_call(legendre_kernel, out_shape=(jax.ShapeDtypeStruct((ORDERS,...  12.6 us
    pallas_call x1, Pallas kernels, mlp(): pl.pallas_call(mlp_kernel, grid=(blocks // take,), out_shape=jax.ShapeDty...  8.05 us
    pallas_call x1, Pallas kernels, spectral_filter(): pl.pallas_call(filter_kernel, grid=(ORDERS // 2 // PAIRS,), out_shape=jax...  7.27 us
  transfers between devices with their start and end apart: 2, of which 1 were waited for; matrix products, arithmetic and copies ran while one was open for 1% of the time, Pallas kernels for 12%

profile of v11, /device:TPU:1, one launch (start us, length us, event | category | flops | bytes accessed | tf_op | source)
XLA Modules:
  0.0 257.0 jit_solution(11826377820611672991)
XLA Ops:
  6.5 0.7 pad_maximum_fusion.1
  7.2 0.7 broadcast_in_dim.2
  8.0 16.8 %all-to-all-start = ((bf16[32,8,512]{2,1,0:T(8,128)(2,1)}), bf16[32,8,512]{2,1,0:T(8,128)(2,1)S(1)}, u32[]{:S(2)}, u32[]{:S(2)}) async-start(bf16[32,8,512]{2,1,0:T(8,128)(2,1)} %broadcast_in_dim.2), calls=%async_computation | async-start | bytes 524288 | tf_op jit(solution)/shard_map/all_to_all | solution.py:380
  24.7 0.0 all-gather.2.cloned.1.call-start
  24.8 1.1 reshape.51
  25.9 0.3 copy.18
  26.2 0.7 copy.19.bias_ref
  26.8 5.6 %forward_fourier.1 = (bf16[768,384]{1,0:T(8,128)(2,1)}, bf16[768,1024]{1,0:T(8,128)(2,1)}) custom-call(bf16[384,1024]{1,0:T(8,128)(2,1)} %bitcast.27), custom_call_target="tpu_custom_call" | custom-call | tf_op jit(solution)/shard_map/forward_fourier/pallas_call | solution.py:76
  32.4 0.0 copy-start
  32.4 12.6 %legendre_table.1 = (bf16[12,384,384]{2,1,0:T(8,128)(2,1)}, f32[16,128]{1,0:T(8,128)}) custom-call(s32[1]{0:T(128)} %bitcast.2.first_ref, f32[16,128]{1,0:T(8,128)} %copy.19.bias_ref), custom_call_target="tpu_custom_call" | custom-call | flops 100000000 | bytes 20000000 | tf_op jit(solution)/shard_map/legendre_table/pallas_call | solution.py:157
  45.0 1.7 all-to-all-done
  46.7 0.1 copy.20
  46.8 0.1 copy.21
  46.9 0.1 reshape_squeeze.6
  47.0 0.1 copy.23
  47.2 0.1 copy.24
  47.3 0.7 pad_maximum_fusion
  48.0 0.0 all-gather.2.cloned.1.call-update
  48.1 0.0 copy-done
  48.1 44.0 %all_to_all.25 = bf16[32,24,384]{2,1,0:T(8,128)(2,1)} all-to-all(bf16[32,24,384]{2,1,0:T(8,128)(2,1)S(1)} %bitcast.38), channel_id=1, replica_groups=mesh['field'=16,'spatial'=32] {'spatial'}, dimensions={0} | all-to-all | bytes 1179648 | tf_op jit(solution)/shard_map/all_to_all | solution.py:409
  92.0 7.3 %spectral_filter.1 = bf16[768,384]{1,0:T(8,128)(2,1)} custom-call(bf16[768,384]{1,0:T(8,128)(2,1)} %bitcast.33, bf16[12,384,384]{2,1,0:T(8,128)(2,1)} %get-tuple-element.15.p_ref, f32[2,32,384]{2,1,0:T(8,128)} %w_ref.1), custom_call_target="tpu_custom_call" | custom-call | tf_op jit(solution)/shard_map/spectral_filter/pallas_call | solution.py:238
  99.3 26.8 %all_to_all.26 = bf16[32,24,384]{2,1,0:T(8,128)(2,1)} all-to-all(bf16[32,24,384]{2,1,0:T(8,128)(2,1)} %bitcast.34), channel_id=1, replica_groups=mesh['field'=16,'spatial'=32] {'spatial'}, dimensions={0} | all-to-all | bytes 1179648 | tf_op jit(solution)/shard_map/all_to_all | solution.py:413
  126.1 4.5 %inverse_fourier.1 = bf16[1536,256]{1,0:T(8,128)(2,1)} custom-call(bf16[768,384]{1,0:T(8,128)(2,1)} %bitcast.35, bf16[768,1024]{1,0:T(8,128)(2,1)} %get-tuple-element.16.t_ref, bf16[384,1024]{1,0:T(8,128)(2,1)} %bitcast.28), custom_call_target="tpu_custom_call" | custom-call | tf_op jit(solution)/shard_map/inverse_fourier/pallas_call | solution.py:276
  130.6 64.3 %all_to_all.27 = bf16[16,96,256]{2,1,0:T(8,128)(2,1)} all-to-all(bf16[16,96,256]{2,1,0:T(8,128)(2,1)} %bitcast.29), channel_id=1, replica_groups=mesh['field'=16,'spatial'=32] {'field'}, dimensions={0} | all-to-all | bytes 1572864 | tf_op jit(solution)/shard_map/all_to_all | solution.py:417
  194.9 0.0 all-gather.2.cloned.1.call-done
  194.9 8.1 %pointwise_mlp.1 = bf16[1536,256]{1,0:T(8,128)(2,1)} custom-call(bf16[1536,256]{1,0:T(8,128)(2,1)} %bitcast.31, bf16[16,1024,128]{2,1,0:T(8,128)(2,1)} %bitcast.26, f32[16,128]{1,0:T(8,128)} %get-tuple-element.18.bias_ref), custom_call_target="tpu_custom_call" | custom-call | tf_op jit(solution)/shard_map/pointwise_mlp/pallas_call | solution.py:338
  203.0 45.1 %all_to_all.28 = bf16[16,96,256]{2,1,0:T(8,128)(2,1)} all-to-all(bf16[16,96,256]{2,1,0:T(8,128)(2,1)} %bitcast.32), channel_id=1, replica_groups=mesh['field'=16,'spatial'=32] {'field'}, dimensions={0} | all-to-all | bytes 1572864 | tf_op jit(solution)/shard_map/all_to_all | solution.py:421
  248.0 2.1 home_layout.1
  (3 shorter events, 0.1 us)
Async XLA Ops:
  8.0 38.8 %all-to-all-start = ((bf16[32,8,512]{2,1,0:T(8,128)(2,1)}), bf16[32,8,512]{2,1,0:T(8,128)(2,1)S(1)}, u32[]{:S(2)}, u32[]{:S(2)}) async-start(bf16[32,8,512]{2,1,0:T(8,128)(2,1)} %broadcast_in_dim.2), calls=%async_computation | async-start | bytes 524288 | tf_op jit(solution)/shard_map/all_to_all | solution.py:380
  24.7 170.2 %all-gather.2.cloned.1.call-start = ((), (), s32[]{:S(2)}) async-start(), calls=%async_computation.5 | async-start | bytes 4456448 | tf_op jit(solution)/shard_map/all_gather | solution.py:396
  32.4 15.7 %copy-start = (bf16[768,384]{1,0:T(8,128)(2,1)S(1)}, bf16[768,384]{1,0:T(8,128)(2,1)}, u32[]{:S(2)}) copy-start(bf16[768,384]{1,0:T(8,128)(2,1)} %get-tuple-element.14) | copy-start | bytes 1769476
Sparse Core Ops, SparseCore 0:
  48.2 73.1 all-gather.1

commit v12 on v7

--- a/solution.py
+++ b/solution.py
@@ -377,14 +377,7 @@
 def gather_first(proj_in, proj_out):
     column = [[xy * 32 + place for place in range(32)] for xy in range(16)]
     both = jnp.concatenate([proj_in, proj_out], axis=0)
-    return lax.all_to_all(
-        jnp.broadcast_to(both[None], (32,) + both.shape),
-        ("spatial", "field"),
-        split_axis=0,
-        concat_axis=0,
-        axis_index_groups=column,
-        tiled=True,
-    )
+    return lax.all_gather(both, ("spatial", "field"), axis=0, axis_index_groups=column, tiled=True)
 
 
 def gather_second(column):

time: 251 us -> 260 us (1.036)
  blocking collectives: 144 us -> 182 us
  waiting for transfers between devices: 23.5 us -> 7.84 us
  starting transfers between devices: 24.2 us -> 11.9 us
    all_gather x0 -> x1, blocking collectives: none -> 38.3 us  [gather_first(): lax.all_gather(both, ('spatial', 'field'), axis=0, axis_index_groups=colu...]
    all_to_all x1 -> x0, starting transfers between devices: 16.7 us -> none  [gather_first(): lax.all_to_all(jnp.broadcast_to(both[None], (32,) + both.shape), ('spatia...]
    all_to_all x1 -> x0, waiting for transfers between devices: 16.4 us -> none  [gather_first(): lax.all_to_all(jnp.broadcast_to(both[None], (32,) + both.shape), ('spatia...]
    all_to_all x1, starting transfers between devices: 7.43 us -> 11.9 us  [shards(): lax.all_to_all(spectrum.reshape(BANDS, 2 * ORDERS, ROWS), 'spatial', spli...]
  transfers between devices with their start and end apart: 3 -> 2, of which waited for: 2 -> 1; matrix products, arithmetic and copies ran while one was open for 1% -> 1% of each run, Pallas kernels for 12% -> 9%
where the time goes in v12:
time: 260 us; the launch traced here: 259 us
  blocking collectives  182 us (70%)
  Pallas kernels  40 us (15%)
  between operations  13.5 us (5%)
  starting transfers between devices  11.9 us (5%)
  waiting for transfers between devices  7.84 us (3%)
    all_to_all x1, blocking collectives, shards(): lax.all_to_all(mixed.reshape(MEMBERS, BLOCK, LONS), 'field', split_axis=0...  69.6 us
    all_to_all x1, blocking collectives, shards(): lax.all_to_all(result.reshape(MEMBERS, BLOCK, LONS), 'field', split_axis=...  45.1 us
    all_gather x1, blocking collectives, gather_first(): lax.all_gather(both, ('spatial', 'field'), axis=0, axis_index_groups=colu...  38.3 us
    all_to_all x1, blocking collectives, shards(): lax.all_to_all(synth.reshape(BANDS, 2 * ORDERS, ROWS), 'spatial', split_a...  28.9 us
    pallas_call x1, Pallas kernels, legendre(): pl.pallas_call(legendre_kernel, out_shape=(jax.ShapeDtypeStruct((ORDERS,...  12.6 us
    all_to_all x1, starting transfers between devices, shards(): lax.all_to_all(spectrum.reshape(BANDS, 2 * ORDERS, ROWS), 'spatial', spli...  11.9 us
    pallas_call x1, Pallas kernels, mlp(): pl.pallas_call(mlp_kernel, grid=(blocks // take,), out_shape=jax.ShapeDty...  8.05 us
    all_to_all x1, waiting for transfers between devices, shards(): lax.all_to_all(spectrum.reshape(BANDS, 2 * ORDERS, ROWS), 'spatial', spli...  7.82 us
  transfers between devices with their start and end apart: 2, of which 1 were waited for; matrix products, arithmetic and copies ran while one was open for 1% of the time, Pallas kernels for 9%

profile of v12, /device:TPU:1, one launch (start us, length us, event | category | flops | bytes accessed | tf_op | source)
XLA Modules:
  0.0 258.9 jit_solution(17309277738977456251)
XLA Ops:
  6.5 0.0 copy-start.1
  6.5 0.0 all-gather.2.cloned.1.call-start
  6.5 5.6 %forward_fourier.1 = (bf16[768,384]{1,0:T(8,128)(2,1)}, bf16[768,1024]{1,0:T(8,128)(2,1)}) custom-call(bf16[384,1024]{1,0:T(8,128)(2,1)} %bitcast.30), custom_call_target="tpu_custom_call" | custom-call | tf_op jit(solution)/shard_map/forward_fourier/pallas_call | solution.py:76
  12.1 0.7 pad_maximum_fusion.1
  12.8 38.3 %all_gather.6 = bf16[256,512]{1,0:T(8,128)(2,1)S(1)} all-gather(bf16[8,512]{1,0:T(8,128)(2,1)S(1)} %pad_maximum_fusion.1), channel_id=1, replica_groups={{0,32,64,96,128,160,192,224,256,288,320,352,384,416,448,480,1,33,65,97,..., dimensions={0}, use_global_device_ids=true | all-gather | bytes 270336 | tf_op jit(solution)/shard_map/all_gather | solution.py:380
  51.1 0.1 reshape.58
  51.2 0.1 slice_bitcast_fusion.1
  51.3 0.1 copy.22
  51.4 0.1 reshape_squeeze.6
  51.5 0.7 pad_maximum_fusion
  52.2 0.0 all-gather.2.cloned.1.call-update
  52.3 11.9 %all-to-all-start = ((bf16[32,24,384]{2,1,0:T(8,128)(2,1)}), bf16[32,24,384]{2,1,0:T(8,128)(2,1)S(1)}, u32[]{:S(2)}, u32[]{:S(2)}) async-start(bf16[32,24,384]{2,1,0:T(8,128)(2,1)} %bitcast.40), calls=%async_computation | async-start | bytes 1179648 | tf_op jit(solution)/shard_map/all_to_all | solution.py:400
  64.1 0.0 copy-done.1
  64.1 0.4 reshape.52
  64.6 0.3 copy.17
  64.8 0.7 copy.18.bias_ref
  65.5 12.6 %legendre_table.1 = (bf16[12,384,384]{2,1,0:T(8,128)(2,1)}, f32[16,128]{1,0:T(8,128)}) custom-call(s32[1]{0:T(128)} %bitcast.4.first_ref, f32[16,128]{1,0:T(8,128)} %copy.18.bias_ref), custom_call_target="tpu_custom_call" | custom-call | flops 100000000 | bytes 20000000 | tf_op jit(solution)/shard_map/legendre_table/pallas_call | solution.py:157
  78.1 7.8 %all-to-all-done = bf16[32,24,384]{2,1,0:T(8,128)(2,1)S(1)} async-done(((bf16[32,24,384]{2,1,0:T(8,128)(2,1)}), bf16[32,24,384]{2,1,0:T(8,128)(2,1)S(1)}, u32[]{:S(2)}, u32[]{:S(2)}) %all-to-all-start) | async-done | bytes 589856 | tf_op jit(solution)/shard_map/all_to_all | solution.py:400
  85.9 0.0 copy-start
  85.9 0.8 copy-done
  86.7 7.3 %spectral_filter.1 = bf16[768,384]{1,0:T(8,128)(2,1)} custom-call(bf16[768,384]{1,0:T(8,128)(2,1)} %bitcast.36, bf16[12,384,384]{2,1,0:T(8,128)(2,1)} %get-tuple-element.13.p_ref, f32[2,32,384]{2,1,0:T(8,128)} %w_ref.1), custom_call_target="tpu_custom_call" | custom-call | tf_op jit(solution)/shard_map/spectral_filter/pallas_call | solution.py:238
  94.0 28.9 %all_to_all.20 = bf16[32,24,384]{2,1,0:T(8,128)(2,1)} all-to-all(bf16[32,24,384]{2,1,0:T(8,128)(2,1)} %bitcast.37), channel_id=1, replica_groups=mesh['field'=16,'spatial'=32] {'spatial'}, dimensions={0} | all-to-all | bytes 1179648 | tf_op jit(solution)/shard_map/all_to_all | solution.py:406
  122.8 4.5 %inverse_fourier.1 = bf16[1536,256]{1,0:T(8,128)(2,1)} custom-call(bf16[768,384]{1,0:T(8,128)(2,1)} %bitcast.38, bf16[768,1024]{1,0:T(8,128)(2,1)} %get-tuple-element.14.t_ref, bf16[384,1024]{1,0:T(8,128)(2,1)} %bitcast.31), custom_call_target="tpu_custom_call" | custom-call | tf_op jit(solution)/shard_map/inverse_fourier/pallas_call | solution.py:276
  127.3 69.6 %all_to_all.21 = bf16[16,96,256]{2,1,0:T(8,128)(2,1)} all-to-all(bf16[16,96,256]{2,1,0:T(8,128)(2,1)} %bitcast.32), channel_id=1, replica_groups=mesh['field'=16,'spatial'=32] {'field'}, dimensions={0} | all-to-all | bytes 1572864 | tf_op jit(solution)/shard_map/all_to_all | solution.py:410
  196.9 0.0 all-gather.2.cloned.1.call-done
  196.9 8.1 %pointwise_mlp.1 = bf16[1536,256]{1,0:T(8,128)(2,1)} custom-call(bf16[1536,256]{1,0:T(8,128)(2,1)} %bitcast.34, bf16[16,1024,128]{2,1,0:T(8,128)(2,1)} %bitcast.29, f32[16,128]{1,0:T(8,128)} %get-tuple-element.16.bias_ref), custom_call_target="tpu_custom_call" | custom-call | tf_op jit(solution)/shard_map/pointwise_mlp/pallas_call | solution.py:338
  205.0 45.1 %all_to_all.22 = bf16[16,96,256]{2,1,0:T(8,128)(2,1)} all-to-all(bf16[16,96,256]{2,1,0:T(8,128)(2,1)} %bitcast.35), channel_id=1, replica_groups=mesh['field'=16,'spatial'=32] {'field'}, dimensions={0} | all-to-all | bytes 1572864 | tf_op jit(solution)/shard_map/all_to_all | solution.py:414
  250.0 2.1 home_layout.1
  (2 shorter events, 0.1 us)
Async XLA Ops:
  6.5 57.6 %copy-start.1 = (f32[2048]{0:T(1024)S(1)}, f32[2048]{0:T(1024)}, u32[]{:S(2)}) copy-start(f32[2048]{0:T(1024)} %param.8) | copy-start | bytes 24580
  6.5 190.4 %all-gather.2.cloned.1.call-start = ((), (), s32[]{:S(2)}) async-start(), calls=%async_computation.4 | async-start | bytes 4456448 | tf_op jit(solution)/shard_map/all_gather | solution.py:389
  52.3 33.6 %all-to-all-start = ((bf16[32,24,384]{2,1,0:T(8,128)(2,1)}), bf16[32,24,384]{2,1,0:T(8,128)(2,1)S(1)}, u32[]{:S(2)}, u32[]{:S(2)}) async-start(bf16[32,24,384]{2,1,0:T(8,128)(2,1)} %bitcast.40), calls=%async_computation | async-start | bytes 1179648 | tf_op jit(solution)/shard_map/all_to_all | solution.py:400
  85.9 0.8 copy-start
Sparse Core Ops, SparseCore 0:
  52.4 72.0 all-gather.1
